TPU v7x, 128 devices: a whole 4x4x4 slice. The times are simulated.
128 devices in a mesh: seq: 4 (over x), ctx: 32 (over z, y, core).
Axes of the slice: x: 4, y: 4, z: 4, core: 2. Of those that a mesh axis runs over, the one named last changes fastest.
Arguments:
- tokens: bfloat16 [16384, 1600], P(('seq', 'ctx')), may hold values from -6 to 6
- norm_gain: float32 [1600], replicated, may hold values from 0.5 to 1.5
- qkv_weight: bfloat16 [1600, 2240], P('ctx'), may hold values from -0.15625 to 0.15625
- attn_out_weight: bfloat16 [1600, 1600], P('ctx'), may hold values from -0.15625 to 0.15625
- in_weight: bfloat16 [1600, 6400], P('ctx'), may hold values from -0.15625 to 0.15625
- conv_weight: float32 [4, 3200], replicated, may hold values from -3 to 3
- conv_bias: float32 [3200], replicated, may hold values from -3 to 3
- xproj_weight: bfloat16 [3200, 132], P('ctx'), may hold values from -0.109375 to 0.109375
- dt_weight: bfloat16 [3200, 100], P('ctx'), may hold values from -0.625 to 0.625
- dt_bias: float32 [3200], replicated, may hold values from -7 to -2
- decay_log: float32 [3200, 16], replicated, may hold values from -7 to 0
- skip_gain: float32 [3200], replicated, may hold values from 0.5 to 1.5
- mamba_out_weight: bfloat16 [3200, 1600], P('ctx'), may hold values from -0.109375 to 0.109375
- attn_gain: float32 [1600], replicated, may hold values from 0.5 to 1.5
- mamba_gain: float32 [1600], replicated, may hold values from 0.5 to 1.5
- ffn_gain: float32 [1600], replicated, may hold values from 0.5 to 1.5
- gate_up_weight: bfloat16 [1600, 11008], P('ctx'), may hold values from -0.15625 to 0.15625
- down_weight: bfloat16 [5504, 1600], P('ctx'), may hold values from -0.078125 to 0.078125
- cotangent: bfloat16 [16384, 1600], P(('seq', 'ctx')), may hold values from -6 to 6
Outputs:
- output: bfloat16 [16384, 1600], P(('seq', 'ctx'))
- tokens_grad: float32 [16384, 1600], P(('seq', 'ctx'))
- norm_gain_grad: float32 [1600], replicated
- qkv_weight_grad: float32 [1600, 2240], P('ctx')
- attn_out_weight_grad: float32 [1600, 1600], P('ctx')
- in_weight_grad: float32 [1600, 6400], P('ctx')
- conv_weight_grad: float32 [4, 3200], replicated
- conv_bias_grad: float32 [3200], replicated
- xproj_weight_grad: float32 [3200, 132], P('ctx')
- dt_weight_grad: float32 [3200, 100], P('ctx')
- dt_bias_grad: float32 [3200], replicated
- decay_log_grad: float32 [3200, 16], replicated
- skip_gain_grad: float32 [3200], replicated
- mamba_out_weight_grad: float32 [3200, 1600], P('ctx')
- attn_gain_grad: float32 [1600], replicated
- mamba_gain_grad: float32 [1600], replicated
- ffn_gain_grad: float32 [1600], replicated
- gate_up_weight_grad: float32 [1600, 11008], P('ctx')
- down_weight_grad: float32 [5504, 1600], P('ctx')
All inputs are finite; a program needn't handle non-finite values.
Results may differ from a plain program's by a relative error of at most 0.024.
Values may be sent and summed in bfloat16 or wider, within the bound.
No kernel may reach another device: no remote copies, remote signals or barrier semaphores. Data moves between devices by JAX's collectives and lax.ppermute only.
A program may use at most 576 MiB of HBM per device.

v0:
```python
import jax
import jax.numpy as jnp
from jax import lax
from jax.sharding import PartitionSpec as P

HEADS = 25
KV_HEADS = 5
HEAD_DIM = 64
DI = 3200
N_STATE = 16
CONV = 4
DT_RANK = 100
FF = 5504
WINDOW = 1024


EPS = 1e-05
NEG_BIG = -1e30


def shifted(value, axis, by):
    size = lax.axis_size(axis)
    pairs = [(i, i + by) for i in range(size) if 0 <= i + by < size]
    return lax.ppermute(value, axis, pairs)


def carried_in(part, axis, combine, identity, reverse):
    count = lax.axis_size(axis)
    place = lax.axis_index(axis)
    ahead = count - 1 - place if reverse else place
    gathered = jax.tree.map(lambda a: lax.all_gather(a, axis), part)
    state = jax.tree.map(lambda a, e: jnp.zeros_like(a) + jnp.asarray(e, a.dtype), part, identity)

    def one(lap, state):
        source = count - 1 - lap if reverse else lap
        return combine(
            state, jax.tree.map(lambda a: lax.dynamic_index_in_dim(a, source, 0, False), gathered)
        )

    return lax.fori_loop(0, ahead, one, state)


def norm_scale(values, gain):
    return values * lax.rsqrt(jnp.mean(values * values, axis=-1, keepdims=True) + EPS) * gain


def matmul(operand, other):
    return jnp.dot(operand, other, preferred_element_type=jnp.float32)


def matmul_last(operand, other):
    return lax.dot_general(
        operand, other, (((1,), (1,)), ((), ())), preferred_element_type=jnp.float32
    )


def combine_affine(earlier, later):
    return (earlier[0] * later[0], later[0] * earlier[1] + later[1])


def rows_gradient(activation, upstream):
    return lax.psum_scatter(
        lax.dot_general(
            activation, upstream, (((0,), (0,)), ((), ())), preferred_element_type=jnp.float32
        ).astype(jnp.bfloat16),
        "ctx",
        scatter_dimension=0,
        tiled=True,
    ).astype(jnp.float32)


def body(
    tokens,
    norm_gain,
    qkv_weight,
    attn_out_weight,
    in_weight,
    conv_weight,
    conv_bias,
    xproj_weight,
    dt_weight,
    dt_bias,
    decay_log,
    skip_gain,
    mamba_out_weight,
    attn_gain,
    mamba_gain,
    ffn_gain,
    gate_up_weight,
    down_weight,
    cotangent,
):
    shards = (
        qkv_weight,
        attn_out_weight,
        in_weight,
        xproj_weight,
        dt_weight,
        mamba_out_weight,
        gate_up_weight,
        down_weight,
    )
    w_qkv, w_attn, w_in, w_xproj, w_step, w_mamba, w_gate_up, w_down = (
        lax.all_gather(shards[0], "ctx", axis=0, tiled=True),
        lax.all_gather(shards[1], "ctx", axis=0, tiled=True),
        lax.all_gather(shards[2], "ctx", axis=0, tiled=True),
        lax.all_gather(shards[3], "ctx", axis=0, tiled=True),
        lax.all_gather(shards[4], "ctx", axis=0, tiled=True),
        lax.all_gather(shards[5], "ctx", axis=0, tiled=True),
        lax.all_gather(shards[6], "ctx", axis=0, tiled=True),
        lax.all_gather(shards[7], "ctx", axis=0, tiled=True),
    )
    rows_here = tokens.shape[0]
    ctx_index = lax.axis_index("ctx")
    head_width = HEADS * HEAD_DIM
    kv_width = KV_HEADS * HEAD_DIM
    per_group = HEADS // KV_HEADS
    score_scale = HEAD_DIM ** (-0.5)
    reach = WINDOW // rows_here
    width_keys = (reach + 1) * rows_here
    inputs = tokens.astype(jnp.float32)
    normed_f, norm1_pullback = jax.vjp(norm_scale, inputs, norm_gain)
    normed = normed_f.astype(jnp.bfloat16)
    projected = matmul(normed, w_qkv).astype(jnp.bfloat16)
    queries = projected[:, :head_width]
    key_own = projected[:, head_width : head_width + kv_width]
    value_own = projected[:, head_width + kv_width :]
    key_list = [key_own]
    value_list = [value_own]
    for offset in range(1, reach + 1):
        far_key, far_value = shifted((key_own, value_own), "ctx", offset)
        key_list.insert(0, far_key)
        value_list.insert(0, far_value)
    key_rows = jnp.concatenate(key_list, axis=0)
    value_rows = jnp.concatenate(value_list, axis=0)
    query_pos = ctx_index * rows_here + jnp.arange(rows_here, dtype=jnp.int32)
    key_pos = (ctx_index - reach) * rows_here + jnp.arange(width_keys, dtype=jnp.int32)
    visible = (
        (key_pos[None, :] >= 0)
        & (key_pos[None, :] <= query_pos[:, None])
        & (query_pos[:, None] - key_pos[None, :] < WINDOW)
    )
    query_heads = queries.reshape(rows_here, KV_HEADS, per_group, HEAD_DIM)
    key_heads = key_rows.reshape(width_keys, KV_HEADS, HEAD_DIM)
    value_heads = value_rows.reshape(width_keys, KV_HEADS, HEAD_DIM)
    scores = (
        jnp.einsum("tkgd,skd->kgts", query_heads, key_heads, preferred_element_type=jnp.float32)
        * score_scale
    )
    masked = jnp.where(visible[None, None], scores, NEG_BIG)
    row_peak = jnp.max(masked, axis=-1, keepdims=True)
    expd = jnp.exp(masked - row_peak)
    probs = expd / jnp.sum(expd, axis=-1, keepdims=True)
    probs_low = probs.astype(jnp.bfloat16)
    attended = (
        jnp.einsum("kgts,skd->tkgd", probs_low, value_heads, preferred_element_type=jnp.float32)
        .reshape(rows_here, head_width)
        .astype(jnp.bfloat16)
    )
    attn_branch = matmul(attended, w_attn)
    in_proj = matmul(normed, w_in)
    conv_in = in_proj[:, :DI]
    gate_z = in_proj[:, DI:]
    tail_rows = shifted(conv_in[rows_here - (CONV - 1) :], "ctx", 1)
    padded = jnp.concatenate([tail_rows, conv_in])
    conv_sum = conv_bias
    for offset in range(CONV):
        conv_sum = conv_sum + conv_weight[offset] * padded[offset : offset + rows_here]
    act_f, conv_pullback = jax.vjp(jax.nn.silu, conv_sum)
    inner_act = act_f.astype(jnp.bfloat16)
    act_values = inner_act.astype(jnp.float32)
    xproj = matmul(inner_act, w_xproj)
    dt_low = xproj[:, :DT_RANK].astype(jnp.bfloat16)
    b_in = xproj[:, DT_RANK : DT_RANK + N_STATE]
    c_out = xproj[:, DT_RANK + N_STATE :]
    pre = matmul_last(dt_low, w_step) + dt_bias
    step_size = jax.nn.softplus(pre)
    decay_rate = -jnp.exp(decay_log)
    decay_step = jnp.exp(step_size[:, :, None] * decay_rate[None])
    drive_term = (step_size * act_values)[:, :, None] * b_in[:, None, :]

    def forward_step(running, sequence):
        updated = sequence[0] * running + sequence[1]
        return (updated, updated)

    last_state, local_states = lax.scan(
        forward_step, jnp.zeros((DI, N_STATE), jnp.float32), (decay_step, drive_term)
    )
    cumulative = jnp.cumsum(step_size, axis=0)
    whole_decay = jnp.exp(decay_rate * cumulative[-1][:, None])
    identity = (jnp.ones((DI, N_STATE), jnp.float32), jnp.zeros((DI, N_STATE), jnp.float32))
    _, start_state = carried_in((whole_decay, last_state), "ctx", combine_affine, identity, False)
    states = local_states + jnp.exp(decay_rate[None] * cumulative[:, :, None]) * start_state[None]
    scan_out = jnp.sum(states * c_out[:, None, :], axis=-1) + skip_gain * act_values
    silu_z, gate_pullback = jax.vjp(jax.nn.silu, gate_z)
    gated = (scan_out * silu_z).astype(jnp.bfloat16)
    mamba_branch = matmul(gated, w_mamba)

    def mixing(attn_part, mamba_part, gain_attn, gain_mamba):
        return 0.5 * (norm_scale(attn_part, gain_attn) + norm_scale(mamba_part, gain_mamba))

    mixed, mix_pullback = jax.vjp(mixing, attn_branch, mamba_branch, attn_gain, mamba_gain)
    residual = inputs + mixed
    ffn_f, norm2_pullback = jax.vjp(norm_scale, residual, ffn_gain)
    ffn_input = ffn_f.astype(jnp.bfloat16)
    gate_up = matmul(ffn_input, w_gate_up)

    def swiglu(both):
        return jax.nn.silu(both[:, :FF]) * both[:, FF:]

    hidden_f, swiglu_pullback = jax.vjp(swiglu, gate_up)
    hidden = hidden_f.astype(jnp.bfloat16)
    output = (residual + matmul(hidden, w_down)).astype(jnp.bfloat16)
    upstream = cotangent.astype(jnp.float32)
    grad_down = rows_gradient(hidden, cotangent)
    grad_hidden = matmul_last(cotangent, w_down)
    (grad_gate_up_f,) = swiglu_pullback(grad_hidden)
    grad_gate_up = grad_gate_up_f.astype(jnp.bfloat16)
    grad_gate_up_w = rows_gradient(ffn_input, grad_gate_up)
    grad_ffn_in = matmul_last(grad_gate_up, w_gate_up)
    grad_resid_norm, grad_ffn_gain = norm2_pullback(grad_ffn_in)
    grad_residual = upstream + grad_resid_norm
    grad_attn_f, grad_mamba_f, grad_attn_gain, grad_mamba_gain = mix_pullback(grad_residual)
    grad_attn_branch = grad_attn_f.astype(jnp.bfloat16)
    grad_mamba_branch = grad_mamba_f.astype(jnp.bfloat16)
    grad_attn_w = rows_gradient(attended, grad_attn_branch)
    grad_attended = (
        matmul_last(grad_attn_branch, w_attn)
        .astype(jnp.bfloat16)
        .reshape(rows_here, KV_HEADS, per_group, HEAD_DIM)
    )
    grad_probs = jnp.einsum(
        "tkgd,skd->kgts", grad_attended, value_heads, preferred_element_type=jnp.float32
    )
    grad_values = jnp.einsum(
        "kgts,tkgd->skd", probs_low, grad_attended, preferred_element_type=jnp.float32
    )
    grad_scores = (
        probs * (grad_probs - jnp.sum(probs * grad_probs, axis=-1, keepdims=True))
    ).astype(jnp.bfloat16)
    grad_queries = (
        jnp.einsum("kgts,skd->tkgd", grad_scores, key_heads, preferred_element_type=jnp.float32)
        * score_scale
    )
    grad_keys = (
        jnp.einsum("kgts,tkgd->skd", grad_scores, query_heads, preferred_element_type=jnp.float32)
        * score_scale
    )
    grad_kv = jnp.concatenate(
        [grad_keys.reshape(width_keys, kv_width), grad_values.reshape(width_keys, kv_width)], axis=1
    )
    grad_kv_own = grad_kv[reach * rows_here :]
    for offset in range(1, reach + 1):
        lower = (reach - offset) * rows_here
        grad_kv_own = grad_kv_own + shifted(
            grad_kv[lower : lower + rows_here].astype(jnp.bfloat16), "ctx", -offset
        ).astype(jnp.float32)
    grad_projected = jnp.concatenate(
        [grad_queries.reshape(rows_here, head_width), grad_kv_own], axis=1
    ).astype(jnp.bfloat16)
    grad_qkv_w = rows_gradient(normed, grad_projected)
    grad_normed = matmul_last(grad_projected, w_qkv)
    grad_mamba_w = rows_gradient(gated, grad_mamba_branch)
    grad_gated = matmul_last(grad_mamba_branch, w_mamba)
    grad_scan_out = grad_gated * silu_z
    (grad_gate_z,) = gate_pullback(grad_gated * scan_out)
    grad_skip = jnp.sum(grad_scan_out * act_values, axis=0)
    grad_states = grad_scan_out[:, :, None] * c_out[:, None, :]
    grad_c_out = jnp.sum(grad_scan_out[:, :, None] * states, axis=1)
    next_decay = jnp.concatenate([decay_step[1:], jnp.zeros((1, DI, N_STATE), jnp.float32)])

    def backward_step(running, sequence):
        updated = sequence[0] + sequence[1] * running
        return (updated, updated)

    _, local_adjoint = lax.scan(
        backward_step,
        jnp.zeros((DI, N_STATE), jnp.float32),
        (grad_states, next_decay),
        reverse=True,
    )
    start_grad = decay_step[0] * local_adjoint[0]
    _, later_grad = carried_in((whole_decay, start_grad), "ctx", combine_affine, identity, True)
    adjoint = (
        local_adjoint
        + jnp.exp(decay_rate[None] * (cumulative[-1][None] - cumulative)[:, :, None])
        * later_grad[None]
    )
    prev_states = jnp.concatenate([start_state[None], states[:-1]])
    flow = adjoint * prev_states * decay_step
    adjoint_b = jnp.sum(adjoint * b_in[:, None, :], axis=-1)
    grad_step = jnp.sum(flow * decay_rate[None], axis=-1) + act_values * adjoint_b
    grad_decay_log = jnp.sum(flow * step_size[:, :, None], axis=0) * decay_rate
    grad_b_in = jnp.sum(adjoint * (step_size * act_values)[:, :, None], axis=1)
    grad_act = step_size * adjoint_b + skip_gain * grad_scan_out
    grad_pre_f = grad_step * jax.nn.sigmoid(pre)
    grad_dt_bias = jnp.sum(grad_pre_f, axis=0)
    grad_pre = grad_pre_f.astype(jnp.bfloat16)
    grad_step_w = rows_gradient(grad_pre, dt_low)
    grad_dt_low = matmul(grad_pre, w_step)
    grad_xproj = jnp.concatenate([grad_dt_low, grad_b_in, grad_c_out], axis=1).astype(jnp.bfloat16)
    grad_xproj_w = rows_gradient(inner_act, grad_xproj)
    grad_act = grad_act + matmul_last(grad_xproj, w_xproj)
    (grad_conv_sum,) = conv_pullback(grad_act)
    grad_conv_bias = jnp.sum(grad_conv_sum, axis=0)
    grad_conv_w = jnp.stack(
        [
            jnp.sum(grad_conv_sum * padded[offset : offset + rows_here], axis=0)
            for offset in range(CONV)
        ]
    )
    grad_padded = jnp.zeros((rows_here + CONV - 1, DI), jnp.float32)
    for offset in range(CONV):
        grad_padded = grad_padded + jnp.pad(
            conv_weight[offset] * grad_conv_sum, ((offset, CONV - 1 - offset), (0, 0))
        )
    back_tail = shifted(grad_padded[: CONV - 1].astype(jnp.bfloat16), "ctx", -1).astype(jnp.float32)
    grad_conv_in = grad_padded[CONV - 1 :] + jnp.concatenate(
        [jnp.zeros((rows_here - (CONV - 1), DI), jnp.float32), back_tail]
    )
    grad_in_proj = jnp.concatenate([grad_conv_in, grad_gate_z], axis=1).astype(jnp.bfloat16)
    grad_in_w = rows_gradient(normed, grad_in_proj)
    grad_normed = grad_normed + matmul_last(grad_in_proj, w_in)
    grad_inputs_norm, grad_norm_gain = norm1_pullback(grad_normed)
    tokens_grad = grad_residual + grad_inputs_norm
    matrices = (
        lax.psum(grad_qkv_w.astype(jnp.bfloat16), "seq").astype(jnp.float32),
        lax.psum(grad_attn_w.astype(jnp.bfloat16), "seq").astype(jnp.float32),
        lax.psum(grad_in_w.astype(jnp.bfloat16), "seq").astype(jnp.float32),
        lax.psum(grad_xproj_w.astype(jnp.bfloat16), "seq").astype(jnp.float32),
        lax.psum(grad_step_w.astype(jnp.bfloat16), "seq").astype(jnp.float32),
        lax.psum(grad_mamba_w.astype(jnp.bfloat16), "seq").astype(jnp.float32),
        lax.psum(grad_gate_up_w.astype(jnp.bfloat16), "seq").astype(jnp.float32),
        lax.psum(grad_down.astype(jnp.bfloat16), "seq").astype(jnp.float32),
    )
    smalls = lax.psum(
        (
            grad_norm_gain,
            grad_conv_w,
            grad_conv_bias,
            grad_dt_bias,
            grad_decay_log,
            grad_skip,
            grad_attn_gain,
            grad_mamba_gain,
            grad_ffn_gain,
        ),
        ("seq", "ctx"),
    )
    return (
        output,
        tokens_grad,
        smalls[0],
        matrices[0],
        matrices[1],
        matrices[2],
        smalls[1],
        smalls[2],
        matrices[3],
        matrices[4],
        smalls[3],
        smalls[4],
        smalls[5],
        matrices[5],
        smalls[6],
        smalls[7],
        smalls[8],
        matrices[6],
        matrices[7],
    )


def solution(mesh):
    return jax.shard_map(
        body,
        mesh=mesh,
        in_specs=(
            P(("seq", "ctx"), None),
            P(),
            P("ctx", None),
            P("ctx", None),
            P("ctx", None),
            P(),
            P(),
            P("ctx", None),
            P("ctx", None),
            P(),
            P(),
            P(),
            P("ctx", None),
            P(),
            P(),
            P(),
            P("ctx", None),
            P("ctx", None),
            P(("seq", "ctx"), None),
        ),
        out_specs=(
            P(("seq", "ctx"), None),
            P(("seq", "ctx"), None),
            P(),
            P("ctx", None),
            P("ctx", None),
            P("ctx", None),
            P(),
            P(),
            P("ctx", None),
            P("ctx", None),
            P(),
            P(),
            P(),
            P("ctx", None),
            P(),
            P(),
            P(),
            P("ctx", None),
            P("ctx", None),
        ),
        check_vma=False,
    )
```

profile of v0, /device:TPU:14, one launch (start us, length us, event | category | flops | bytes accessed | tf_op | source)
XLA Modules:
  0.0 2881.9 jit_solution(124398556105351100)
XLA Ops:
  11.9 29.5 %all-gather.6 = bf16[32,100,100]{2,1,0:T(8,128)(2,1)} all-gather(bf16[1,100,100]{2,1,0:T(8,128)(2,1)} %bitcast.217), channel_id=1, replica_groups=mesh['seq'=4,'ctx'=32] {'ctx'}, dimensions={0}, use_global_device_ids=true | all-gather | bytes 660000 | tf_op jit(solution)/shard_map/all_gather | solution.py:108
  41.4 24.5 all-gather.5
  65.9 37.6 %all-gather.30.cloned.1.call-done = bf16[32,50,6400]{2,1,0:T(8,128)(2,1)} async-done(((bf16[1,50,6400]{2,1,0:T(8,128)(2,1)}), bf16[32,50,6400]{2,1,0:T(8,128)(2,1)}) %all-gather.30.cloned.1.call-update) | async-done | bytes 20480016 | tf_op jit(solution)/shard_map/all_gather | solution.py:106
  184.0 241.7 %while.58 = (s32[]{:T(128)}, f32[3200,16]{0,1:T(8,128)S(1)}, f32[128,3200,16]{1,2,0:T(8,128)}, f32[128,3200,16]{1,2,0:T(8,128)}, f32[128,3200,16]{1,2,0:T(8,128)}, /*index=5*/s32[]{:T(128)}, s32[]{:T(128)}) while((s32[]{:T(128)}, f32[3200,16]{0,1:T(8,128)S(1)}, f32[128,3200,16]{1,2,0:T(8,128)}, f32[128,3200,16]{1,2,0:T(8,128)}, ...), condition=%wide.region_5.6_spmd.clone, body=%wide.region_4.5_spmd.clone.sunk | while | flops 153603 | bytes 1024099 | solution.py:186
  565.3 21.1 reshape.281
  605.2 19.6 concatenate.40
  644.3 38.2 %multiply_reduce_fusion.5 = (f32[128,3200]{1,0:T(8,128)S(1)}, f32[128,3200,16]{1,2,0:T(8,128)}) fusion(f32[128,16]{1,0:T(8,128)S(1)} %copy.64, f32[128,3200,16]{1,2,0:T(8,128)} %get-tuple-element.278, f32[3200,16]{0,1:T(8,128)S(1)} %get-tuple-element.280, f32[128,3200]{1,0:T(8,128)S(1)} %copy-done.6, f32[3200,16]{0,1:T(8,128)S(1)} %get-tuple-element.483), kind=kLoop, calls=%fused_computation.23 | loop fusion | flops 32358400 | bytes 56123392 | tf_op jit(solution)/shard_map/reduce_sum | solution.py:194
  707.0 46.9 %reshape.279 = bf16[1600,11008]{1,0:T(8,128)(2,1)} reshape(bf16[32,50,11008]{2,1,0:T(8,128)(2,1)} %all-gather.34.cloned.1.call-done) | data formatting | bytes 70451200
  783.0 20.8 multiply_reduce_fusion.11
  888.0 20.4 multiply_reduce_fusion.1
  918.7 240.6 %while.59 = (s32[]{:T(128)}, f32[3200,16]{0,1:T(8,128)S(1)}, f32[128,3200,16]{1,2,0:T(8,128)}, f32[128,3200,16]{1,2,0:T(8,128)}, f32[128,3200,16]{1,2,0:T(8,128)}, /*index=5*/s32[]{:T(128)}, s32[]{:T(128)}, s32[]{:T(128)}) while((s32[]{:T(128)}, f32[3200,16]{0,1:T(8,128)S(1)}, f32[128,3200,16]{1,2,0:T(8,128)}, ...), condition=%wide.region_17.18_spmd.clone, body=%wide.region_16.17_spmd.clone.sunk | while | flops 153604 | bytes 1024119 | solution.py:276
  1173.8 172.8 %fusion.6 = bf16[176,1600]{1,0:T(8,128)(2,1)} fusion(bf16[5504,1600]{1,0:T(8,128)(2,1)} %convolution_convert_fusion.2), kind=kCustom, calls=%all-reduce-scatter.6 | all-reduce-scatter fusion | flops 9011201 | bytes 18176512
  1346.6 268.2 %fusion.5 = bf16[64,11008]{1,0:T(8,128)(2,1)} fusion(bf16[1600,11008]{1,0:T(8,128)(2,1)} %convolution_convert_fusion), kind=kCustom, calls=%all-reduce-scatter.5 | all-reduce-scatter fusion | flops 22544384 | bytes 36635136
  1657.2 59.4 %collective-permute-done.56 = bf16[124,1600]{1,0:T(8,128)(2,1)} collective-permute-done((bf16[124,1600]{1,0:T(8,128)(2,1)S(1)}, bf16[124,1600]{1,0:T(8,128)(2,1)}, u32[]{:S(2)}, u32[]{:S(2)}) %collective-permute-start.56) | collective-permute-done | bytes 396832
  1724.7 53.2 %while.57 = (s32[]{:T(128)}, f32[3200,16]{0,1:T(8,128)}, s32[]{:T(128)}, f32[32,3200,16]{1,2,0:T(8,128)}, f32[32,3200,16]{1,2,0:T(8,128)}, /*index=5*/s32[]{:T(128)}, s32[]{:T(128)}, s32[]{:T(128)}, s32[]{:T(128)}) while((s32[]{:T(128)}, f32[3200,16]{0,1:T(8,128)}, s32[]{:T(128)}, f32[32,3200,16]{1,2,0:T(8,128)}, ...), condition=%wide.region_19.20_spmd, body=%wide.region_18.19_spmd.sunk | while | flops 102406 | bytes 819351 | solution.py:40
  1777.9 28.8 multiply_reduce_fusion
  1823.8 29.4 %collective-permute-start.55 = (bf16[50,11008]{1,0:T(8,128)(2,1)S(1)}, bf16[50,11008]{1,0:T(8,128)(2,1)S(1)}, u32[]{:S(2)}, u32[]{:S(2)}) collective-permute-start(bf16[50,11008]{1,0:T(8,128)(2,1)S(1)} %copy-done.44), channel_id=1, source_target_pairs={{0,7},{1,8},{2,9},{3,10},{4,11},{5,12},{6,13},{7,14},{8,15},{9,16}... | collective-permute-start | bytes 3302408
  1881.3 320.8 %fusion.92 = (bf16[56,2240]{1,0:T(8,128)(2,1)}, bf16[64,1600]{1,0:T(8,128)(2,1)S(1)}, bf16[56,6400]{1,0:T(8,128)(2,1)S(1)}, bf16[112,1600]{1,0:T(8,128)(2,1)S(1)}, bf16[112,100]{1,0:T(8,128)(2,1)S(1)}) fusion(bf16[1600,2240]{1,0:T(8,128)(2,1)} %convolution_convert_fusion.4, bf16[1600,1600]{1,0:T(8,128)(2,1)} %convolution_convert_fusion.5, ...), kind=kCustom, calls=%all-reduce-scatter.7 | all-reduce-scatter fusion | flops 24852480 | bytes 45201792
  2227.3 83.6 %concatenate.51 = bf16[498,11008]{1,0:T(8,128)(2,1)} concatenate(bf16[50,11008]{1,0:T(8,128)(2,1)} %copy-done.43, bf16[64,11008]{1,0:T(8,128)(2,1)} %collective-permute-done.54, bf16[64,11008]{1,0:T(8,128)(2,1)} %collective-permute-done.53, bf16[64,11008]{1,0:T(8,128)(2,1)} %collective-permute-done.52, bf16[64,11008]{1,0:T(8,128)(2,1)} %collective-permute-done.51, ...), dimensions={0} | concatenate | bytes 21927936
  2386.9 19.4 collective-permute-done.46
  2427.5 27.4 concatenate.48
  2522.4 46.1 %all-reduce.38.cloned.1.call-done = (bf16[50,2240]{1,0:T(8,128)(2,1)}, bf16[50,1600]{1,0:T(8,128)(2,1)}, bf16[50,6400]{1,0:T(8,128)(2,1)}, bf16[100,1600]{1,0:T(...) async-done(((bf16[50,2240]{1,0:T(8,128)(2,1)}, bf16[50,1600]{1,0:T(8,128)(2,1)}, bf16[50,6400]{1,0:T(8,128)(2,1)}, bf16[100,1600]{1,0:T(8,128)(2,1)}, ...) | async-done | bytes 2995216 | tf_op jit(solution)/shard_map/psum | solution.py:327
  2578.0 142.4 %all-reduce.36.cloned.1.call-done = (f32[1600]{0:T(1024)}, f32[4,3200]{1,0:T(4,128)}, f32[3200]{0:T(1024)}, f32[3200]{0:T(1024)}, f32[3200]{0:T(1024)}, /*index=5*/f32[1600]{0:T(1024)}, f32[1600]{0:T(1024)}, f32[1600]{0:T(1024)}) async-done(((f32[1600]{0:T(1024)}, f32[4,3200]{1,0:T(4,128)}, f32[3200]{0:T(1024)}, f32[3200]{0:T(1024)}, f32[3200]{0:T(1024)}, /*index=5*/f32[1600]{0:T(1024)}, f32[1600]{0:T(1024)}, ...) | async-done | bytes 115216 | tf_op jit(solution)/shard_map/psum | solution.py:336
  2720.4 142.6 %all-reduce.32.cloned.1.call-done = f32[3200,16]{0,1:T(8,128)} async-done(((f32[3200,16]{0,1:T(8,128)}), f32[3200,16]{0,1:T(8,128)}) %all-reduce.32.cloned.1.call-update) | async-done | bytes 204816 | tf_op jit(solution)/shard_map/psum | solution.py:336
  (832 shorter events, 1268.1 us)
Async XLA Ops:
  7.9 435.3 %all-gather.26.cloned.1.call-start = ((), (), s32[]{:S(2)}) async-start(), calls=%async_computation.4 | async-start | bytes 8515584 | tf_op jit(solution)/shard_map/all_gather | solution.py:104
  8.7 457.3 %all-gather.28.cloned.1.call-start = ((), (), s32[]{:S(2)}) async-start(), calls=%async_computation.5 | async-start | bytes 6150144 | tf_op jit(solution)/shard_map/all_gather | solution.py:105
  9.4 540.9 %all-gather.32.cloned.1.call-start = ((), (), s32[]{:S(2)}) async-start(), calls=%async_computation.7 | async-start | bytes 11421696 | tf_op jit(solution)/shard_map/all_gather | solution.py:109
  10.0 555.3 %all-gather.36.cloned.1.call-start = ((), (), s32[]{:S(2)}) async-start(), calls=%async_computation.9 | async-start | bytes 19329024 | tf_op jit(solution)/shard_map/all_gather | solution.py:111
  10.6 615.5 %all-gather.22.cloned.1.call-start = ((), (), s32[]{:S(2)}) async-start(), calls=%async_computation.2 | async-start | bytes 6758400 | tf_op jit(solution)/shard_map/all_gather | solution.py:31
  173.6 458.5 %all-gather.24.cloned.1.call-start = ((), (), s32[]{:S(2)}) async-start(), calls=%async_computation.3 | async-start | bytes 6758400 | tf_op jit(solution)/shard_map/all_gather | solution.py:31
  426.4 280.5 %all-gather.34.cloned.1.call-start = ((), (), s32[]{:S(2)}) async-start(), calls=%async_computation.8 | async-start | bytes 40685568 | tf_op jit(solution)/shard_map/all_gather | solution.py:110
  427.2 1296.8 %all-gather.20.cloned.1.call-start = ((), (), s32[]{:S(2)}) async-start(), calls=%async_computation | async-start | bytes 6758400 | tf_op jit(solution)/shard_map/all_gather | solution.py:31
  881.3 733.5 %collective-permute-start.24 = (bf16[128,640]{0,1:T(8,128)(2,1)}, bf16[128,640]{0,1:T(8,128)(2,1)}, u32[]{:S(2)}, u32[]{:S(2)}) collective-permute-start(bf16[128,640]{0,1:T(8,128)(2,1)} %get-tuple-element.469), channel_id=1, source_target_pairs={{8,0},{9,1},{10,2},{11,3},{12,4},{13,5},{14,6},{15,7},{16,8},{17,9... | collective-permute-start | bytes 491528 | tf_op jit(solution)/shard_map/ppermute | solution.py:24
  882.8 733.4 %collective-permute-start.23 = (bf16[128,640]{0,1:T(8,128)(2,1)}, bf16[128,640]{0,1:T(8,128)(2,1)}, u32[]{:S(2)}, u32[]{:S(2)}) collective-permute-start(bf16[128,640]{0,1:T(8,128)(2,1)} %get-tuple-element.470), channel_id=1, source_target_pairs={{7,0},{8,1},{9,2},{10,3},{11,4},{12,5},{13,6},{14,7},{15,8},{16,9}... | collective-permute-start | bytes 491528 | tf_op jit(solution)/shard_map/ppermute | solution.py:24
  884.1 739.1 %collective-permute-start.22 = (bf16[128,640]{0,1:T(8,128)(2,1)}, bf16[128,640]{0,1:T(8,128)(2,1)}, u32[]{:S(2)}, u32[]{:S(2)}) collective-permute-start(bf16[128,640]{0,1:T(8,128)(2,1)} %get-tuple-element.471), channel_id=1, source_target_pairs={{6,0},{7,1},{8,2},{9,3},{10,4},{11,5},{12,6},{13,7},{14,8},{15,9},... | collective-permute-start | bytes 491528 | tf_op jit(solution)/shard_map/ppermute | solution.py:24
  885.4 749.4 %collective-permute-start.21 = (bf16[128,640]{0,1:T(8,128)(2,1)}, bf16[128,640]{0,1:T(8,128)(2,1)}, u32[]{:S(2)}, u32[]{:S(2)}) collective-permute-start(bf16[128,640]{0,1:T(8,128)(2,1)} %get-tuple-element.472), channel_id=1, source_target_pairs={{5,0},{6,1},{7,2},{8,3},{9,4},{10,5},{11,6},{12,7},{13,8},{14,9},{... | collective-permute-start | bytes 491528 | tf_op jit(solution)/shard_map/ppermute | solution.py:24
  886.7 751.6 %collective-permute-start.20 = (bf16[128,640]{0,1:T(8,128)(2,1)}, bf16[128,640]{0,1:T(8,128)(2,1)}, u32[]{:S(2)}, u32[]{:S(2)}) collective-permute-start(bf16[128,640]{0,1:T(8,128)(2,1)} %get-tuple-element.473), channel_id=1, source_target_pairs={{4,0},{5,1},{6,2},{7,3},{8,4},{9,5},{10,6},{11,7},{12,8},{13,9},{1... | collective-permute-start | bytes 491528 | tf_op jit(solution)/shard_map/ppermute | solution.py:24
  1161.1 1342.7 %all-reduce.34.cloned.1.call-start = ((), (), s32[]{:S(2)}) async-start(), calls=%async_computation.10 | async-start | bytes 1740800
  1634.8 234.2 %collective-permute-start.54 = (bf16[64,11008]{1,0:T(8,128)(2,1)}, bf16[64,11008]{1,0:T(8,128)(2,1)}, u32[]{:S(2)}, u32[]{:S(2)}) collective-permute-start(bf16[64,11008]{1,0:T(8,128)(2,1)} %fusion.5), channel_id=1, source_target_pairs={{0,6},{1,7},{2,8},{3,9},{4,10},{5,11},{6,12},{7,13},{8,14},{9,15},... | collective-permute-start | bytes 4227080
  1638.3 565.5 %collective-permute-start.53 = (bf16[64,11008]{1,0:T(8,128)(2,1)}, bf16[64,11008]{1,0:T(8,128)(2,1)}, u32[]{:S(2)}, u32[]{:S(2)}) collective-permute-start(bf16[64,11008]{1,0:T(8,128)(2,1)} %fusion.5), channel_id=1, source_target_pairs={{0,5},{1,6},{2,7},{3,8},{4,9},{5,10},{6,11},{7,12},{8,13},{9,14},{... | collective-permute-start | bytes 4227080
  1640.7 578.7 %collective-permute-start.52 = (bf16[64,11008]{1,0:T(8,128)(2,1)}, bf16[64,11008]{1,0:T(8,128)(2,1)}, u32[]{:S(2)}, u32[]{:S(2)}) collective-permute-start(bf16[64,11008]{1,0:T(8,128)(2,1)} %fusion.5), channel_id=1, source_target_pairs={{0,4},{1,5},{2,6},{3,7},{4,8},{5,9},{6,10},{7,11},{8,12},{9,13},{1... | collective-permute-start | bytes 4227080
  1645.2 576.1 %collective-permute-start.51 = (bf16[64,11008]{1,0:T(8,128)(2,1)}, bf16[64,11008]{1,0:T(8,128)(2,1)}, u32[]{:S(2)}, u32[]{:S(2)}) collective-permute-start(bf16[64,11008]{1,0:T(8,128)(2,1)} %fusion.5), channel_id=1, source_target_pairs={{0,3},{1,4},{2,5},{3,6},{4,7},{5,8},{6,9},{7,10},{8,11},{9,12},{10... | collective-permute-start | bytes 4227080
  1867.0 356.2 %collective-permute-start.50 = (bf16[64,11008]{1,0:T(8,128)(2,1)}, bf16[64,11008]{1,0:T(8,128)(2,1)}, u32[]{:S(2)}, u32[]{:S(2)}) collective-permute-start(bf16[64,11008]{1,0:T(8,128)(2,1)} %fusion.5), channel_id=1, source_target_pairs={{0,2},{1,3},{2,4},{3,5},{4,6},{5,7},{6,8},{7,9},{8,10},{9,11},{10,... | collective-permute-start | bytes 4227080
  1869.0 358.3 %collective-permute-start.49 = (bf16[64,11008]{1,0:T(8,128)(2,1)}, bf16[64,11008]{1,0:T(8,128)(2,1)}, u32[]{:S(2)}, u32[]{:S(2)}) collective-permute-start(bf16[64,11008]{1,0:T(8,128)(2,1)} %fusion.5), channel_id=1, source_target_pairs={{0,1},{1,2},{2,3},{3,4},{4,5},{5,6},{6,7},{7,8},{8,9},{9,10},{10,1... | collective-permute-start | bytes 4227080
  2203.8 113.6 %collective-permute-start.35 = (bf16[64,1600]{1,0:T(8,128)(2,1)S(1)}, bf16[64,1600]{1,0:T(8,128)(2,1)}, u32[]{:S(2)}, u32[]{:S(2)}) collective-permute-start(bf16[64,1600]{1,0:T(8,128)(2,1)S(1)} %get-tuple-element.437), channel_id=1, source_target_pairs={{0,6},{1,7},{2,8},{3,9},{4,10},{5,11},{6,12},{7,13},{8,14},{9,15},... | collective-permute-start | bytes 614408
  2335.5 233.0 %all-reduce.38.cloned.1.call-start = ((), (), s32[]{:S(2)}) async-start(), calls=%async_computation.12 | async-start | bytes 6651904 | tf_op jit(solution)/shard_map/psum | solution.py:327
  2457.2 263.2 %all-reduce.36.cloned.1.call-start = ((), (), s32[]{:S(2)}) async-start(), calls=%async_computation.11 | async-start | bytes 266240 | tf_op jit(solution)/shard_map/psum | solution.py:336
  2487.7 375.3 %all-reduce.32.cloned.1.call-start = ((), (), s32[]{:S(2)}) async-start(), calls=%async_computation.1 | async-start | bytes 409600 | tf_op jit(solution)/shard_map/psum | solution.py:336
  (166 other events, 4290.6 us)
Sparse Core Ops, SparseCore 0:
  10.4 93.1 all-gather.29
  105.9 51.5 all-gather.25
  159.8 47.6 all-gather.27
  209.6 58.8 all-gather.31
  270.7 76.6 all-gather.35
  350.2 48.1 all-gather.21
  426.5 50.6 all-gather.23
  479.5 142.7 all-gather.33
  1161.2 220.0 all-gather.19
  2335.7 150.1 all-reduce.33
  2490.3 78.1 all-reduce.37
  2577.1 143.2 all-reduce.35
  2725.7 137.2 all-reduce.31
where the time goes:
time: 2910 us; the launch traced here: 2880 us
  blocking collectives  832 us (29%)
  other arithmetic  688 us (24%)
  waiting for transfers between devices  466 us (16%)
  local copies, waits for them, and re-layouts  433 us (15%)
  matrix products  229 us (8%)
  starting transfers between devices  214 us (7%)
    unnamed x3, blocking collectives  762 us
    dynamic_update_slice x256, other arithmetic, body(): lax.scan(forward_step, jnp.zeros((DI, N_STATE), jnp.float32), (decay_step...  482 us
    unnamed x297, local copies, waits for them, and re-layouts  338 us
    psum x2, waiting for transfers between devices, body(): lax.psum((grad_norm_gain, grad_conv_w, grad_conv_bias, grad_dt_bias, grad...  285 us
    unnamed x32, starting transfers between devices  131 us
    unnamed x45, waiting for transfers between devices  88.2 us
    dot_general x8, matrix products, matmul_last(): lax.dot_general(operand, other, (((1,), (1,)), ((), ())), preferred_eleme...  69.9 us
    ppermute x26, starting transfers between devices, shifted(): return lax.ppermute(value, axis, pairs)  67.1 us
  transfers between devices with their start and end apart: 70, of which 14 were waited for; matrix products, arithmetic and copies ran while one was open for 67% of the time, Pallas kernels for 0%

commit v1 on v0

v1 whole, which is shorter than its diff:
```python
import functools

import jax
import jax.numpy as jnp
from jax import lax
from jax.experimental import pallas as pl
from jax.experimental.pallas import tpu as pltpu
from jax.sharding import PartitionSpec as P

D = 1600
HEADS = 25
KV_HEADS = 5
GROUP = HEADS // KV_HEADS
HEAD_DIM = 64
DI = 3200
N_STATE = 16
CONV = 4
DT_RANK = 100
FF = 5504
WINDOW = 1024
EPS = 1e-05
NEG_BIG = -1e30
LOG2E = 1.4426950408889634
LN2 = 0.6931471805599453

NX = 4
NC = 32
T = 128
KEYS = WINDOW + T
ROWS = 50
ROWS_P = 56
ROWS_64 = 64
DP = NC * ROWS_P
CH = DI // NX
CHP = 896
FFX = FF // NX
FFP = 1408
CSUB = CH // NC
FSUB = FFX // NC
QKV = 2240
QKV_P = 2304
AO_P = 1664
XD = 256

F32 = jnp.float32
BF16 = jnp.bfloat16
VMEM_LIMIT = 60 * 1024 * 1024


def dot(a, b, ca, cb, out=F32):
    return lax.dot_general(a, b, (((ca,), (cb,)), ((), ())), preferred_element_type=F32).astype(out)


def norm_scale(values, gain):
    return values * lax.rsqrt(jnp.mean(values * values, axis=-1, keepdims=True) + EPS) * gain


RIGHT = [(i, (i + 1) % NX) for i in range(NX)]
LEFT = [(i, (i - 1) % NX) for i in range(NX)]


def gather_x(v):
    half = v.shape[0] // 2
    before = lax.ppermute(v, "seq", RIGHT)
    after = lax.ppermute(v, "seq", LEFT)
    far_a = lax.ppermute(before[:half], "seq", RIGHT)
    far_b = lax.ppermute(after[half:], "seq", LEFT)
    return [v, after, jnp.concatenate([far_a, far_b]), before]


def scatter_x(parts):
    half = parts[0].shape[0] // 2
    from_left = lax.ppermute(parts[2][:half], "seq", RIGHT)
    from_right = lax.ppermute(parts[2][half:], "seq", LEFT)
    to_right = jnp.concatenate(
        [(parts[1][:half].astype(F32) + from_left.astype(F32)).astype(BF16), parts[1][half:]]
    )
    to_left = jnp.concatenate(
        [parts[3][:half], (parts[3][half:].astype(F32) + from_right.astype(F32)).astype(BF16)]
    )
    a = lax.ppermute(to_right, "seq", RIGHT)
    b = lax.ppermute(to_left, "seq", LEFT)
    return parts[0].astype(F32) + a.astype(F32) + b.astype(F32)


def total_x(v):
    blocks = [v[:, k * T : (k + 1) * T] for k in range(NX)]

    def turned(by):
        return jnp.concatenate([blocks[(k + by) % NX] for k in range(NX)], axis=1)

    a = lax.ppermute(turned(1), "seq", RIGHT)
    b = lax.ppermute(turned(-1), "seq", LEFT)
    c = lax.ppermute(turned(2), "seq", [(i, (i + 2) % NX) for i in range(NX)])
    return v.astype(F32) + a.astype(F32) + b.astype(F32) + c.astype(F32)


def in_order(pieces, place):
    out = []
    for j in range(NX):
        value = pieces[0]
        for k in range(1, NX):
            value = jnp.where(place == (j - k) % NX, pieces[k], value)
        out.append(value)
    return out


def place_index(x, z, y, c):
    return x * NC + z * 8 + y * 2 + c


TURN = [
    (place_index(x, z, y, c), place_index(z, y, 2 * c + x // 2, x % 2))
    for x in range(4)
    for z in range(4)
    for y in range(4)
    for c in range(2)
]
TURN_BACK = [(b, a) for a, b in TURN]


def shift_ctx(v, by):
    return lax.ppermute(v, "ctx", [(i, i + by) for i in range(NC) if 0 <= i + by < NC])


def tie(*values):
    return lax.optimization_barrier(values)


SWAP = [(i, i ^ 1) for i in range(NC)]


def carried(part, rate2, index, reverse):
    sign = -1 if reverse else 1

    def after(first, then):
        state = then[:, :N_STATE] + jnp.exp2(rate2[None] * then[:, N_STATE:]) * first[:, :N_STATE]
        return jnp.concatenate([state, first[:, N_STATE:] + then[:, N_STATE:]], axis=1)

    def keep(flag, v):
        return jnp.where(flag, v, 0.0)

    def send(v, pairs):
        flat = lax.ppermute(v.reshape(NX * (N_STATE + 1), CHP).astype(BF16), "ctx", pairs)
        return flat.astype(F32).reshape(NX, N_STATE + 1, CHP)

    core = index % 2
    y = (index // 2) % 4
    if reverse:
        core, y = 1 - core, 3 - y
    other = send(part, SWAP)
    inside = keep(core == 1, other)
    chip = jnp.where(core == 1, after(other, part), after(part, other))
    rows = []
    for k in range(1, 4):
        rows.append(send(chip, [(i, i // 8 * 8 + (i + sign * 2 * k) % 8) for i in range(NC)]))
    pre = [keep(y >= k, rows[k - 1]) for k in range(1, 4)]
    suc = [keep(y < k, rows[k - 1]) for k in range(1, 4)]
    row_pre = after(after(pre[2], pre[1]), pre[0])
    row = after(after(after(after(row_pre, chip), suc[2]), suc[1]), suc[0])
    planes = []
    for k in range(1, 4):
        by = sign * 8 * k
        planes.append(send(row, [(i, i + by) for i in range(NC) if 0 <= i + by < NC]))
    plane_pre = after(after(planes[2], planes[1]), planes[0])
    return after(after(plane_pre, row_pre), inside)[:, :N_STATE]


def key_window(own, core):
    mine = jnp.concatenate([shift_ctx(own, 2 * k) for k in (4, 3, 2, 1)] + [own])
    other = lax.ppermute(mine, "ctx", SWAP)
    odd = jnp.where(core == 0, other[: 4 * T], other[T:])
    blocks = []
    for k in range(4):
        blocks += [mine[k * T : (k + 1) * T], odd[k * T : (k + 1) * T]]
    return jnp.concatenate(blocks + [mine[4 * T :]])


def key_window_back(grad, core):
    blocks = [grad[k * T : (k + 1) * T] for k in range(9)]
    other = lax.ppermute(jnp.concatenate(blocks[1::2]).astype(BF16), "ctx", SWAP).astype(F32)
    none = jnp.zeros_like(blocks[0])
    mine = jnp.concatenate(blocks[::2]) + jnp.where(
        core == 0, jnp.concatenate([none, other]), jnp.concatenate([other, none])
    )
    total = mine[4 * T :]
    for k in range(1, 5):
        term = mine[(4 - k) * T : (5 - k) * T].astype(BF16)
        total = total + shift_ctx(term, -2 * k).astype(F32)
    return total


TILES = CHP // 128


def lanes(j):
    return slice(j * 128, (j + 1) * 128)


def spread(source, target):
    for t in range(T):
        target[t] = jnp.broadcast_to(source[:, t : t + 1], (N_STATE, 128))


CHUNK = 16
WIDE = CHUNK * N_STATE
SCAN_GROUPS = ((0, 1, 2, 3), (4, 5, 6))
ADJOINT_GROUPS = ((0, 1, 2), (3, 4), (5, 6))


def chunk_diagonal():
    column = lax.broadcasted_iota(jnp.int32, (T, WIDE), 1) // N_STATE
    return column == lax.broadcasted_iota(jnp.int32, (T, WIDE), 0) % CHUNK


def chunk_rows(coef):
    pick = lax.broadcasted_iota(jnp.int32, (N_STATE, WIDE), 1) % N_STATE
    pick = (pick == lax.broadcasted_iota(jnp.int32, (N_STATE, WIDE), 0)).astype(BF16)
    wide = dot(coef.astype(BF16), pick, 0, 0)
    return jnp.where(chunk_diagonal(), wide, 0.0).astype(BF16)


def lane_sums(partial):
    flat = partial.reshape(T * N_STATE, 128).astype(BF16)
    wide = dot(flat, jnp.ones((128, 128), BF16), 1, 0).reshape(T, N_STATE, 128)
    token = lax.broadcasted_iota(jnp.int32, (T, N_STATE, 128), 0)
    lane = lax.broadcasted_iota(jnp.int32, (T, N_STATE, 128), 2)
    return jnp.sum(jnp.where(token == lane, wide, 0.0), axis=0)


def token_rows(chunk):
    return pl.ds(pl.multiple_of(chunk * CHUNK, CHUNK), CHUNK)


def state_rows(token):
    return pl.ds(pl.multiple_of(token * N_STATE, N_STATE), N_STATE)


def forward_scan(step, drive, spread_b, rate2, group, states, emit):
    rates = [rate2[:, lanes(j)] for j in group]

    def one(chunk, states):
        rows = token_rows(chunk)
        steps = [step[rows, lanes(j)] for j in group]
        drives = [drive[rows, lanes(j)] for j in group]
        states = list(states)
        for r in range(CHUNK):
            b_here = spread_b[chunk * CHUNK + r]
            for k, j in enumerate(group):
                a = jnp.exp2(steps[k][r : r + 1] * rates[k])
                states[k] = a * states[k] + drives[k][r : r + 1] * b_here
                emit(chunk * CHUNK + r, j, states[k])
        return tuple(states)

    return lax.fori_loop(0, T // CHUNK, one, tuple(states))


def chunks():
    return [(slice(c * CHUNK, (c + 1) * CHUNK), slice(c * WIDE, (c + 1) * WIDE)) for c in range(T // CHUNK)]


def scan_end_kernel(step, act, b_t, rate2, out, spread_b, drive):
    spread(b_t, spread_b)
    drive[...] = step[...] * act[...].astype(F32)
    for group in SCAN_GROUPS:
        zero = [jnp.zeros((N_STATE, 128), F32) for _ in group]
        states = forward_scan(step, drive, spread_b, rate2, group, zero, lambda t, j, h: None)
        for k, j in enumerate(group):
            out[0, :N_STATE, lanes(j)] = states[k]
    out[0, N_STATE:, :] = jnp.sum(step[...], axis=0, keepdims=True)


def scan_kernel(
    step, act, gate_z, b_t, c_t, start, rate2, skip, states_out, scan_out, gated, spread_b, drive, sum_c
):
    spread(b_t, spread_b)
    drive[...] = step[...] * act[...].astype(F32)
    sum_c[...] = chunk_rows(c_t[...])

    def emit(t, j, h):
        states_out[0, state_rows(t), lanes(j)] = h.astype(BF16)

    for group in SCAN_GROUPS:
        forward_scan(step, drive, spread_b, rate2, group, [start[0, :, lanes(j)] for j in group], emit)
    for rows, wide in chunks():
        y = dot(sum_c[rows, :], states_out[0, wide, :], 1, 0) + skip[...] * act[rows, :].astype(F32)
        scan_out[rows, :] = y
        z = gate_z[rows, :]
        gated[rows, :] = (y * (z * jax.nn.sigmoid(z))).astype(BF16)


def adjoint_end_kernel(step, g_scan, c_t, rate2, out, spread_c):
    spread(c_t, spread_c)
    for group in SCAN_GROUPS:
        rates = [rate2[:, lanes(j)] for j in group]

        def one(lap, adjoints):
            chunk = T // CHUNK - 1 - lap
            rows = token_rows(chunk)
            steps = [step[rows, lanes(j)] for j in group]
            grads = [g_scan[rows, lanes(j)] for j in group]
            adjoints = list(adjoints)
            for r in reversed(range(CHUNK)):
                c_here = spread_c[chunk * CHUNK + r]
                for k in range(len(group)):
                    a = jnp.exp2(steps[k][r : r + 1] * rates[k])
                    adjoints[k] = a * (grads[k][r : r + 1] * c_here + adjoints[k])
            return tuple(adjoints)

        zero = tuple(jnp.zeros((N_STATE, 128), F32) for _ in group)
        adjoints = lax.fori_loop(0, T // CHUNK, one, zero)
        for k, j in enumerate(group):
            out[0, :N_STATE, lanes(j)] = adjoints[k]
    out[0, N_STATE:, :] = jnp.sum(step[...], axis=0, keepdims=True)


def adjoint_kernel(
    step, act, g_scan, b_t, c_t, states, start, later, rate2, skip,
    g_step, g_act, g_rate, g_b, g_c, spread_c, drive, sum_b, adjoint, flow_rate, part_b, part_c,
):
    spread(c_t, spread_c)
    drive[...] = step[...] * act[...].astype(F32)
    sum_b[...] = chunk_rows(b_t[...])
    ones = chunk_diagonal()[:CHUNK].astype(BF16)
    for group in ADJOINT_GROUPS:
        rates = [rate2[:, lanes(j)] for j in group]

        def one(lap, carry):
            chunk = T // CHUNK - 1 - lap
            rows = token_rows(chunk)
            steps = [step[rows, lanes(j)] for j in group]
            grads = [g_scan[rows, lanes(j)] for j in group]
            drives = [drive[rows, lanes(j)] for j in group]
            adjoints, totals = list(carry[0]), list(carry[1])
            last = chunk * CHUNK + CHUNK - 1
            held = [states[0, state_rows(last), lanes(j)].astype(F32) for j in group]
            for r in reversed(range(CHUNK)):
                t = chunk * CHUNK + r
                here = state_rows(t)
                c_here = spread_c[t]
                b_sum = c_sum = None
                for k, j in enumerate(group):
                    g_row = grads[k][r : r + 1]
                    lam = g_row * c_here + adjoints[k]
                    adjoint[here, lanes(j)] = lam.astype(BF16)
                    step_row = steps[k][r : r + 1]
                    m = jnp.exp2(step_row * rates[k]) * lam
                    b_term = lam * drives[k][r : r + 1]
                    c_term = held[k] * g_row
                    b_sum = b_term if b_sum is None else b_sum + b_term
                    c_sum = c_term if c_sum is None else c_sum + c_term
                    before = states[0, state_rows(jnp.maximum(t - 1, 0)), lanes(j)].astype(F32)
                    if r == 0:
                        before = jnp.where(chunk == 0, start[0, :, lanes(j)], before)
                    flow = m * before
                    totals[k] = totals[k] + flow * step_row
                    flow_rate[here, lanes(j)] = (flow * rates[k]).astype(BF16)
                    adjoints[k] = m
                    held[k] = before
                if group[0] == 0:
                    part_b[t] = b_sum
                    part_c[t] = c_sum
                else:
                    part_b[t] += b_sum
                    part_c[t] += c_sum
            return (tuple(adjoints), tuple(totals))

        zero = tuple(jnp.zeros((N_STATE, 128), F32) for _ in group)
        first = tuple(later[0, :, lanes(j)] for j in group)
        _, totals = lax.fori_loop(0, T // CHUNK, one, (first, zero))
        for k, j in enumerate(group):
            g_rate[0, :, lanes(j)] = totals[k]
    for rows, wide in chunks():
        lam_b = dot(sum_b[rows, :], adjoint[wide, :], 1, 0)
        flow_sum = dot(ones, flow_rate[wide, :], 1, 0)
        g_step[rows, :] = flow_sum * LN2 + act[rows, :].astype(F32) * lam_b
        g_act[rows, :] = step[rows, :] * lam_b + skip[...] * g_scan[rows, :]
    g_b[...] = lane_sums(part_b[...])
    g_c[...] = lane_sums(part_c[...])


def seq_call(kernel, ins, outs, scratch, cost):
    def spec(shape, kind):
        if kind == "rows":
            return pl.BlockSpec((shape[0] // NX,) + tuple(shape[1:]), lambda s: (s, 0))
        if kind == "lanes":
            return pl.BlockSpec((shape[0], shape[1] // NX), lambda s: (0, s))
        if kind == "lead":
            return pl.BlockSpec((1,) + tuple(shape[1:]), lambda s: (s, 0, 0))
        return pl.BlockSpec(tuple(shape), lambda s: (0,) * len(shape))

    return pl.pallas_call(
        kernel,
        grid=(NX,),
        in_specs=[spec(a.shape, kind) for a, kind in ins],
        out_specs=[spec(shape, kind) for shape, _, kind in outs],
        out_shape=[jax.ShapeDtypeStruct(shape, dtype) for shape, dtype, _ in outs],
        scratch_shapes=scratch,
        compiler_params=pltpu.CompilerParams(vmem_limit_bytes=VMEM_LIMIT),
        cost_estimate=cost,
    )(*[a for a, _ in ins])


def cost(us):
    return pl.CostEstimate(flops=int(us * 1e9), bytes_accessed=int(us * 1e6), transcendentals=0)


def visible_keys(lowest):
    t = lax.broadcasted_iota(jnp.int32, (T, KEYS), 0)
    s = lax.broadcasted_iota(jnp.int32, (T, KEYS), 1)
    return (s > t) & (s <= t + WINDOW) & (s >= lowest)


def attend_kernel(lowest, q, k, v, out, lse):
    seen = visible_keys(lowest[0])
    for g in range(GROUP):
        rows = slice(g * T, (g + 1) * T)
        scores = jnp.where(seen, dot(q[0, rows, :], k[0], 1, 1), NEG_BIG)
        peak = jnp.max(scores, axis=-1, keepdims=True)
        raised = jnp.exp(scores - peak)
        mass = jnp.sum(raised, axis=-1, keepdims=True)
        probs = (raised / mass).astype(BF16)
        out[0, rows, :] = dot(probs, v[0], 1, 0, BF16)
        lse[0, rows, :] = peak + jnp.log(mass)


def attend_back_kernel(lowest, q, k, v, g_out, lse, g_q, g_k, g_v):
    seen = visible_keys(lowest[0])
    for g in range(GROUP):
        rows = slice(g * T, (g + 1) * T)
        q_here = q[0, rows, :]
        g_here = g_out[0, rows, :]
        scores = jnp.where(seen, dot(q_here, k[0], 1, 1), NEG_BIG)
        probs = jnp.exp(scores - lse[0, rows, :])
        g_probs = dot(g_here, v[0], 1, 1)
        inner = jnp.sum(probs * g_probs, axis=-1, keepdims=True)
        g_scores = (probs * (g_probs - inner)).astype(BF16)
        g_q[0, rows, :] = (dot(g_scores, k[0], 1, 0) * HEAD_DIM ** (-0.5)).astype(BF16)
        k_term = dot(g_scores, q_here, 0, 0)
        v_term = dot(probs.astype(BF16), g_here, 0, 0)
        if g == 0:
            g_k[0] = k_term
            g_v[0] = v_term
        else:
            g_k[0] += k_term
            g_v[0] += v_term


def head_call(kernel, lowest, ins, outs, us):
    def spec(shape):
        return pl.BlockSpec((1,) + tuple(shape[1:]), lambda h: (h, 0, 0))

    return pl.pallas_call(
        kernel,
        grid=(KV_HEADS,),
        in_specs=[pl.BlockSpec(memory_space=pltpu.SMEM)] + [spec(a.shape) for a in ins],
        out_specs=[spec(shape) for shape, _ in outs],
        out_shape=[jax.ShapeDtypeStruct(shape, dtype) for shape, dtype in outs],
        compiler_params=pltpu.CompilerParams(vmem_limit_bytes=VMEM_LIMIT),
        cost_estimate=cost(us),
    )(lowest, *ins)


def split_queries(v):
    return v.reshape(T, KV_HEADS, GROUP, HEAD_DIM).transpose(1, 2, 0, 3).reshape(KV_HEADS, GROUP * T, HEAD_DIM)


def join_queries(v):
    return v.reshape(KV_HEADS, GROUP, T, HEAD_DIM).transpose(2, 0, 1, 3).reshape(T, HEADS * HEAD_DIM)


def split_keys(v):
    return v.reshape(v.shape[0], KV_HEADS, HEAD_DIM).transpose(1, 0, 2)


def join_keys(v):
    return v.transpose(1, 0, 2).reshape(v.shape[1], KV_HEADS * HEAD_DIM)


def pad_to(v, rows, columns):
    return jnp.pad(v, ((0, rows - v.shape[0]), (0, columns - v.shape[1])))


def rows_64(v):
    turned = v.T.reshape(NC, ROWS_P, v.shape[0])
    return jnp.pad(turned, ((0, 0), (0, ROWS_64 - ROWS_P), (0, 0))).reshape(NC * ROWS_64, v.shape[0])


def products_kernel(count, *refs):
    out = refs[-1]
    at = 0
    for k in range(count):
        width = refs[2 * k + 1].shape[1]
        out[:, at : at + width] = dot(refs[2 * k][...], refs[2 * k + 1][...], 1, 0, BF16)
        at += width


def products(pairs, us):
    block = 512
    rows = NC * ROWS_64
    width = sum(b.shape[1] for _, b in pairs)
    specs = []
    for a, b in pairs:
        specs.append(pl.BlockSpec((block, a.shape[1]), lambda i: (i, 0)))
        specs.append(pl.BlockSpec(b.shape, lambda i: (0, 0)))
    return pl.pallas_call(
        functools.partial(products_kernel, len(pairs)),
        grid=(rows // block,),
        in_specs=specs,
        out_specs=pl.BlockSpec((block, width), lambda i: (i, 0)),
        out_shape=jax.ShapeDtypeStruct((rows, width), BF16),
        compiler_params=pltpu.CompilerParams(vmem_limit_bytes=VMEM_LIMIT),
        cost_estimate=cost(us),
    )(*[v for pair in pairs for v in pair])


def rows_sum(v):
    return lax.psum_scatter(v, "ctx", scatter_dimension=0, tiled=True)


def ring_sum(v, dim, place, plus, minus):
    parts = [lax.dynamic_index_in_dim(v, (place + k) % 4, dim, False) for k in range(4)]
    half = v.shape[-1] // 2
    from_left = lax.ppermute(parts[2][..., :half], "ctx", plus)
    from_right = lax.ppermute(parts[2][..., half:], "ctx", minus)
    to_right = jnp.concatenate(
        [(parts[1][..., :half].astype(F32) + from_left.astype(F32)).astype(BF16), parts[1][..., half:]], axis=-1
    )
    to_left = jnp.concatenate(
        [parts[3][..., :half], (parts[3][..., half:].astype(F32) + from_right.astype(F32)).astype(BF16)], axis=-1
    )
    a = lax.ppermute(to_right, "ctx", plus)
    b = lax.ppermute(to_left, "ctx", minus)
    return parts[0].astype(F32) + a.astype(F32) + b.astype(F32)


def ring_pairs(stride, by):
    return [(i, i + (((i // stride) % 4 + by) % 4 - (i // stride) % 4) * stride) for i in range(NC)]


def rows_sum_by_rings(v, index, y_first):
    core, y, z = index % 2, (index // 2) % 4, index // 8
    width = v.shape[1]
    v = v.reshape(NC // 2, 2, ROWS_P, width)
    other = lax.ppermute(lax.dynamic_index_in_dim(v, 1 - core, 1, False), "ctx", SWAP)
    v = lax.dynamic_index_in_dim(v, core, 1, False).astype(F32) + other.astype(F32)
    v = v.astype(BF16).reshape(4, 4, ROWS_P, width)
    along_y = (y, ring_pairs(2, 1), ring_pairs(2, -1))
    along_z = (z, ring_pairs(8, 1), ring_pairs(8, -1))
    if y_first:
        return ring_sum(ring_sum(v, 1, *along_y).astype(BF16), 0, *along_z)
    return ring_sum(ring_sum(v, 0, *along_z).astype(BF16), 0, *along_y)


def body(
    tokens,
    norm_gain,
    qkv_weight,
    attn_out_weight,
    in_weight,
    conv_weight,
    conv_bias,
    xproj_weight,
    dt_weight,
    dt_bias,
    decay_log,
    skip_gain,
    mamba_out_weight,
    attn_gain,
    mamba_gain,
    ffn_gain,
    gate_up_weight,
    down_weight,
    cotangent,
):
    x = lax.axis_index("seq")
    index = lax.axis_index("ctx")

    def columns(v, first, count):
        return lax.dynamic_slice_in_dim(v, first, count, v.ndim - 1)

    def order(count, size, rows):
        place = lax.broadcasted_iota(jnp.int32, (size, DP), 1)
        source = place // ROWS_P * rows + place % ROWS_P
        hit = (source == lax.broadcasted_iota(jnp.int32, (size, DP), 0)) & (place % ROWS_P < rows)
        return lax.optimization_barrier((hit & (source < count)).astype(BF16))

    widen_m = order(D, D, ROWS)
    widen_channels = order(CH, CHP, CSUB)
    widen_hidden = order(FFX, FFP, FSUB)

    def widen(v, matrix=widen_m):
        return dot(v, matrix, 1, 0, BF16)

    def narrow(v, matrix=widen_m):
        return dot(v.astype(BF16), matrix, 1, 1)

    by_channel = pad_to(jnp.concatenate([xproj_weight, dt_weight], axis=1), 2 * ROWS, XD)
    first = jnp.concatenate(
        [
            pad_to(columns(in_weight, x * CH, CH), ROWS_P, CHP),
            pad_to(columns(in_weight, DI + x * CH, CH), ROWS_P, CHP),
            pad_to(by_channel[:ROWS], ROWS_P, XD),
            pad_to(by_channel[ROWS:], ROWS_P, XD),
        ],
        axis=1,
    )
    first = lax.all_gather(first, "ctx", axis=0, tiled=True)
    sub_mamba = lax.dynamic_slice_in_dim(mamba_out_weight, x * CSUB, CSUB, 0)
    sub_down = lax.dynamic_slice_in_dim(down_weight, x * FSUB, FSUB, 0)
    sub_wide = lax.ppermute(
        jnp.concatenate([pad_to(sub_down, 48, D), pad_to(sub_mamba, 32, D)]), ("seq", "ctx"), TURN
    )
    second = jnp.concatenate(
        [
            pad_to(qkv_weight, ROWS_P, QKV_P),
            pad_to(attn_out_weight, ROWS_P, AO_P),
            pad_to(sub_wide[48 : 48 + CSUB], ROWS_P, AO_P),
        ],
        axis=1,
    )
    second = lax.all_gather(second, "ctx", axis=0, tiled=True)
    third = jnp.concatenate(
        [
            pad_to(columns(gate_up_weight, x * FFX, FFX), ROWS_P, FFP),
            pad_to(columns(gate_up_weight, FF + x * FFX, FFX), ROWS_P, FFP),
            pad_to(sub_wide[:FSUB], ROWS_P, AO_P),
        ],
        axis=1,
    )
    third = lax.all_gather(third, "ctx", axis=0, tiled=True)
    w_in = first[:, : 2 * CHP]
    small = first[:, 2 * CHP :].reshape(NC, ROWS_P, 2 * XD)
    small = lax.dynamic_slice_in_dim(small, x * (NC // NX), NC // NX, 0)[:, :ROWS]
    small = jnp.stack([small[:, :, :XD], small[:, :, XD:]], axis=1).reshape(CH, XD)
    w_small = pad_to(small, CHP, XD)
    w_xproj = w_small[:, : DT_RANK + 2 * N_STATE]
    w_dt = w_small[:, DT_RANK + 2 * N_STATE : 2 * DT_RANK + 2 * N_STATE]
    w_qkv = second[:, :QKV]
    w_attn = second[:, QKV_P : QKV_P + D]
    w_mamba = second[:, QKV_P + AO_P :]
    w_gate_up = third[:, : 2 * FFP]
    w_down = third[:, 2 * FFP :]

    def channel(v):
        part = columns(v, x * CH, CH)
        return jnp.pad(part, ((0, 0),) * (v.ndim - 1) + ((0, CHP - CH),))

    taps = channel(conv_weight)
    conv_b = channel(conv_bias)[None]
    dt_b = channel(dt_bias)[None]
    skip = channel(skip_gain)[None]
    decay_rate = -jnp.exp(channel(decay_log.T))
    rate2 = decay_rate * LOG2E

    inputs = tokens.astype(F32)
    normed_f, norm1_pullback = jax.vjp(norm_scale, inputs, norm_gain)
    normed = widen(normed_f.astype(BF16))
    normed_all = jnp.concatenate(gather_x(normed))
    cot_all = jnp.concatenate(gather_x(pad_to(cotangent, T, AO_P)))

    in_proj = dot(normed_all, w_in, 1, 0)
    conv_in = in_proj[:, :CHP].reshape(NX, T, CHP)
    gate_z = in_proj[:, CHP:]
    tails = shift_ctx(conv_in[:, T - (CONV - 1) :].reshape(NX * (CONV - 1), CHP), 1)
    padded = jnp.concatenate([tails.reshape(NX, CONV - 1, CHP), conv_in], axis=1)
    conv_sum = conv_b[None]
    for j in range(CONV):
        conv_sum = conv_sum + taps[j] * padded[:, j : j + T]
    conv_sum = conv_sum.reshape(NX * T, CHP)
    act_f, conv_pullback = jax.vjp(jax.nn.silu, conv_sum)
    act = act_f.astype(BF16)
    xproj_t = total_x(dot(w_xproj, act, 0, 1, BF16))
    dt_low_t = xproj_t[:DT_RANK].astype(BF16)
    b_t = xproj_t[DT_RANK : DT_RANK + N_STATE]
    c_t = xproj_t[DT_RANK + N_STATE :]
    pre = dot(dt_low_t, w_dt, 0, 1) + dt_b
    step = jax.nn.softplus(pre)
    (scan_end,) = seq_call(
        scan_end_kernel,
        [(step, "rows"), (act, "rows"), (b_t, "lanes"), (rate2, "all")],
        [((NX, N_STATE + 1, CHP), F32, "lead")],
        [pltpu.VMEM((T, N_STATE, 128), F32), pltpu.VMEM((T, CHP), F32)],
        cost(8),
    )
    start = carried(scan_end, rate2, index, False)

    projected = dot(normed, w_qkv, 1, 0, BF16)
    kv_own = projected[:, D:]
    core = index % 2
    kv = key_window(kv_own, core)
    queries = split_queries(projected[:, :D] * jnp.asarray(HEAD_DIM ** (-0.5), BF16))
    keys = split_keys(kv[:, : KV_HEADS * HEAD_DIM])
    values = split_keys(kv[:, KV_HEADS * HEAD_DIM :])
    lowest = jnp.maximum(0, WINDOW - index * T).astype(jnp.int32).reshape(1)
    attended_h, lse = head_call(
        attend_kernel,
        lowest,
        [queries, keys, values],
        [((KV_HEADS, GROUP * T, HEAD_DIM), BF16), ((KV_HEADS, GROUP * T, 1), F32)],
        12,
    )
    attended = widen(join_queries(attended_h))
    attn_branch = dot(attended, w_attn, 1, 0)

    states, scan_out, gated = seq_call(
        scan_kernel,
        [
            (step, "rows"),
            (act, "rows"),
            (gate_z, "rows"),
            (b_t, "lanes"),
            (c_t, "lanes"),
            (start, "lead"),
            (rate2, "all"),
            (skip, "all"),
        ],
        [
            ((NX, T * N_STATE, CHP), BF16, "lead"),
            ((NX * T, CHP), F32, "rows"),
            ((NX * T, CHP), BF16, "rows"),
        ],
        [
            pltpu.VMEM((T, N_STATE, 128), F32),
            pltpu.VMEM((T, CHP), F32),
            pltpu.VMEM((T, WIDE), BF16),
        ],
        cost(14),
    )
    gated = widen(gated, widen_channels)
    mamba_terms = dot(gated, w_mamba, 1, 0, BF16)
    mamba_branch = scatter_x([mamba_terms[k * T : (k + 1) * T] for k in range(NX)])[:, :D]

    def mixing(attn_part, mamba_part, gain_attn, gain_mamba):
        return 0.5 * (norm_scale(attn_part, gain_attn) + norm_scale(mamba_part, gain_mamba))

    mixed, mix_pullback = jax.vjp(mixing, attn_branch, mamba_branch, attn_gain, mamba_gain)
    residual = inputs + mixed
    ffn_f, norm2_pullback = jax.vjp(norm_scale, residual, ffn_gain)
    ffn_all = jnp.concatenate(gather_x(widen(ffn_f.astype(BF16))))
    g_hidden = narrow(dot(cot_all, w_down, 1, 1, BF16), widen_hidden)
    ffn_all, g_hidden = tie(ffn_all, g_hidden)
    gate_up = dot(ffn_all, w_gate_up, 1, 0)

    def swiglu(gate, up):
        return jax.nn.silu(gate) * up

    hidden_f, swiglu_pullback = jax.vjp(swiglu, gate_up[:, :FFP], gate_up[:, FFP:])
    hidden = widen(hidden_f.astype(BF16), widen_hidden)
    g_gate, g_up = swiglu_pullback(g_hidden)
    g_gate_up = jnp.concatenate([g_gate.astype(BF16), g_up.astype(BF16)], axis=1)
    g_ffn_terms = dot(g_gate_up, w_gate_up, 1, 1, BF16)
    g_ffn_in = narrow(scatter_x([g_ffn_terms[k * T : (k + 1) * T] for k in range(NX)]))
    down_terms = dot(hidden, w_down, 1, 0, BF16)
    down_sum = scatter_x([down_terms[k * T : (k + 1) * T] for k in range(NX)])
    output = (residual + down_sum[:, :D]).astype(BF16)
    g_norm2, g_ffn_gain = norm2_pullback(g_ffn_in)
    g_residual = cotangent.astype(F32) + g_norm2
    g_attn_f, g_mamba_f, g_attn_gain, g_mamba_gain = mix_pullback(g_residual)
    g_attn = g_attn_f.astype(BF16)
    g_mamba_all = jnp.concatenate(gather_x(pad_to(g_mamba_f.astype(BF16), T, AO_P)))

    ffn_term = products([(rows_64(ffn_all), g_gate_up), (rows_64(hidden), cot_all)], 12)
    ffn_sum = rows_sum(ffn_term)
    g_mamba_all, ffn_term = tie(g_mamba_all, ffn_term)

    (g_gated,) = tie(narrow(dot(g_mamba_all, w_mamba, 1, 1, BF16), widen_channels))
    silu_z, gate_pullback = jax.vjp(jax.nn.silu, gate_z)
    g_scan = g_gated * silu_z
    (g_gate_z,) = gate_pullback(g_gated * scan_out)
    g_skip = jnp.sum(g_scan * act.astype(F32), axis=0)
    (adjoint_end,) = seq_call(
        adjoint_end_kernel,
        [(step, "rows"), (g_scan, "rows"), (c_t, "lanes"), (rate2, "all")],
        [((NX, N_STATE + 1, CHP), F32, "lead")],
        [pltpu.VMEM((T, N_STATE, 128), F32)],
        cost(8),
    )
    later = carried(adjoint_end, rate2, index, True)

    g_attended = narrow(dot(g_attn, w_attn, 1, 1, BF16)).astype(BF16)
    g_queries, g_keys, g_values = head_call(
        attend_back_kernel,
        lowest,
        [queries, keys, values, split_queries(g_attended), lse],
        [
            ((KV_HEADS, GROUP * T, HEAD_DIM), BF16),
            ((KV_HEADS, KEYS, HEAD_DIM), F32),
            ((KV_HEADS, KEYS, HEAD_DIM), F32),
        ],
        25,
    )
    g_kv = jnp.concatenate([join_keys(g_keys), join_keys(g_values)], axis=1)
    g_kv = key_window_back(g_kv, core)
    g_projected = jnp.concatenate([join_queries(g_queries), g_kv.astype(BF16)], axis=1)
    branch_term = products(
        [(rows_64(attended), pad_to(g_attn, T, AO_P)), (rows_64(gated), g_mamba_all)], 8
    )
    branch_term, ffn_sum = tie(branch_term, ffn_sum)
    branch_sum = rows_sum(branch_term)
    qkv_term = dot(normed, pad_to(g_projected, T, QKV_P), 0, 0, BF16)
    qkv_sum = rows_sum_by_rings(qkv_term, index, True)
    g_normed_attn = dot(g_projected, w_qkv, 1, 1)
    later, g_queries = tie(later, g_queries)

    g_step, g_act, g_rate, g_b, g_c = seq_call(
        adjoint_kernel,
        [
            (step, "rows"),
            (act, "rows"),
            (g_scan, "rows"),
            (b_t, "lanes"),
            (c_t, "lanes"),
            (states, "lead"),
            (start, "lead"),
            (later, "lead"),
            (rate2, "all"),
            (skip, "all"),
        ],
        [
            ((NX * T, CHP), F32, "rows"),
            ((NX * T, CHP), F32, "rows"),
            ((NX, N_STATE, CHP), F32, "lead"),
            ((N_STATE, NX * T), F32, "lanes"),
            ((N_STATE, NX * T), F32, "lanes"),
        ],
        [
            pltpu.VMEM((T, N_STATE, 128), F32),
            pltpu.VMEM((T, CHP), F32),
            pltpu.VMEM((T, WIDE), BF16),
            pltpu.VMEM((T * N_STATE, CHP), BF16),
            pltpu.VMEM((T * N_STATE, CHP), BF16),
            pltpu.VMEM((T, N_STATE, 128), F32),
            pltpu.VMEM((T, N_STATE, 128), F32),
        ],
        cost(25),
    )
    g_decay = jnp.sum(g_rate, axis=0) * decay_rate
    g_pre_f = g_step * jax.nn.sigmoid(pre)
    g_dt_bias = jnp.sum(g_pre_f, axis=0)
    g_pre = g_pre_f.astype(BF16)
    dt_term = dot(g_pre, dt_low_t, 0, 1, BF16)
    g_xproj_t = jnp.concatenate([dot(w_dt, g_pre, 0, 1), g_b, g_c]).astype(BF16)
    g_xproj_t = total_x(g_xproj_t).astype(BF16)
    xproj_term = dot(act, g_xproj_t, 0, 1, BF16)
    g_act = g_act + dot(g_xproj_t, w_xproj, 0, 1)
    (g_conv_sum,) = conv_pullback(g_act)
    g_conv_bias = jnp.sum(g_conv_sum, axis=0)
    g_conv_3 = g_conv_sum.reshape(NX, T, CHP)
    g_taps = [jnp.sum(g_conv_3 * padded[:, j : j + T], axis=(0, 1)) for j in range(CONV)]
    g_padded = jnp.zeros((NX, T + CONV - 1, CHP), F32)
    for j in range(CONV):
        g_padded = g_padded + jnp.pad(taps[j] * g_conv_3, ((0, 0), (j, CONV - 1 - j), (0, 0)))
    back = shift_ctx(g_padded[:, : CONV - 1].reshape(NX * (CONV - 1), CHP).astype(BF16), -1)
    back = back.astype(F32).reshape(NX, CONV - 1, CHP)
    g_conv_in = g_padded[:, CONV - 1 :] + jnp.pad(back, ((0, 0), (T - (CONV - 1), 0), (0, 0)))
    g_in_proj = jnp.concatenate(
        [g_conv_in.reshape(NX * T, CHP).astype(BF16), g_gate_z.astype(BF16)], axis=1
    )
    small_term = pad_to(jnp.concatenate([xproj_term[:CH], dt_term[:CH]], axis=1), CH, XD)
    small_term = jnp.pad(small_term.reshape(NC, CSUB, XD), ((0, 0), (0, ROWS_P - CSUB), (0, 0)))
    in_term = jnp.concatenate(
        [dot(normed_all, g_in_proj, 0, 0, BF16), small_term.reshape(DP, XD)], axis=1
    )
    in_sum = rows_sum_by_rings(in_term, index, False).astype(BF16)
    g_normed_terms = dot(g_in_proj, w_in, 1, 1, BF16)
    g_normed = scatter_x([g_normed_terms[k * T : (k + 1) * T] for k in range(NX)]) + g_normed_attn
    g_norm1, g_norm_gain = norm1_pullback(narrow(g_normed))
    tokens_grad = g_residual + g_norm1

    def all_columns(total, width):
        pieces = in_order(gather_x(total), x)
        halves = []
        for first_column in range(0, total.shape[1], total.shape[1] // 2):
            halves += [p[:ROWS, first_column : first_column + width] for p in pieces]
        return jnp.concatenate(halves, axis=1).astype(F32)

    def sequences_sum(total, width):
        a, b, c, d = gather_x(total)
        return (a.astype(F32) + b.astype(F32) + c.astype(F32) + d.astype(F32))[:ROWS, :width]

    def all_rows(total):
        turned = lax.ppermute(total, ("seq", "ctx"), TURN_BACK)
        a = lax.ppermute(turned, "seq", RIGHT)
        b = lax.ppermute(turned, "seq", LEFT)
        c = lax.ppermute(turned, "seq", [(i, (i + 2) % NX) for i in range(NX)])
        return jnp.concatenate(in_order([turned, b, c, a], x)).astype(F32)

    small_rows = all_rows(in_sum[:CSUB, 2 * CHP :])
    g_xproj_w = small_rows[:, : DT_RANK + 2 * N_STATE]
    g_dt_w = small_rows[:, DT_RANK + 2 * N_STATE : 2 * DT_RANK + 2 * N_STATE]

    gains = jnp.stack([g_norm_gain, g_attn_gain, g_mamba_gain, g_ffn_gain])
    gains = jnp.pad(gains, ((0, 0), (0, 2 * CHP - D))).reshape(8, CHP)
    table = jnp.concatenate(
        [
            jnp.stack(g_taps),
            g_conv_bias[None],
            g_dt_bias[None],
            g_skip[None],
            g_decay,
            jnp.zeros((1, CHP), F32),
            gains,
        ]
    )
    own = jnp.sum(lax.all_to_all(table, "ctx", 0, 0, tiled=True), axis=0, keepdims=True)
    a = lax.ppermute(own, "seq", RIGHT)
    b = lax.ppermute(own, "seq", LEFT)
    c = lax.ppermute(own, "seq", [(i, (i + 2) % NX) for i in range(NX)])
    whole = own + a + b + c
    shared = index >= 24
    four = jnp.concatenate([jnp.where(shared, whole, p) for p in in_order([own, b, c, a], x)])
    spread_rows = jnp.broadcast_to(four[None], (NC, NX, CHP))
    every = lax.all_to_all(spread_rows, "ctx", 0, 0, tiled=True)
    by_rows = every[:24, :, :CH].reshape(24, DI)
    gains = every[24:, 0].reshape(4, 2 * CHP)[:, :D]

    return (
        output,
        tokens_grad,
        gains[0],
        sequences_sum(qkv_sum.astype(BF16), QKV),
        sequences_sum(branch_sum[:ROWS_P, :AO_P], D),
        all_columns(in_sum[:, : 2 * CHP], CH),
        by_rows[:4],
        by_rows[4],
        g_xproj_w,
        g_dt_w,
        by_rows[5],
        by_rows[7:23].T,
        by_rows[6],
        all_rows(branch_sum[:CSUB, AO_P : AO_P + D]),
        gains[1],
        gains[2],
        gains[3],
        all_columns(ffn_sum[:ROWS_P, : 2 * FFP], FFX),
        all_rows(ffn_sum[:FSUB, 2 * FFP : 2 * FFP + D]),
    )


def solution(mesh):
    whole = P()
    ctx = P("ctx", None)
    both = P(("seq", "ctx"), None)
    return jax.shard_map(
        body,
        mesh=mesh,
        in_specs=(
            both, whole, ctx, ctx, ctx, whole, whole, ctx, ctx, whole, whole, whole,
            ctx, whole, whole, whole, ctx, ctx, both,
        ),
        out_specs=(
            both, both, whole, ctx, ctx, ctx, whole, whole, ctx, ctx, whole, whole,
            whole, ctx, whole, whole, whole, ctx, ctx,
        ),
        check_vma=False,
    )
```

time: 2910 us -> 933 us (0.32)
  blocking collectives: 832 us -> 0 us
  other arithmetic: 688 us -> 95.3 us
  local copies, waits for them, and re-layouts: 433 us -> 126 us
  waiting for transfers between devices: 466 us -> 196 us
  Pallas kernels: 0 us -> 130 us
  matrix products: 229 us -> 142 us
    unnamed x3 -> x0, blocking collectives: 762 us -> none
    dynamic_update_slice x256 -> x0, other arithmetic: 482 us -> none  [body(): lax.scan(forward_step, jnp.zeros((DI, N_STATE), jnp.float32), (decay_step...]
    psum x3 -> x0, waiting for transfers between devices: 331 us -> none  [the longest x2 285 us: body(): lax.psum((grad_norm_gain, grad_conv_w, grad_conv_bias, grad_dt_bias, grad...]
    unnamed x297 -> x245, local copies, waits for them, and re-layouts: 338 us -> 26 us
    ppermute x26 -> x114, waiting for transfers between devices: 9.33 us -> 179 us  [the longest x4 26.4 us: ring_sum(): b = lax.ppermute(to_left, 'ctx', minus)]
    unnamed x32 -> x0, starting transfers between devices: 131 us -> none
    pallas_call x0 -> x8, Pallas kernels: none -> 130 us  [the longest x4 68.8 us: seq_call(): pl.pallas_call(kernel, grid=(NX,), in_specs=[spec(a.shape, kind) for a, k...]
    ppermute x26 -> x114, starting transfers between devices: 67.1 us -> 192 us  [the longest x10 27 us: shift_ctx(): lax.ppermute(v, 'ctx', [(i, i + by) for i in range(NC) if 0 <= i + by < NC])]
  transfers between devices with their start and end apart: 70 -> 121, of which waited for: 14 -> 51; matrix products, arithmetic and copies ran while one was open for 67% -> 34% of each run, Pallas kernels for 0% -> 14%
where the time goes in v1:
time: 933 us; the launch traced here: 919 us
  starting transfers between devices  212 us (23%)
  waiting for transfers between devices  196 us (21%)
  matrix products  142 us (15%)
  Pallas kernels  130 us (14%)
  local copies, waits for them, and re-layouts  126 us (14%)
  other arithmetic  95.3 us (10%)
  between operations  17.6 us (2%)
    dot_general x26, matrix products, dot(): lax.dot_general(a, b, (((ca,), (cb,)), ((), ())), preferred_element_type=...  142 us
    pallas_call x4, Pallas kernels, seq_call(): pl.pallas_call(kernel, grid=(NX,), in_specs=[spec(a.shape, kind) for a, k...  68.8 us
    pallas_call x2, Pallas kernels, head_call(): pl.pallas_call(kernel, grid=(KV_HEADS,), in_specs=[pl.BlockSpec(memory_sp...  35.4 us
    ppermute x10, starting transfers between devices, shift_ctx(): lax.ppermute(v, 'ctx', [(i, i + by) for i in range(NC) if 0 <= i + by < NC])  27 us
    ppermute x4, waiting for transfers between devices, ring_sum(): b = lax.ppermute(to_left, 'ctx', minus)  26.4 us
    unnamed x245, local copies, waits for them, and re-layouts  26 us
    pallas_call x2, Pallas kernels, products(): pl.pallas_call(functools.partial(products_kernel, len(pairs)), grid=(rows...  25.5 us
    ppermute x14, starting transfers between devices, send(): lax.ppermute(v.reshape(NX * (N_STATE + 1), CHP).astype(BF16), 'ctx', pairs)  23.7 us
  transfers between devices with their start and end apart: 121, of which 51 were waited for; matrix products, arithmetic and copies ran while one was open for 34% of the time, Pallas kernels for 14%

profile of v1, /device:TPU:14, one launch (start us, length us, event | category | flops | bytes accessed | tf_op | source)
XLA Modules:
  0.0 919.1 jit_solution(16911628031623338308)
XLA Ops:
  16.1 11.5 %collective-permute-done = bf16[80,1600]{1,0:T(8,128)(2,1)S(1)} collective-permute-done((bf16[80,1600]{1,0:T(8,128)(2,1)S(1)}, bf16[80,1600]{1,0:T(8,128)(2,1)S(1)}, u32[]{:S(2)}, u32[]{:S(2)}) %collective-permute-start) | collective-permute-done | bytes 256032 | tf_op jit(solution)/shard_map/ppermute | solution.py:611
  76.1 6.9 fusion.24
  109.3 9.7 %shard_map.331 = f32[4,17,896]{2,1,0:T(8,128)} custom-call(f32[512,896]{1,0:T(8,128)} %get-tuple-element.328.step, bf16[512,896]{1,0:T(8,128)(2,1)} %copy-done.13, f32[16,512]{1,0:T(8,128)} %get-tuple-element.277.b_t, f32[16,896]{1,0:T(8,128)} %fusion.203.rate2), custom_call_target="tpu_custom_call" | custom-call | flops 8000000000 | bytes 8000000 | tf_op jit(solution)/shard_map/pallas_call | solution.py:392
  132.1 7.5 collective-permute-done.16
  159.1 15.6 %shard_map.332 = (bf16[4,2048,896]{2,1,0:T(8,128)(2,1)}, f32[512,896]{1,0:T(8,128)}, bf16[512,896]{1,0:T(8,128)(2,1)}) custom-call(f32[512,896]{1,0:T(8,128)} %get-tuple-element.328.step, bf16[512,896]{1,0:T(8,128)(2,1)} %copy-done.13, f32[512,896]{1,0:T(8,128)} %get-tuple-element.164.gate_z, f32[16,512]{1,0:T(8,128)} %get-tuple-element.277.b_t, ...), custom_call_target="tpu_custom_call" | custom-call | flops 14000000000 | bytes 14000000 | tf_op jit(solution)/shard_map/pallas_call | solution.py:392
  183.6 6.8 fusion.42
  241.6 15.2 %shard_map.330 = (bf16[5,640,64]{2,1,0:T(8,128)(2,1)}, f32[5,640,1]{2,1,0:T(8,128)}) custom-call(s32[1]{0:T(128)} %bitcast.lowest, bf16[5,640,64]{2,1,0:T(8,128)(2,1)} %bitcast.289, bf16[5,1152,64]{2,1,0:T(8,128)(2,1)} %bitcast.282, bf16[5,1152,64]{2,1,0:T(8,128)(2,1)} %bitcast.284), custom_call_target="tpu_custom_call" | custom-call | flops 12000000000 | bytes 12000000 | tf_op jit(solution)/shard_map/pallas_call | solution.py:453
  277.6 12.6 %fusion.108 = f32[512,1408]{1,0:T(8,128)} fusion(bf16[1408,1792]{1,0:T(8,128)(2,1)} %fusion.7, bf16[512,1664]{1,0:T(8,128)(2,1)} %constant_dynamic-update-slice_fusion.20.refs_3_, bf16[1792,4480]{1,0:T(8,128)(2,1)} %all-gather.8.cloned.1.call-done), kind=kOutput, calls=%fused_computation.206 | convolution fusion | flops 5638062080 | bytes 15597568 | tf_op jit(solution)/shard_map/dot_general | solution.py:51
  306.9 9.1 fusion.10
  319.5 6.9 fusion.54
  343.1 9.3 %fusion.60 = bf16[512,1792]{1,0:T(8,128)(2,1)S(1)} fusion(bf16[1792,4480]{1,0:T(8,128)(2,1)} %all-gather.8.cloned.1.call-done, bf16[512,1408]{1,0:T(8,128)(2,1)S(1)} %get-tuple-element.156, bf16[512,1408]{1,0:T(8,128)(2,1)S(1)} %get-tuple-element.155), kind=kOutput, calls=%fused_computation.81 | convolution fusion | flops 5174067200 | bytes 14811136 | tf_op jit(solution)/shard_map/dot_general | solution.py:51
  363.4 15.3 %shard_map.333 = bf16[2048,4480]{1,0:T(8,128)(2,1)} custom-call(bf16[2048,512]{1,0:T(8,128)(2,1)} %bitcast.272, bf16[512,2816]{1,0:T(8,128)(2,1)} %pad_maximum_fusion.1.refs_1_, bf16[2048,512]{1,0:T(8,128)(2,1)} %bitcast.273, bf16[512,1664]{1,0:T(8,128)(2,1)} %constant_dynamic-update-slice_fusion.20.refs_3_), custom_call_target="tpu_custom_call" | custom-call | flops 12000000000 | bytes 12000000 | tf_op jit(solution)/shard_map/pallas_call | solution.py:506
  408.5 9.1 convolution_convert_fusion.4
  418.8 20.2 %shard_map.335 = (bf16[5,640,64]{2,1,0:T(8,128)(2,1)}, f32[5,1152,64]{2,1,0:T(8,128)}, f32[5,1152,64]{2,1,0:T(8,128)}) custom-call(s32[1]{0:T(128)} %bitcast.lowest, bf16[5,640,64]{2,1,0:T(8,128)(2,1)} %bitcast.290, bf16[5,1152,64]{2,1,0:T(8,128)(2,1)} %bitcast.283, bf16[5,1152,64]{2,1,0:T(8,128)(2,1)} %bitcast.285, bf16[5,640,64]{2,1,0:T(8,128)(2,1)} %bitcast.292, ...), custom_call_target="tpu_custom_call" | custom-call | flops 24999999488 | bytes 25000000 | tf_op jit(solution)/shard_map/pallas_call | solution.py:453
  462.4 11.2 %fusion.111 = f32[512,896]{1,0:T(8,128)} fusion(bf16[896,1792]{1,0:T(8,128)(2,1)} %fusion.21, bf16[512,1664]{1,0:T(8,128)(2,1)} %constant_dynamic-update-slice_fusion.25.refs_3_, bf16[1792,5632]{1,0:T(8,128)(2,1)} %all-gather.4.cloned.1.call-done), kind=kOutput, calls=%fused_computation.207 | convolution fusion | flops 4698537984 | bytes 12713984 | tf_op jit(solution)/shard_map/dot_general | solution.py:51
  479.3 9.5 %shard_map.334 = f32[4,17,896]{2,1,0:T(8,128)} custom-call(f32[512,896]{1,0:T(8,128)} %get-tuple-element.328.step, f32[512,896]{1,0:T(8,128)} %get-tuple-element.138.g_scan, f32[16,512]{1,0:T(8,128)} %get-tuple-element.276.c_t, f32[16,896]{1,0:T(8,128)} %fusion.203.rate2), custom_call_target="tpu_custom_call" | custom-call | flops 8000000000 | bytes 8000000 | tf_op jit(solution)/shard_map/pallas_call | solution.py:392
  490.0 10.2 %shard_map.337 = bf16[2048,3328]{1,0:T(8,128)(2,1)} custom-call(bf16[2048,128]{1,0:T(8,128)(2,1)} %bitcast.296, bf16[128,1664]{1,0:T(8,128)(2,1)} %pad.168.refs_1_, bf16[2048,512]{1,0:T(8,128)(2,1)} %bitcast.271, bf16[512,1664]{1,0:T(8,128)(2,1)} %constant_dynamic-update-slice_fusion.25.refs_3_), custom_call_target="tpu_custom_call" | custom-call | flops 8000000000 | bytes 8000000 | tf_op jit(solution)/shard_map/pallas_call | solution.py:506
  561.6 33.9 %shard_map.336 = (f32[512,896]{1,0:T(8,128)}, f32[512,896]{1,0:T(8,128)}, f32[4,16,896]{2,1,0:T(8,128)}, f32[16,512]{1,0:T(8,128)}, f32[16,512]{1,0:T(8,128)}) custom-call(f32[512,896]{1,0:T(8,128)} %get-tuple-element.328.step, bf16[512,896]{1,0:T(8,128)(2,1)} %copy-done.13, f32[512,896]{1,0:T(8,128)} %get-tuple-element.138.g_scan, ...), custom_call_target="tpu_custom_call" | custom-call | flops 24999999488 | bytes 25000000 | tf_op jit(solution)/shard_map/pallas_call | solution.py:392
  648.6 6.7 collective-permute-done.59
  655.6 11.0 %fusion.100 = (f32[1600]{0:T(1024)S(1)}, f32[128]{0:T(128)S(1)}, f32[128,1600]{1,0:T(8,128)}) fusion(bf16[128,1600]{1,0:T(8,128)(2,1)S(1)} %copy-done.12, f32[128]{0:T(128)S(1)} %copy-done.90, f32[1600]{0:T(1024)S(1)} %copy-done.85, bf16[1600,1792]{1,0:T(8,128)(2,1)} %copy-done.2, bf16[128,1792]{1,0:T(8,128)(2,1)} %collective-permute-done.59, ...), kind=kOutput, calls=%fused_computation.187 | convolution fusion | flops 1765792128 | bytes 17184256 | tf_op jit(solution)/shard_map/dot_general | solution.py:51
  667.6 14.1 %all-to-all-start = ((f32[32,1,896]{2,1,0:T(1,128)}), f32[32,1,896]{2,1,0:T(1,128)S(1)}, u32[]{:S(2)}, u32[]{:S(2)}) async-start(f32[32,1,896]{2,1,0:T(1,128)} %copy.116), calls=%async_computation | async-start | bytes 229376 | tf_op jit(solution)/shard_map/all_to_all | solution.py:906
  706.3 11.6 %all-to-all-done.1 = f32[32,4,896]{2,1,0:T(4,128)} async-done(((f32[32,4,896]{2,1,0:T(4,128)}), f32[32,4,896]{2,1,0:T(4,128)}, u32[]{:S(2)}, u32[]{:S(2)}) %all-to-all-start.1) | async-done | bytes 458784 | tf_op jit(solution)/shard_map/all_to_all | solution.py:914
  739.6 8.6 collective-permute-done.88
  754.4 23.6 %collective-permute-done.89 = bf16[4,56,2048]{2,1,0:T(8,128)(2,1)S(1)} collective-permute-done((bf16[4,56,2048]{2,1,0:T(8,128)(2,1)S(1)}, bf16[4,56,2048]{2,1,0:T(8,128)(2,1)S(1)}, u32[]{:S(2)}, u32[]{:S(2)}) %collective-permute-start.89) | collective-permute-done | bytes 917536 | tf_op jit(solution)/shard_map/ppermute | solution.py:533
  (831 shorter events, 605.4 us)
Async XLA Ops:
  7.2 68.9 %all-gather.6.cloned.1.call-start = ((), (), s32[]{:S(2)}) async-start(), calls=%async_computation.5 | async-start | bytes 8515584 | tf_op jit(solution)/shard_map/all_gather | solution.py:608
  11.8 171.8 %all-gather.4.cloned.1.call-start = ((), (), s32[]{:S(2)}) async-start(), calls=%async_computation.4 | async-start | bytes 20815872 | tf_op jit(solution)/shard_map/all_gather | solution.py:622
  28.5 249.1 %all-gather.8.cloned.1.call-start = ((), (), s32[]{:S(2)}) async-start(), calls=%async_computation.6 | async-start | bytes 16558080 | tf_op jit(solution)/shard_map/all_gather | solution.py:631
  30.6 614.8 %reduce-scatter.3.cloned.1.call-start = ((), (), s32[]{:S(2)}) async-start(), calls=%async_computation.7 | async-start | bytes 18923520 | tf_op jit(solution)/shard_map/reduce_scatter | solution.py:518
  31.9 26.0 %collective-permute-start.30 = (bf16[128,1664]{1,0:T(8,128)(2,1)S(1)}, bf16[128,1664]{1,0:T(8,128)(2,1)S(1)}, u32[]{:S(2)}, u32[]{:S(2)}) collective-permute-start(bf16[128,1664]{1,0:T(8,128)(2,1)S(1)} %get-tuple-element.248), channel_id=1, source_target_pairs={{0,32},{32,64},{64,96},{96,0},{1,33},{33,65},{65,97},{97,1},{2,34}... | collective-permute-start | bytes 1277960 | tf_op jit(solution)/shard_map/ppermute | solution.py:64
  31.9 28.0 %collective-permute-start.29 = (bf16[128,1664]{1,0:T(8,128)(2,1)S(1)}, bf16[128,1664]{1,0:T(8,128)(2,1)S(1)}, u32[]{:S(2)}, u32[]{:S(2)}) collective-permute-start(bf16[128,1664]{1,0:T(8,128)(2,1)S(1)} %get-tuple-element.248), channel_id=1, source_target_pairs={{0,96},{32,0},{64,32},{96,64},{1,97},{33,1},{65,33},{97,65},{2,98}... | collective-permute-start | bytes 1277960 | tf_op jit(solution)/shard_map/ppermute | solution.py:65
  58.6 40.0 %collective-permute-start.31 = (bf16[64,1664]{1,0:T(8,128)(2,1)}, bf16[64,1664]{1,0:T(8,128)(2,1)}, u32[]{:S(2)}, u32[]{:S(2)}) collective-permute-start(bf16[64,1664]{1,0:T(8,128)(2,1)} %slice.1092), channel_id=1, source_target_pairs={{0,32},{32,64},{64,96},{96,0},{1,33},{33,65},{65,97},{97,1},{2,34}... | collective-permute-start | bytes 638984 | tf_op jit(solution)/shard_map/ppermute | solution.py:66
  60.6 59.7 %collective-permute-start.32 = (bf16[64,1664]{1,0:T(8,128)(2,1)}, bf16[64,1664]{1,0:T(8,128)(2,1)S(1)}, u32[]{:S(2)}, u32[]{:S(2)}) collective-permute-start(bf16[64,1664]{1,0:T(8,128)(2,1)} %slice.1093), channel_id=1, source_target_pairs={{0,96},{32,0},{64,32},{96,64},{1,97},{33,1},{65,33},{97,65},{2,98}... | collective-permute-start | bytes 638984 | tf_op jit(solution)/shard_map/ppermute | solution.py:67
  190.5 27.5 %collective-permute-start.4 = (bf16[128,640]{0,1:T(8,128)(2,1)S(1)}, bf16[128,640]{0,1:T(8,128)(2,1)S(1)}, u32[]{:S(2)}, u32[]{:S(2)}) collective-permute-start(bf16[128,640]{0,1:T(8,128)(2,1)S(1)} %slice.1022), channel_id=1, source_target_pairs={{0,2},{1,3},{2,4},{3,5},{4,6},{5,7},{6,8},{7,9},{8,10},{9,11},{10,... | collective-permute-start | bytes 491528 | tf_op jit(solution)/shard_map/ppermute | solution.py:123
  192.4 24.9 %collective-permute-start.3 = (bf16[128,640]{0,1:T(8,128)(2,1)S(1)}, bf16[128,640]{0,1:T(8,128)(2,1)S(1)}, u32[]{:S(2)}, u32[]{:S(2)}) collective-permute-start(bf16[128,640]{0,1:T(8,128)(2,1)S(1)} %slice.1022), channel_id=1, source_target_pairs={{0,4},{1,5},{2,6},{3,7},{4,8},{5,9},{6,10},{7,11},{8,12},{9,13},{1... | collective-permute-start | bytes 491528 | tf_op jit(solution)/shard_map/ppermute | solution.py:123
  338.9 39.9 %collective-permute-start.33 = (bf16[64,1664]{1,0:T(8,128)(2,1)}, bf16[64,1664]{1,0:T(8,128)(2,1)}, u32[]{:S(2)}, u32[]{:S(2)}) collective-permute-start(bf16[64,1664]{1,0:T(8,128)(2,1)} %get-tuple-element.186), channel_id=1, source_target_pairs={{0,32},{32,64},{64,96},{96,0},{1,33},{33,65},{65,97},{97,1},{2,34}... | collective-permute-start | bytes 638984 | tf_op jit(solution)/shard_map/ppermute | solution.py:73
  339.0 39.8 %collective-permute-start.35 = (bf16[64,1664]{1,0:T(8,128)(2,1)}, bf16[64,1664]{1,0:T(8,128)(2,1)}, u32[]{:S(2)}, u32[]{:S(2)}) collective-permute-start(bf16[64,1664]{1,0:T(8,128)(2,1)} %get-tuple-element.187), channel_id=1, source_target_pairs={{0,96},{32,0},{64,32},{96,64},{1,97},{33,1},{65,33},{97,65},{2,98}... | collective-permute-start | bytes 638984 | tf_op jit(solution)/shard_map/ppermute | solution.py:74
  354.5 25.7 %collective-permute-start.37 = (bf16[64,1792]{1,0:T(8,128)(2,1)}, bf16[64,1792]{1,0:T(8,128)(2,1)}, u32[]{:S(2)}, u32[]{:S(2)}) collective-permute-start(bf16[64,1792]{1,0:T(8,128)(2,1)} %get-tuple-element.178), channel_id=1, source_target_pairs={{0,32},{32,64},{64,96},{96,0},{1,33},{33,65},{65,97},{97,1},{2,34}... | collective-permute-start | bytes 688136 | tf_op jit(solution)/shard_map/ppermute | solution.py:73
  355.8 24.4 %collective-permute-start.39 = (bf16[64,1792]{1,0:T(8,128)(2,1)}, bf16[64,1792]{1,0:T(8,128)(2,1)}, u32[]{:S(2)}, u32[]{:S(2)}) collective-permute-start(bf16[64,1792]{1,0:T(8,128)(2,1)} %get-tuple-element.179), channel_id=1, source_target_pairs={{0,96},{32,0},{64,32},{96,64},{1,97},{33,1},{65,33},{97,65},{2,98}... | collective-permute-start | bytes 688136 | tf_op jit(solution)/shard_map/ppermute | solution.py:74
  378.7 498.1 %reduce-scatter.5.cloned.1.call-start = ((), (), s32[]{:S(2)}) async-start(), calls=%async_computation.8 | async-start | bytes 14057472 | tf_op jit(solution)/shard_map/reduce_scatter | solution.py:518
  403.6 44.1 %collective-permute-start.42 = (bf16[128,1664]{1,0:T(8,128)(2,1)}, bf16[128,1664]{1,0:T(8,128)(2,1)S(1)}, u32[]{:S(2)}, u32[]{:S(2)}) collective-permute-start(bf16[128,1664]{1,0:T(8,128)(2,1)} %get-tuple-element.246), channel_id=1, source_target_pairs={{0,32},{32,64},{64,96},{96,0},{1,33},{33,65},{65,97},{97,1},{2,34}... | collective-permute-start | bytes 1277960 | tf_op jit(solution)/shard_map/ppermute | solution.py:64
  407.0 44.1 %collective-permute-start.41 = (bf16[128,1664]{1,0:T(8,128)(2,1)}, bf16[128,1664]{1,0:T(8,128)(2,1)}, u32[]{:S(2)}, u32[]{:S(2)}) collective-permute-start(bf16[128,1664]{1,0:T(8,128)(2,1)} %get-tuple-element.246), channel_id=1, source_target_pairs={{0,96},{32,0},{64,32},{96,64},{1,97},{33,1},{65,33},{97,65},{2,98}... | collective-permute-start | bytes 1277960 | tf_op jit(solution)/shard_map/ppermute | solution.py:65
  447.6 52.6 %collective-permute-start.60 = (bf16[512,640]{0,1:T(8,128)(2,1)}, bf16[512,640]{0,1:T(8,128)(2,1)}, u32[]{:S(2)}, u32[]{:S(2)}) collective-permute-start(bf16[512,640]{0,1:T(8,128)(2,1)} %pad_maximum_fusion.10), channel_id=1, source_target_pairs={{0,1},{1,0},{2,3},{3,2},{4,5},{5,4},{6,7},{7,6},{8,9},{9,8},{10,11... | collective-permute-start | bytes 1966088 | tf_op jit(solution)/shard_map/ppermute | solution.py:181
  549.2 183.3 %collective-permute-start.68 = (bf16[16,56,2304]{2,1,0:T(8,128)(2,1)}, bf16[16,56,2304]{2,1,0:T(8,128)(2,1)}, u32[]{:S(2)}, u32[]{:S(2)}) collective-permute-start(bf16[16,56,2304]{2,1,0:T(8,128)(2,1)} %dynamic-slice_bitcast_fusion), channel_id=1, source_target_pairs={{0,1},{1,0},{2,3},{3,2},{4,5},{5,4},{6,7},{7,6},{8,9},{9,8},{10,11... | collective-permute-start | bytes 12386312 | tf_op jit(solution)/shard_map/ppermute | solution.py:545
  639.9 85.1 %collective-permute-start.85 = (bf16[16,56,2048]{2,1,0:T(8,128)(2,1)}, bf16[16,56,2048]{2,1,0:T(8,128)(2,1)}, u32[]{:S(2)}, u32[]{:S(2)}) collective-permute-start(bf16[16,56,2048]{2,1,0:T(8,128)(2,1)} %fusion.39), channel_id=1, source_target_pairs={{0,1},{1,0},{2,3},{3,2},{4,5},{5,4},{6,7},{7,6},{8,9},{9,8},{10,11... | collective-permute-start | bytes 11010056 | tf_op jit(solution)/shard_map/ppermute | solution.py:545
  748.5 29.5 %collective-permute-start.89 = (bf16[4,56,2048]{2,1,0:T(8,128)(2,1)S(1)}, bf16[4,56,2048]{2,1,0:T(8,128)(2,1)S(1)}, u32[]{:S(2)}, u32[]{:S(2)}) collective-permute-start(bf16[4,56,2048]{2,1,0:T(8,128)(2,1)S(1)} %pad_maximum_fusion.9), channel_id=1, source_target_pairs={{0,24},{1,25},{2,26},{3,27},{4,28},{5,29},{6,30},{7,31},{8,0},{9,1... | collective-permute-start | bytes 2752520 | tf_op jit(solution)/shard_map/ppermute | solution.py:533
  750.7 30.1 %collective-permute-start.87 = (bf16[4,56,2048]{2,1,0:T(8,128)(2,1)S(1)}, bf16[4,56,2048]{2,1,0:T(8,128)(2,1)S(1)}, u32[]{:S(2)}, u32[]{:S(2)}) collective-permute-start(bf16[4,56,2048]{2,1,0:T(8,128)(2,1)S(1)} %pad_maximum_fusion.8), channel_id=1, source_target_pairs={{0,8},{1,9},{2,10},{3,11},{4,12},{5,13},{6,14},{7,15},{8,16},{9,17... | collective-permute-start | bytes 2752520 | tf_op jit(solution)/shard_map/ppermute | solution.py:532
  752.0 37.2 %collective-permute-start.72 = (bf16[4,56,2304]{2,1,0:T(8,128)(2,1)S(1)}, bf16[4,56,2304]{2,1,0:T(8,128)(2,1)S(1)}, u32[]{:S(2)}, u32[]{:S(2)}) collective-permute-start(bf16[4,56,2304]{2,1,0:T(8,128)(2,1)S(1)} %pad_maximum_fusion.7), channel_id=1, source_target_pairs={{0,6},{1,7},{2,0},{3,1},{4,2},{5,3},{6,4},{7,5},{8,14},{9,15},{10,... | collective-permute-start | bytes 3096584 | tf_op jit(solution)/shard_map/ppermute | solution.py:533
  753.6 35.5 %collective-permute-start.70 = (bf16[4,56,2304]{2,1,0:T(8,128)(2,1)S(1)}, bf16[4,56,2304]{2,1,0:T(8,128)(2,1)S(1)}, u32[]{:S(2)}, u32[]{:S(2)}) collective-permute-start(bf16[4,56,2304]{2,1,0:T(8,128)(2,1)S(1)} %pad_maximum_fusion.6), channel_id=1, source_target_pairs={{0,2},{1,3},{2,4},{3,5},{4,6},{5,7},{6,0},{7,1},{8,10},{9,11},{10,... | collective-permute-start | bytes 3096584 | tf_op jit(solution)/shard_map/ppermute | solution.py:532
  (194 other events, 2318.2 us)
Sparse Core Ops, SparseCore 0:
  11.9 60.5 all-gather.5
  75.3 83.5 all-gather.3
  161.8 77.1 all-gather.7
  378.9 121.2 reduce-scatter.2
  645.6 129.1 reduce-scatter.4

commit v2 on v1

--- a/solution.py
+++ b/solution.py
@@ -59,16 +59,27 @@
 LEFT = [(i, (i - 1) % NX) for i in range(NX)]
 
 
-def gather_x(v):
+def gather_x_near(v):
+    return v, lax.ppermute(v, "seq", LEFT), lax.ppermute(v, "seq", RIGHT)
+
+
+def gather_x_far(v, after, before):
     half = v.shape[0] // 2
-    before = lax.ppermute(v, "seq", RIGHT)
-    after = lax.ppermute(v, "seq", LEFT)
     far_a = lax.ppermute(before[:half], "seq", RIGHT)
     far_b = lax.ppermute(after[half:], "seq", LEFT)
     return [v, after, jnp.concatenate([far_a, far_b]), before]
 
 
-def scatter_x(parts):
+def gather_x(v):
+    return gather_x_far(*gather_x_near(v))
+
+
+def spread_x(v):
+    far = lax.ppermute(v, "seq", [(i, (i + 2) % NX) for i in range(NX)])
+    return [v, lax.ppermute(v, "seq", LEFT), far, lax.ppermute(v, "seq", RIGHT)]
+
+
+def scatter_x_far(parts):
     half = parts[0].shape[0] // 2
     from_left = lax.ppermute(parts[2][:half], "seq", RIGHT)
     from_right = lax.ppermute(parts[2][half:], "seq", LEFT)
@@ -78,9 +89,17 @@
     to_left = jnp.concatenate(
         [parts[3][:half], (parts[3][half:].astype(F32) + from_right.astype(F32)).astype(BF16)]
     )
+    return parts[0], to_right, to_left
+
+
+def scatter_x_near(own, to_right, to_left):
     a = lax.ppermute(to_right, "seq", RIGHT)
     b = lax.ppermute(to_left, "seq", LEFT)
-    return parts[0].astype(F32) + a.astype(F32) + b.astype(F32)
+    return own.astype(F32) + a.astype(F32) + b.astype(F32)
+
+
+def scatter_x(parts):
+    return scatter_x_near(*scatter_x_far(parts))
 
 
 def total_x(v):
@@ -130,27 +149,29 @@
 SWAP = [(i, i ^ 1) for i in range(NC)]
 
 
-def carried(part, rate2, index, reverse):
+def carried(state, steps, rate2, index, reverse, beside):
     sign = -1 if reverse else 1
 
     def after(first, then):
-        state = then[:, :N_STATE] + jnp.exp2(rate2[None] * then[:, N_STATE:]) * first[:, :N_STATE]
-        return jnp.concatenate([state, first[:, N_STATE:] + then[:, N_STATE:]], axis=1)
-
-    def keep(flag, v):
-        return jnp.where(flag, v, 0.0)
-
-    def send(v, pairs):
-        flat = lax.ppermute(v.reshape(NX * (N_STATE + 1), CHP).astype(BF16), "ctx", pairs)
-        return flat.astype(F32).reshape(NX, N_STATE + 1, CHP)
-
+        return (then[0] + jnp.exp2(rate2[None] * then[1]) * first[0], first[1] + then[1])
+
+    def keep(flag, part):
+        return tuple(jnp.where(flag, v, 0.0) for v in part)
+
+    def send(part, pairs):
+        flat = jnp.concatenate([part[0].reshape(NX * N_STATE, CHP), part[1].reshape(NX, CHP)])
+        flat = lax.ppermute(flat.astype(BF16), "ctx", pairs).astype(F32)
+        return (flat[: NX * N_STATE].reshape(NX, N_STATE, CHP), flat[NX * N_STATE :].reshape(NX, 1, CHP))
+
+    part = (state, steps)
     core = index % 2
     y = (index // 2) % 4
     if reverse:
         core, y = 1 - core, 3 - y
     other = send(part, SWAP)
     inside = keep(core == 1, other)
-    chip = jnp.where(core == 1, after(other, part), after(part, other))
+    chip = tuple(jnp.where(core == 1, a, b) for a, b in zip(after(other, part), after(part, other)))
+    *chip, beside = tie(*chip, beside)
     rows = []
     for k in range(1, 4):
         rows.append(send(chip, [(i, i // 8 * 8 + (i + sign * 2 * k) % 8) for i in range(NC)]))
@@ -163,26 +184,15 @@
         by = sign * 8 * k
         planes.append(send(row, [(i, i + by) for i in range(NC) if 0 <= i + by < NC]))
     plane_pre = after(after(planes[2], planes[1]), planes[0])
-    return after(after(plane_pre, row_pre), inside)[:, :N_STATE]
-
-
-def key_window(own, core):
-    mine = jnp.concatenate([shift_ctx(own, 2 * k) for k in (4, 3, 2, 1)] + [own])
-    other = lax.ppermute(mine, "ctx", SWAP)
-    odd = jnp.where(core == 0, other[: 4 * T], other[T:])
-    blocks = []
-    for k in range(4):
-        blocks += [mine[k * T : (k + 1) * T], odd[k * T : (k + 1) * T]]
-    return jnp.concatenate(blocks + [mine[4 * T :]])
-
-
-def key_window_back(grad, core):
-    blocks = [grad[k * T : (k + 1) * T] for k in range(9)]
-    other = lax.ppermute(jnp.concatenate(blocks[1::2]).astype(BF16), "ctx", SWAP).astype(F32)
-    none = jnp.zeros_like(blocks[0])
-    mine = jnp.concatenate(blocks[::2]) + jnp.where(
+    return after(after(plane_pre, row_pre), inside)[0], beside
+
+
+def key_window_back(even, odd, core):
+    other = lax.ppermute(odd, "ctx", SWAP)
+    none = jnp.zeros((T, odd.shape[1]), BF16)
+    mine = even.astype(F32) + jnp.where(
         core == 0, jnp.concatenate([none, other]), jnp.concatenate([other, none])
-    )
+    ).astype(F32)
     total = mine[4 * T :]
     for k in range(1, 5):
         term = mine[(4 - k) * T : (5 - k) * T].astype(BF16)
@@ -259,15 +269,15 @@
     return [(slice(c * CHUNK, (c + 1) * CHUNK), slice(c * WIDE, (c + 1) * WIDE)) for c in range(T // CHUNK)]
 
 
-def scan_end_kernel(step, act, b_t, rate2, out, spread_b, drive):
+def scan_end_kernel(step, act, b_t, rate2, out, total, spread_b, drive):
     spread(b_t, spread_b)
     drive[...] = step[...] * act[...].astype(F32)
     for group in SCAN_GROUPS:
         zero = [jnp.zeros((N_STATE, 128), F32) for _ in group]
         states = forward_scan(step, drive, spread_b, rate2, group, zero, lambda t, j, h: None)
         for k, j in enumerate(group):
-            out[0, :N_STATE, lanes(j)] = states[k]
-    out[0, N_STATE:, :] = jnp.sum(step[...], axis=0, keepdims=True)
+            out[0, :, lanes(j)] = states[k]
+    total[0] = jnp.sum(step[...], axis=0, keepdims=True)
 
 
 def scan_kernel(
@@ -310,8 +320,7 @@
         zero = tuple(jnp.zeros((N_STATE, 128), F32) for _ in group)
         adjoints = lax.fori_loop(0, T // CHUNK, one, zero)
         for k, j in enumerate(group):
-            out[0, :N_STATE, lanes(j)] = adjoints[k]
-    out[0, N_STATE:, :] = jnp.sum(step[...], axis=0, keepdims=True)
+            out[0, :, lanes(j)] = adjoints[k]
 
 
 def adjoint_kernel(
@@ -411,116 +420,176 @@
     return (s > t) & (s <= t + WINDOW) & (s >= lowest)
 
 
-def attend_kernel(lowest, q, k, v, out, lse):
-    seen = visible_keys(lowest[0])
-    for g in range(GROUP):
-        rows = slice(g * T, (g + 1) * T)
-        scores = jnp.where(seen, dot(q[0, rows, :], k[0], 1, 1), NEG_BIG)
-        peak = jnp.max(scores, axis=-1, keepdims=True)
-        raised = jnp.exp(scores - peak)
-        mass = jnp.sum(raised, axis=-1, keepdims=True)
-        probs = (raised / mass).astype(BF16)
-        out[0, rows, :] = dot(probs, v[0], 1, 0, BF16)
-        lse[0, rows, :] = peak + jnp.log(mass)
-
-
-def attend_back_kernel(lowest, q, k, v, g_out, lse, g_q, g_k, g_v):
-    seen = visible_keys(lowest[0])
-    for g in range(GROUP):
-        rows = slice(g * T, (g + 1) * T)
-        q_here = q[0, rows, :]
-        g_here = g_out[0, rows, :]
-        scores = jnp.where(seen, dot(q_here, k[0], 1, 1), NEG_BIG)
-        probs = jnp.exp(scores - lse[0, rows, :])
-        g_probs = dot(g_here, v[0], 1, 1)
-        inner = jnp.sum(probs * g_probs, axis=-1, keepdims=True)
-        g_scores = (probs * (g_probs - inner)).astype(BF16)
-        g_q[0, rows, :] = (dot(g_scores, k[0], 1, 0) * HEAD_DIM ** (-0.5)).astype(BF16)
-        k_term = dot(g_scores, q_here, 0, 0)
-        v_term = dot(probs.astype(BF16), g_here, 0, 0)
-        if g == 0:
-            g_k[0] = k_term
-            g_v[0] = v_term
-        else:
-            g_k[0] += k_term
-            g_v[0] += v_term
-
-
-def head_call(kernel, lowest, ins, outs, us):
+def head_lanes(h, base=0):
+    return slice(base + h * HEAD_DIM, base + (h + 1) * HEAD_DIM)
+
+
+def stage(core, projected, mine, other, q_s, k_s, v_s):
+    for block in range(9):
+        rows = slice(block * T, (block + 1) * T)
+        half = block // 2
+        source = mine if block % 2 == 0 else other
+        start = half * T if block % 2 == 0 else pl.multiple_of((half + core) * T, T)
+        for n in range(KV_HEADS):
+            k_s[n, rows, :] = source[pl.ds(start, T), head_lanes(n)]
+            v_s[n, rows, :] = source[pl.ds(start, T), head_lanes(n, KV_HEADS * HEAD_DIM)]
+    for n in range(KV_HEADS):
+        for g in range(GROUP):
+            q = projected[:, head_lanes(n * GROUP + g)].astype(F32) * HEAD_DIM ** (-0.5)
+            q_s[n, g * T : (g + 1) * T, :] = q.astype(BF16)
+
+
+def attend_kernel(place, projected, mine, other, out, lse, q_s, k_s, v_s, o_s):
+    seen = visible_keys(place[0])
+    stage(place[1], projected, mine, other, q_s, k_s, v_s)
+
+    @pl.loop(0, KV_HEADS)
+    def _(n):
+        for g in range(GROUP):
+            rows = slice(g * T, (g + 1) * T)
+            scores = jnp.where(seen, dot(q_s[n, rows, :], k_s[n], 1, 1), NEG_BIG)
+            peak = jnp.max(scores, axis=-1, keepdims=True)
+            raised = jnp.exp(scores - peak)
+            mass = jnp.sum(raised, axis=-1, keepdims=True)
+            probs = (raised / mass).astype(BF16)
+            o_s[n, rows, :] = dot(probs, v_s[n], 1, 0, BF16)
+            lse[n, rows, :] = peak + jnp.log(mass)
+
+    for n in range(KV_HEADS):
+        for g in range(GROUP):
+            out[:, head_lanes(n * GROUP + g)] = o_s[n, g * T : (g + 1) * T, :]
+
+
+def attend_back_kernel(place, projected, mine, other, g_out, lse, g_q, g_even, g_odd, q_s, k_s, v_s, g_s, gq_s, gk_s, gv_s):
+    seen = visible_keys(place[0])
+    stage(place[1], projected, mine, other, q_s, k_s, v_s)
+    for n in range(KV_HEADS):
+        for g in range(GROUP):
+            g_s[n, g * T : (g + 1) * T, :] = g_out[:, head_lanes(n * GROUP + g)]
+
+    @pl.loop(0, KV_HEADS)
+    def _(n):
+        for g in range(GROUP):
+            rows = slice(g * T, (g + 1) * T)
+            q_here = q_s[n, rows, :]
+            g_here = g_s[n, rows, :]
+            scores = jnp.where(seen, dot(q_here, k_s[n], 1, 1), NEG_BIG)
+            probs = jnp.exp(scores - lse[n, rows, :])
+            g_probs = dot(g_here, v_s[n], 1, 1)
+            inner = jnp.sum(probs * g_probs, axis=-1, keepdims=True)
+            g_scores = (probs * (g_probs - inner)).astype(BF16)
+            gq_s[n, rows, :] = (dot(g_scores, k_s[n], 1, 0) * HEAD_DIM ** (-0.5)).astype(BF16)
+            k_term = dot(g_scores, q_here, 0, 0)
+            v_term = dot(probs.astype(BF16), g_here, 0, 0)
+            if g == 0:
+                gk_s[n] = k_term
+                gv_s[n] = v_term
+            else:
+                gk_s[n] += k_term
+                gv_s[n] += v_term
+
+    for n in range(KV_HEADS):
+        for block in range(9):
+            rows = slice(block * T, (block + 1) * T)
+            out = g_even if block % 2 == 0 else g_odd
+            into = slice(block // 2 * T, (block // 2 + 1) * T)
+            out[into, head_lanes(n)] = gk_s[n, rows, :].astype(BF16)
+            out[into, head_lanes(n, KV_HEADS * HEAD_DIM)] = gv_s[n, rows, :].astype(BF16)
+        for g in range(GROUP):
+            g_q[:, head_lanes(n * GROUP + g)] = gq_s[n, g * T : (g + 1) * T, :]
+
+
+def head_call(kernel, lowest, ins, outs, scratch, us):
     def spec(shape):
-        return pl.BlockSpec((1,) + tuple(shape[1:]), lambda h: (h, 0, 0))
+        return pl.BlockSpec(tuple(shape), lambda: (0,) * len(shape))
 
     return pl.pallas_call(
         kernel,
-        grid=(KV_HEADS,),
         in_specs=[pl.BlockSpec(memory_space=pltpu.SMEM)] + [spec(a.shape) for a in ins],
         out_specs=[spec(shape) for shape, _ in outs],
         out_shape=[jax.ShapeDtypeStruct(shape, dtype) for shape, dtype in outs],
+        scratch_shapes=[pltpu.VMEM(shape, dtype) for shape, dtype in scratch],
         compiler_params=pltpu.CompilerParams(vmem_limit_bytes=VMEM_LIMIT),
         cost_estimate=cost(us),
     )(lowest, *ins)
 
 
-def split_queries(v):
-    return v.reshape(T, KV_HEADS, GROUP, HEAD_DIM).transpose(1, 2, 0, 3).reshape(KV_HEADS, GROUP * T, HEAD_DIM)
-
-
-def join_queries(v):
-    return v.reshape(KV_HEADS, GROUP, T, HEAD_DIM).transpose(2, 0, 1, 3).reshape(T, HEADS * HEAD_DIM)
-
-
-def split_keys(v):
-    return v.reshape(v.shape[0], KV_HEADS, HEAD_DIM).transpose(1, 0, 2)
-
-
-def join_keys(v):
-    return v.transpose(1, 0, 2).reshape(v.shape[1], KV_HEADS * HEAD_DIM)
+Q_SHAPE = (KV_HEADS, GROUP * T, HEAD_DIM)
+K_SHAPE = (KV_HEADS, KEYS, HEAD_DIM)
 
 
 def pad_to(v, rows, columns):
     return jnp.pad(v, ((0, rows - v.shape[0]), (0, columns - v.shape[1])))
 
 
-def rows_64(v):
-    turned = v.T.reshape(NC, ROWS_P, v.shape[0])
-    return jnp.pad(turned, ((0, 0), (0, ROWS_64 - ROWS_P), (0, 0))).reshape(NC * ROWS_64, v.shape[0])
-
-
-def products_kernel(count, *refs):
-    out = refs[-1]
+def products_kernel(count, rows_out, *refs):
+    out = refs[2 * count]
     at = 0
     for k in range(count):
-        width = refs[2 * k + 1].shape[1]
-        out[:, at : at + width] = dot(refs[2 * k][...], refs[2 * k + 1][...], 1, 0, BF16)
+        turned = refs[2 * k][...].T
+        other = refs[2 * k + 1]
+        width = other.shape[1]
+        for first in range(0, width, 512):
+            size = min(512, width - first)
+            product = dot(turned, other[:, first : first + size], 1, 0)
+            if rows_out == ROWS_P:
+                out[:, at + first : at + first + size] = product.astype(BF16)
+                continue
+            for d in range(NC // 2):
+                rows = product[d * ROWS_P : (d + 1) * ROWS_P]
+                rows = jnp.concatenate([rows, jnp.zeros((rows_out - ROWS_P, size), F32)])
+                out[d * rows_out : (d + 1) * rows_out, at + first : at + first + size] = rows.astype(BF16)
         at += width
 
 
-def products(pairs, us):
-    block = 512
-    rows = NC * ROWS_64
+def products(pairs, us, rows_out=ROWS_64, spare=0):
     width = sum(b.shape[1] for _, b in pairs)
     specs = []
     for a, b in pairs:
-        specs.append(pl.BlockSpec((block, a.shape[1]), lambda i: (i, 0)))
+        specs.append(pl.BlockSpec((a.shape[0], DP // 2), lambda i: (0, i)))
         specs.append(pl.BlockSpec(b.shape, lambda i: (0, 0)))
     return pl.pallas_call(
-        functools.partial(products_kernel, len(pairs)),
-        grid=(rows // block,),
+        functools.partial(products_kernel, len(pairs), rows_out),
+        grid=(2,),
         in_specs=specs,
-        out_specs=pl.BlockSpec((block, width), lambda i: (i, 0)),
-        out_shape=jax.ShapeDtypeStruct((rows, width), BF16),
+        out_specs=pl.BlockSpec((NC // 2 * rows_out, width), lambda i: (i, 0)),
+        out_shape=jax.ShapeDtypeStruct((NC * rows_out, width + spare), BF16),
         compiler_params=pltpu.CompilerParams(vmem_limit_bytes=VMEM_LIMIT),
         cost_estimate=cost(us),
     )(*[v for pair in pairs for v in pair])
 
 
+def product_into(held, a, b, us):
+    width = b.shape[1]
+    block = 384
+    skip = (held.shape[1] - width) // block
+
+    def kernel(a_ref, b_ref, _, out):
+        products_kernel(1, ROWS_64, a_ref, b_ref, out)
+
+    return pl.pallas_call(
+        kernel,
+        grid=(2, width // block),
+        in_specs=[
+            pl.BlockSpec((a.shape[0], DP // 2), lambda i, j: (0, i)),
+            pl.BlockSpec((b.shape[0], block), lambda i, j: (0, j)),
+            pl.BlockSpec(memory_space=pl.ANY),
+        ],
+        out_specs=pl.BlockSpec((NC // 2 * ROWS_64, block), lambda i, j: (i, j + skip)),
+        out_shape=jax.ShapeDtypeStruct(held.shape, BF16),
+        input_output_aliases={2: 0},
+        compiler_params=pltpu.CompilerParams(vmem_limit_bytes=VMEM_LIMIT),
+        cost_estimate=cost(us),
+    )(a, b, held)
+
+
 def rows_sum(v):
     return lax.psum_scatter(v, "ctx", scatter_dimension=0, tiled=True)
 
 
-def ring_sum(v, dim, place, plus, minus):
+def ring_far(v, dim, place, plus, minus):
     parts = [lax.dynamic_index_in_dim(v, (place + k) % 4, dim, False) for k in range(4)]
-    half = v.shape[-1] // 2
+    half = -(-v.shape[-1] // 256) * 128
     from_left = lax.ppermute(parts[2][..., :half], "ctx", plus)
     from_right = lax.ppermute(parts[2][..., half:], "ctx", minus)
     to_right = jnp.concatenate(
@@ -529,27 +598,36 @@
     to_left = jnp.concatenate(
         [parts[3][..., :half], (parts[3][..., half:].astype(F32) + from_right.astype(F32)).astype(BF16)], axis=-1
     )
+    return parts[0], to_right, to_left
+
+
+def ring_near(own, to_right, to_left, plus, minus):
     a = lax.ppermute(to_right, "ctx", plus)
     b = lax.ppermute(to_left, "ctx", minus)
-    return parts[0].astype(F32) + a.astype(F32) + b.astype(F32)
+    return own.astype(F32) + a.astype(F32) + b.astype(F32)
 
 
 def ring_pairs(stride, by):
     return [(i, i + (((i // stride) % 4 + by) % 4 - (i // stride) % 4) * stride) for i in range(NC)]
 
 
-def rows_sum_by_rings(v, index, y_first):
-    core, y, z = index % 2, (index // 2) % 4, index // 8
-    width = v.shape[1]
-    v = v.reshape(NC // 2, 2, ROWS_P, width)
-    other = lax.ppermute(lax.dynamic_index_in_dim(v, 1 - core, 1, False), "ctx", SWAP)
-    v = lax.dynamic_index_in_dim(v, core, 1, False).astype(F32) + other.astype(F32)
-    v = v.astype(BF16).reshape(4, 4, ROWS_P, width)
-    along_y = (y, ring_pairs(2, 1), ring_pairs(2, -1))
-    along_z = (z, ring_pairs(8, 1), ring_pairs(8, -1))
-    if y_first:
-        return ring_sum(ring_sum(v, 1, *along_y).astype(BF16), 0, *along_z)
-    return ring_sum(ring_sum(v, 0, *along_z).astype(BF16), 0, *along_y)
+def core_halves(terms, core):
+    def half(which):
+        return jnp.concatenate(
+            [
+                lax.dynamic_index_in_dim(v.reshape(NC // 2, 2, ROWS_P, v.shape[1]), which, 1, False)
+                for v in terms
+            ],
+            axis=-1,
+        )
+
+    return half(1 - core), half(core)
+
+
+def core_sum(theirs, mine):
+    other = lax.ppermute(theirs, "ctx", SWAP)
+    v = mine.astype(F32) + other.astype(F32)
+    return v.reshape(4, 4, ROWS_P, v.shape[-1])
 
 
 def body(
@@ -589,10 +667,14 @@
     widen_channels = order(CH, CHP, CSUB)
     widen_hidden = order(FFX, FFP, FSUB)
 
-    def widen(v, matrix=widen_m):
-        return dot(v, matrix, 1, 0, BF16)
-
-    def narrow(v, matrix=widen_m):
+    def widen(v, matrix=None):
+        return dot(v, widen_m if matrix is None else matrix, 1, 0, BF16)
+
+    narrow_m = lax.optimization_barrier(widen_m.T)
+
+    def narrow(v, matrix=None):
+        if matrix is None:
+            return dot(v.astype(BF16), narrow_m, 1, 0)
         return dot(v.astype(BF16), matrix, 1, 1)
 
     by_channel = pad_to(jnp.concatenate([xproj_weight, dt_weight], axis=1), 2 * ROWS, XD)
@@ -602,6 +684,7 @@
             pad_to(columns(in_weight, DI + x * CH, CH), ROWS_P, CHP),
             pad_to(by_channel[:ROWS], ROWS_P, XD),
             pad_to(by_channel[ROWS:], ROWS_P, XD),
+            pad_to(qkv_weight, ROWS_P, QKV_P),
         ],
         axis=1,
     )
@@ -613,13 +696,11 @@
     )
     second = jnp.concatenate(
         [
-            pad_to(qkv_weight, ROWS_P, QKV_P),
             pad_to(attn_out_weight, ROWS_P, AO_P),
             pad_to(sub_wide[48 : 48 + CSUB], ROWS_P, AO_P),
         ],
         axis=1,
     )
-    second = lax.all_gather(second, "ctx", axis=0, tiled=True)
     third = jnp.concatenate(
         [
             pad_to(columns(gate_up_weight, x * FFX, FFX), ROWS_P, FFP),
@@ -628,17 +709,27 @@
         ],
         axis=1,
     )
+    inputs = tokens.astype(F32)
+    normed_f, norm1_pullback = jax.vjp(norm_scale, inputs, norm_gain)
+    normed = widen(normed_f.astype(BF16))
+    normed, second = tie(normed, second)
+    second = lax.all_gather(second, "ctx", axis=0, tiled=True)
+    normed_all = jnp.concatenate(gather_x(normed))
+    cot_all = jnp.concatenate(gather_x(pad_to(cotangent, T, AO_P)))
+    first, normed_all, cot_all, third, widen_m, narrow_m, widen_channels, widen_hidden = tie(
+        first, normed_all, cot_all, third, widen_m, narrow_m, widen_channels, widen_hidden
+    )
     third = lax.all_gather(third, "ctx", axis=0, tiled=True)
     w_in = first[:, : 2 * CHP]
-    small = first[:, 2 * CHP :].reshape(NC, ROWS_P, 2 * XD)
+    small = first[:, 2 * CHP : 2 * CHP + 2 * XD].reshape(NC, ROWS_P, 2 * XD)
     small = lax.dynamic_slice_in_dim(small, x * (NC // NX), NC // NX, 0)[:, :ROWS]
     small = jnp.stack([small[:, :, :XD], small[:, :, XD:]], axis=1).reshape(CH, XD)
     w_small = pad_to(small, CHP, XD)
     w_xproj = w_small[:, : DT_RANK + 2 * N_STATE]
     w_dt = w_small[:, DT_RANK + 2 * N_STATE : 2 * DT_RANK + 2 * N_STATE]
-    w_qkv = second[:, :QKV]
-    w_attn = second[:, QKV_P : QKV_P + D]
-    w_mamba = second[:, QKV_P + AO_P :]
+    w_qkv = first[:, 2 * CHP + 2 * XD :]
+    w_attn = second[:, :AO_P]
+    w_mamba = second[:, AO_P:]
     w_gate_up = third[:, : 2 * FFP]
     w_down = third[:, 2 * FFP :]
 
@@ -653,11 +744,6 @@
     decay_rate = -jnp.exp(channel(decay_log.T))
     rate2 = decay_rate * LOG2E
 
-    inputs = tokens.astype(F32)
-    normed_f, norm1_pullback = jax.vjp(norm_scale, inputs, norm_gain)
-    normed = widen(normed_f.astype(BF16))
-    normed_all = jnp.concatenate(gather_x(normed))
-    cot_all = jnp.concatenate(gather_x(pad_to(cotangent, T, AO_P)))
 
     in_proj = dot(normed_all, w_in, 1, 0)
     conv_in = in_proj[:, :CHP].reshape(NX, T, CHP)
@@ -670,38 +756,42 @@
     conv_sum = conv_sum.reshape(NX * T, CHP)
     act_f, conv_pullback = jax.vjp(jax.nn.silu, conv_sum)
     act = act_f.astype(BF16)
-    xproj_t = total_x(dot(w_xproj, act, 0, 1, BF16))
+    xproj_t = dot(w_xproj, act, 0, 1, BF16)
+    in_proj, normed_q = tie(in_proj, normed)
+    projected = dot(normed_q, w_qkv, 1, 0, BF16)
+    xproj_t, projected = tie(xproj_t, projected)
+    xproj_t = total_x(xproj_t)
+    kv_own = projected[:, D:QKV]
+    core = index % 2
+    kv_mine = jnp.concatenate([shift_ctx(kv_own, 2 * k) for k in (4, 3, 2, 1)] + [kv_own])
     dt_low_t = xproj_t[:DT_RANK].astype(BF16)
     b_t = xproj_t[DT_RANK : DT_RANK + N_STATE]
     c_t = xproj_t[DT_RANK + N_STATE :]
     pre = dot(dt_low_t, w_dt, 0, 1) + dt_b
     step = jax.nn.softplus(pre)
-    (scan_end,) = seq_call(
+    scan_end, steps = seq_call(
         scan_end_kernel,
         [(step, "rows"), (act, "rows"), (b_t, "lanes"), (rate2, "all")],
-        [((NX, N_STATE + 1, CHP), F32, "lead")],
+        [((NX, N_STATE, CHP), F32, "lead"), ((NX, 1, CHP), F32, "lead")],
         [pltpu.VMEM((T, N_STATE, 128), F32), pltpu.VMEM((T, CHP), F32)],
         cost(8),
     )
-    start = carried(scan_end, rate2, index, False)
-
-    projected = dot(normed, w_qkv, 1, 0, BF16)
-    kv_own = projected[:, D:]
-    core = index % 2
-    kv = key_window(kv_own, core)
-    queries = split_queries(projected[:, :D] * jnp.asarray(HEAD_DIM ** (-0.5), BF16))
-    keys = split_keys(kv[:, : KV_HEADS * HEAD_DIM])
-    values = split_keys(kv[:, KV_HEADS * HEAD_DIM :])
-    lowest = jnp.maximum(0, WINDOW - index * T).astype(jnp.int32).reshape(1)
-    attended_h, lse = head_call(
+
+    scan_end, kv_mine = tie(scan_end, kv_mine)
+    kv_other = lax.ppermute(kv_mine, "ctx", SWAP)
+    start, kv_other = carried(scan_end, steps, rate2, index, False, kv_other)
+    place_here = jnp.stack([jnp.maximum(0, WINDOW - index * T), core]).astype(jnp.int32)
+    attended, lse = head_call(
         attend_kernel,
-        lowest,
-        [queries, keys, values],
-        [((KV_HEADS, GROUP * T, HEAD_DIM), BF16), ((KV_HEADS, GROUP * T, 1), F32)],
-        12,
-    )
-    attended = widen(join_queries(attended_h))
-    attn_branch = dot(attended, w_attn, 1, 0)
+        place_here,
+        [projected, kv_mine, kv_other],
+        [((T, D), BF16), ((KV_HEADS, GROUP * T, 1), F32)],
+        [(Q_SHAPE, BF16), (K_SHAPE, BF16), (K_SHAPE, BF16), (Q_SHAPE, BF16)],
+        15,
+    )
+    start, attended, lse = tie(start, attended, lse)
+    attended = widen(attended)
+    attn_branch = dot(attended, w_attn, 1, 0)[:, :D]
 
     states, scan_out, gated = seq_call(
         scan_kernel,
@@ -729,42 +819,51 @@
     )
     gated = widen(gated, widen_channels)
     mamba_terms = dot(gated, w_mamba, 1, 0, BF16)
+
     mamba_branch = scatter_x([mamba_terms[k * T : (k + 1) * T] for k in range(NX)])[:, :D]
 
     def mixing(attn_part, mamba_part, gain_attn, gain_mamba):
         return 0.5 * (norm_scale(attn_part, gain_attn) + norm_scale(mamba_part, gain_mamba))
 
+    mamba_branch, cot_all = tie(mamba_branch, cot_all)
     mixed, mix_pullback = jax.vjp(mixing, attn_branch, mamba_branch, attn_gain, mamba_gain)
     residual = inputs + mixed
     ffn_f, norm2_pullback = jax.vjp(norm_scale, residual, ffn_gain)
-    ffn_all = jnp.concatenate(gather_x(widen(ffn_f.astype(BF16))))
-    g_hidden = narrow(dot(cot_all, w_down, 1, 1, BF16), widen_hidden)
-    ffn_all, g_hidden = tie(ffn_all, g_hidden)
+    ffn_near = gather_x_near(widen(ffn_f.astype(BF16)))
+    (g_hidden,) = tie(dot(cot_all, w_down, 1, 1, BF16))
+    g_hidden = narrow(g_hidden, widen_hidden)
+    g_hidden, *ffn_near = tie(g_hidden, *ffn_near)
+    ffn_all = jnp.concatenate(gather_x_far(*ffn_near))
     gate_up = dot(ffn_all, w_gate_up, 1, 0)
 
     def swiglu(gate, up):
         return jax.nn.silu(gate) * up
 
     hidden_f, swiglu_pullback = jax.vjp(swiglu, gate_up[:, :FFP], gate_up[:, FFP:])
-    hidden = widen(hidden_f.astype(BF16), widen_hidden)
+    hidden_f = hidden_f.astype(BF16)
     g_gate, g_up = swiglu_pullback(g_hidden)
     g_gate_up = jnp.concatenate([g_gate.astype(BF16), g_up.astype(BF16)], axis=1)
     g_ffn_terms = dot(g_gate_up, w_gate_up, 1, 1, BF16)
-    g_ffn_in = narrow(scatter_x([g_ffn_terms[k * T : (k + 1) * T] for k in range(NX)]))
-    down_terms = dot(hidden, w_down, 1, 0, BF16)
-    down_sum = scatter_x([down_terms[k * T : (k + 1) * T] for k in range(NX)])
-    output = (residual + down_sum[:, :D]).astype(BF16)
+    g_ffn_terms, hidden_f, g_gate_up, ffn_all = tie(g_ffn_terms, hidden_f, g_gate_up, ffn_all)
+    hidden = widen(hidden_f, widen_hidden)
+    ffn_term = products([(ffn_all, g_gate_up), (hidden, cot_all)], 14)
+    g_ffn_sum = scatter_x([g_ffn_terms[k * T : (k + 1) * T] for k in range(NX)])
+    g_ffn_sum, ffn_term, hidden = tie(g_ffn_sum, ffn_term, hidden)
+    ffn_sum = rows_sum(ffn_term)
+    (g_ffn_in,) = tie(narrow(g_ffn_sum))
     g_norm2, g_ffn_gain = norm2_pullback(g_ffn_in)
     g_residual = cotangent.astype(F32) + g_norm2
     g_attn_f, g_mamba_f, g_attn_gain, g_mamba_gain = mix_pullback(g_residual)
-    g_attn = g_attn_f.astype(BF16)
-    g_mamba_all = jnp.concatenate(gather_x(pad_to(g_mamba_f.astype(BF16), T, AO_P)))
-
-    ffn_term = products([(rows_64(ffn_all), g_gate_up), (rows_64(hidden), cot_all)], 12)
-    ffn_sum = rows_sum(ffn_term)
-    g_mamba_all, ffn_term = tie(g_mamba_all, ffn_term)
-
-    (g_gated,) = tie(narrow(dot(g_mamba_all, w_mamba, 1, 1, BF16), widen_channels))
+    g_attn = pad_to(g_attn_f.astype(BF16), T, AO_P)
+    g_mamba_near = gather_x_near(pad_to(g_mamba_f.astype(BF16), T, AO_P))
+
+    g_attended = narrow(dot(g_attn, w_attn, 1, 1, BF16)).astype(BF16)
+    down_terms = dot(hidden, w_down, 1, 0, BF16)
+    g_attended, *g_mamba_near = tie(g_attended, *g_mamba_near)
+    g_mamba_all = jnp.concatenate(gather_x_far(*g_mamba_near))
+    g_mamba_all, down_terms = tie(g_mamba_all, down_terms)
+    (g_gated,) = tie(dot(g_mamba_all, w_mamba, 1, 1, BF16))
+    (g_gated,) = tie(narrow(g_gated, widen_channels))
     silu_z, gate_pullback = jax.vjp(jax.nn.silu, gate_z)
     g_scan = g_gated * silu_z
     (g_gate_z,) = gate_pullback(g_gated * scan_out)
@@ -772,36 +871,44 @@
     (adjoint_end,) = seq_call(
         adjoint_end_kernel,
         [(step, "rows"), (g_scan, "rows"), (c_t, "lanes"), (rate2, "all")],
-        [((NX, N_STATE + 1, CHP), F32, "lead")],
+        [((NX, N_STATE, CHP), F32, "lead")],
         [pltpu.VMEM((T, N_STATE, 128), F32)],
         cost(8),
     )
-    later = carried(adjoint_end, rate2, index, True)
-
-    g_attended = narrow(dot(g_attn, w_attn, 1, 1, BF16)).astype(BF16)
-    g_queries, g_keys, g_values = head_call(
+    later, g_attended = carried(adjoint_end, steps, rate2, index, True, g_attended)
+
+    g_queries, g_even, g_odd = head_call(
         attend_back_kernel,
-        lowest,
-        [queries, keys, values, split_queries(g_attended), lse],
-        [
-            ((KV_HEADS, GROUP * T, HEAD_DIM), BF16),
-            ((KV_HEADS, KEYS, HEAD_DIM), F32),
-            ((KV_HEADS, KEYS, HEAD_DIM), F32),
-        ],
-        25,
-    )
-    g_kv = jnp.concatenate([join_keys(g_keys), join_keys(g_values)], axis=1)
-    g_kv = key_window_back(g_kv, core)
-    g_projected = jnp.concatenate([join_queries(g_queries), g_kv.astype(BF16)], axis=1)
+        place_here,
+        [projected, kv_mine, kv_other, g_attended, lse],
+        [
+            ((T, D), BF16),
+            ((5 * T, 2 * KV_HEADS * HEAD_DIM), BF16),
+            ((4 * T, 2 * KV_HEADS * HEAD_DIM), BF16),
+        ],
+        [
+            (Q_SHAPE, BF16),
+            (K_SHAPE, BF16),
+            (K_SHAPE, BF16),
+            (Q_SHAPE, BF16),
+            (Q_SHAPE, BF16),
+            (K_SHAPE, F32),
+            (K_SHAPE, F32),
+        ],
+        22,
+    )
+    g_projected = jnp.concatenate([g_queries, key_window_back(g_even, g_odd, core).astype(BF16)], axis=1)
+    g_projected = pad_to(g_projected, T, QKV_P)
     branch_term = products(
-        [(rows_64(attended), pad_to(g_attn, T, AO_P)), (rows_64(gated), g_mamba_all)], 8
-    )
-    branch_term, ffn_sum = tie(branch_term, ffn_sum)
+        [(attended, g_attn), (gated, g_mamba_all), (normed_all, g_gate_z.astype(BF16))],
+        12,
+        spare=QKV_P,
+    )
+    branch_term = product_into(branch_term, normed, g_projected, 4)
+    later, branch_term, ffn_sum = tie(later, branch_term, ffn_sum)
     branch_sum = rows_sum(branch_term)
-    qkv_term = dot(normed, pad_to(g_projected, T, QKV_P), 0, 0, BF16)
-    qkv_sum = rows_sum_by_rings(qkv_term, index, True)
-    g_normed_attn = dot(g_projected, w_qkv, 1, 1)
-    later, g_queries = tie(later, g_queries)
+
+    gate_up_near = gather_x_near(ffn_sum[:ROWS_P, : 2 * FFP])
 
     g_step, g_act, g_rate, g_b, g_c = seq_call(
         adjoint_kernel,
@@ -835,6 +942,7 @@
         ],
         cost(25),
     )
+    g_step, *gate_up_near = tie(g_step, *gate_up_near)
     g_decay = jnp.sum(g_rate, axis=0) * decay_rate
     g_pre_f = g_step * jax.nn.sigmoid(pre)
     g_dt_bias = jnp.sum(g_pre_f, axis=0)
@@ -842,6 +950,7 @@
     dt_term = dot(g_pre, dt_low_t, 0, 1, BF16)
     g_xproj_t = jnp.concatenate([dot(w_dt, g_pre, 0, 1), g_b, g_c]).astype(BF16)
     g_xproj_t = total_x(g_xproj_t).astype(BF16)
+    g_xproj_t, *gate_up = tie(g_xproj_t, *gather_x_far(*gate_up_near))
     xproj_term = dot(act, g_xproj_t, 0, 1, BF16)
     g_act = g_act + dot(g_xproj_t, w_xproj, 0, 1)
     (g_conv_sum,) = conv_pullback(g_act)
@@ -859,37 +968,15 @@
     )
     small_term = pad_to(jnp.concatenate([xproj_term[:CH], dt_term[:CH]], axis=1), CH, XD)
     small_term = jnp.pad(small_term.reshape(NC, CSUB, XD), ((0, 0), (0, ROWS_P - CSUB), (0, 0)))
-    in_term = jnp.concatenate(
-        [dot(normed_all, g_in_proj, 0, 0, BF16), small_term.reshape(DP, XD)], axis=1
-    )
-    in_sum = rows_sum_by_rings(in_term, index, False).astype(BF16)
+    in_c_term = products([(normed_all, g_in_proj[:, :CHP])], 4, ROWS_P)
+    theirs, mine = core_halves([in_c_term, small_term.reshape(DP, XD)], core)
+    theirs, mine, g_in_proj, g_projected = tie(theirs, mine, g_in_proj, g_projected)
+    in_half = core_sum(theirs, mine)
+    g_normed_attn = dot(g_projected, w_qkv, 1, 1)
     g_normed_terms = dot(g_in_proj, w_in, 1, 1, BF16)
-    g_normed = scatter_x([g_normed_terms[k * T : (k + 1) * T] for k in range(NX)]) + g_normed_attn
-    g_norm1, g_norm_gain = norm1_pullback(narrow(g_normed))
-    tokens_grad = g_residual + g_norm1
-
-    def all_columns(total, width):
-        pieces = in_order(gather_x(total), x)
-        halves = []
-        for first_column in range(0, total.shape[1], total.shape[1] // 2):
-            halves += [p[:ROWS, first_column : first_column + width] for p in pieces]
-        return jnp.concatenate(halves, axis=1).astype(F32)
-
-    def sequences_sum(total, width):
-        a, b, c, d = gather_x(total)
-        return (a.astype(F32) + b.astype(F32) + c.astype(F32) + d.astype(F32))[:ROWS, :width]
-
-    def all_rows(total):
-        turned = lax.ppermute(total, ("seq", "ctx"), TURN_BACK)
-        a = lax.ppermute(turned, "seq", RIGHT)
-        b = lax.ppermute(turned, "seq", LEFT)
-        c = lax.ppermute(turned, "seq", [(i, (i + 2) % NX) for i in range(NX)])
-        return jnp.concatenate(in_order([turned, b, c, a], x)).astype(F32)
-
-    small_rows = all_rows(in_sum[:CSUB, 2 * CHP :])
-    g_xproj_w = small_rows[:, : DT_RANK + 2 * N_STATE]
-    g_dt_w = small_rows[:, DT_RANK + 2 * N_STATE : 2 * DT_RANK + 2 * N_STATE]
-
+    g_norm_gain = jnp.sum(g_normed_terms.astype(F32) * normed_all.astype(F32), axis=0)
+    g_norm_gain = g_norm_gain + jnp.sum(g_normed_attn * normed.astype(F32), axis=0)
+    g_norm_gain = g_norm_gain.reshape(NC, ROWS_P)[:, :ROWS].reshape(D) / norm_gain
     gains = jnp.stack([g_norm_gain, g_attn_gain, g_mamba_gain, g_ffn_gain])
     gains = jnp.pad(gains, ((0, 0), (0, 2 * CHP - D))).reshape(8, CHP)
     table = jnp.concatenate(
@@ -903,25 +990,72 @@
             gains,
         ]
     )
-    own = jnp.sum(lax.all_to_all(table, "ctx", 0, 0, tiled=True), axis=0, keepdims=True)
-    a = lax.ppermute(own, "seq", RIGHT)
-    b = lax.ppermute(own, "seq", LEFT)
-    c = lax.ppermute(own, "seq", [(i, (i + 2) % NX) for i in range(NX)])
-    whole = own + a + b + c
-    shared = index >= 24
-    four = jnp.concatenate([jnp.where(shared, whole, p) for p in in_order([own, b, c, a], x)])
-    spread_rows = jnp.broadcast_to(four[None], (NC, NX, CHP))
-    every = lax.all_to_all(spread_rows, "ctx", 0, 0, tiled=True)
-    by_rows = every[:24, :, :CH].reshape(24, DI)
-    gains = every[24:, 0].reshape(4, 2 * CHP)[:, :D]
+    table = jnp.pad(table, ((0, 0), (0, 4 * XD - CHP))).reshape(NC // 2, 8, XD)
+    table = jnp.pad(table, ((0, 0), (32, ROWS_P - 40), (CHP, 0))).reshape(4, 4, ROWS_P, CHP + XD)
+    in_half = (in_half + table).astype(BF16)
+    both = jnp.concatenate([g_normed_terms, down_terms], axis=1)
+    in_half, both = tie(in_half, both)
+    both = scatter_x_far([both[k * T : (k + 1) * T] for k in range(NX)])
+    along_z = (ring_pairs(8, 1), ring_pairs(8, -1))
+    along_y = (ring_pairs(2, 1), ring_pairs(2, -1))
+    in_half = ring_far(in_half, 0, index // 8, *along_z)
+    in_half, both = tie(in_half, both)
+    in_half = ring_near(*in_half, *along_z).astype(BF16)
+    both = scatter_x_near(*both)
+    in_half, branch_sum = tie(in_half, branch_sum)
+    branch = jnp.concatenate([branch_sum[:ROWS_P, :AO_P], branch_sum[:ROWS_P, 2 * AO_P :]], axis=1)
+    branch = gather_x_near(branch)
+    in_sum = ring_near(*ring_far(in_half, 0, (index // 2) % 4, *along_y), *along_y)
+    table = jnp.broadcast_to(in_sum[None, 32:40, CHP:], (NC, 8, XD))
+    in_sum = in_sum.astype(BF16)
+    owned = jnp.concatenate(
+        [
+            ffn_sum[:48, 2 * FFP : 2 * FFP + AO_P],
+            branch_sum[:32, AO_P : 2 * AO_P],
+            pad_to(in_sum[:32, CHP:], 32, AO_P),
+        ]
+    )
+    owned = lax.ppermute(owned, ("seq", "ctx"), TURN_BACK)
+    in_parts = in_order(spread_x(in_sum[:, :CHP]), x)
+    table = lax.all_to_all(table, "ctx", 0, 0, tiled=True)
+    table = jnp.sum(table.reshape(NC // 2, 2, 2, 4 * XD), axis=1).reshape(NC, 4 * XD)
+    last = gather_x(jnp.concatenate([owned, pad_to(table.astype(BF16), NC, AO_P)]))
+    last = in_order(last, x)
+    by_rows = jnp.concatenate([v[112:136, :CH] for v in last], axis=1).astype(F32)
+    gains = sum(v[136:144, :CHP].astype(F32) for v in last).reshape(4, 2 * CHP)[:, :D]
+
+    (g_normed,) = tie(narrow(both[:, :DP] + g_normed_attn))
+    g_norm1, _ = norm1_pullback(g_normed)
+    tokens_grad = g_residual + g_norm1
+    output = (residual + both[:, DP : DP + D]).astype(BF16)
+
+    def side_by_side(parts, width):
+        halves = []
+        size = parts[0].shape[1] // 2
+        for first_column in range(0, 2 * size, size):
+            halves += [p[:ROWS, first_column : first_column + width] for p in parts]
+        return jnp.concatenate(halves, axis=1).astype(F32)
+
+    branch = gather_x_far(*branch)
+    attn_w = sum(v[:ROWS, :D].astype(F32) for v in branch)
+    qkv_w = sum(v[:ROWS, AO_P + CHP : AO_P + CHP + QKV].astype(F32) for v in branch)
+    down_w = jnp.concatenate([v[:FSUB, :D] for v in last]).astype(F32)
+    mamba_w = jnp.concatenate([v[48 : 48 + CSUB, :D] for v in last]).astype(F32)
+    small_rows = jnp.concatenate([v[80 : 80 + CSUB, :XD] for v in last]).astype(F32)
+    in_z = in_order([v[:, AO_P : AO_P + CHP] for v in branch], x)
+    in_w = jnp.concatenate(
+        [v[:ROWS, :CH] for v in in_parts + in_z], axis=1
+    ).astype(F32)
+    g_xproj_w = small_rows[:, : DT_RANK + 2 * N_STATE]
+    g_dt_w = small_rows[:, DT_RANK + 2 * N_STATE : 2 * DT_RANK + 2 * N_STATE]
 
     return (
         output,
         tokens_grad,
         gains[0],
-        sequences_sum(qkv_sum.astype(BF16), QKV),
-        sequences_sum(branch_sum[:ROWS_P, :AO_P], D),
-        all_columns(in_sum[:, : 2 * CHP], CH),
+        qkv_w,
+        attn_w,
+        in_w,
         by_rows[:4],
         by_rows[4],
         g_xproj_w,
@@ -929,12 +1063,12 @@
         by_rows[5],
         by_rows[7:23].T,
         by_rows[6],
-        all_rows(branch_sum[:CSUB, AO_P : AO_P + D]),
+        mamba_w,
         gains[1],
         gains[2],
         gains[3],
-        all_columns(ffn_sum[:ROWS_P, : 2 * FFP], FFX),
-        all_rows(ffn_sum[:FSUB, 2 * FFP : 2 * FFP + D]),
+        side_by_side(in_order(gate_up, x), FFX),
+        down_w,
     )
 
 

time: 933 us -> 752 us (0.81)
  waiting for transfers between devices: 196 us -> 127 us
  starting transfers between devices: 212 us -> 157 us
  local copies, waits for them, and re-layouts: 126 us -> 77.2 us
  Pallas kernels: 130 us -> 155 us
  matrix products: 142 us -> 122 us
  other arithmetic: 95.3 us -> 85.1 us
    ppermute x97 -> x69, waiting for transfers between devices: 150 us -> 91.5 us  [the longest x7 22.7 us: gather_x_far(): far_a = lax.ppermute(before[:half], 'seq', RIGHT)]
    ppermute x97 -> x69, starting transfers between devices: 154 us -> 114 us  [the longest x14 30.3 us: gather_x_near(): return (v, lax.ppermute(v, 'seq', LEFT), lax.ppermute(v, 'seq', RIGHT))]
    pallas_call x4 -> x6, Pallas kernels: 60.9 us -> 86.4 us  [the longest x2 41.8 us: head_call(): pl.pallas_call(kernel, in_specs=[pl.BlockSpec(memory_space=pltpu.SMEM)] +...]
    dot_general x26 -> x27, matrix products: 142 us -> 122 us  [dot(): lax.dot_general(a, b, (((ca,), (cb,)), ((), ())), preferred_element_type=...]
    all_to_all x2 -> x1, waiting for transfers between devices: 16.9 us -> 0.01 us  [body(): table = lax.all_to_all(table, 'ctx', 0, 0, tiled=True)]
    all_gather x1, waiting for transfers between devices: 0.01 us -> 15.5 us  [body(): first = lax.all_gather(first, 'ctx', axis=0, tiled=True)]
    reshape x14 -> x4, local copies, waits for them, and re-layouts: 15.4 us -> 0.32 us  [the longest x1 0.17 us: body(): table.reshape(NC // 2, 2, 2, 4 * XD)]
    all_to_all x2 -> x1, starting transfers between devices: 19.6 us -> 6.76 us  [body(): table = lax.all_to_all(table, 'ctx', 0, 0, tiled=True)]
  transfers between devices with their start and end apart: 121 -> 92, of which waited for: 51 -> 36; matrix products, arithmetic and copies ran while one was open for 34% -> 31% of each run, Pallas kernels for 14% -> 21%
where the time goes in v2:
time: 752 us; the launch traced here: 741 us
  starting transfers between devices  157 us (21%)
  Pallas kernels  155 us (21%)
  waiting for transfers between devices  127 us (17%)
  matrix products  122 us (16%)
  other arithmetic  85.1 us (11%)
  local copies, waits for them, and re-layouts  77.2 us (10%)
  between operations  17.5 us (2%)
    dot_general x27, matrix products, dot(): lax.dot_general(a, b, (((ca,), (cb,)), ((), ())), preferred_element_type=...  122 us
    pallas_call x4, Pallas kernels, seq_call(): pl.pallas_call(kernel, grid=(NX,), in_specs=[spec(a.shape, kind) for a, k...  69 us
    pallas_call x2, Pallas kernels, head_call(): pl.pallas_call(kernel, in_specs=[pl.BlockSpec(memory_space=pltpu.SMEM)] +...  41.8 us
    pallas_call x3, Pallas kernels, products(): pl.pallas_call(functools.partial(products_kernel, len(pairs), rows_out),...  33.9 us
    ppermute x14, starting transfers between devices, gather_x_near(): return (v, lax.ppermute(v, 'seq', LEFT), lax.ppermute(v, 'seq', RIGHT))  30.3 us
    unnamed x291, local copies, waits for them, and re-layouts  25.2 us
    ppermute x10, starting transfers between devices, shift_ctx(): lax.ppermute(v, 'ctx', [(i, i + by) for i in range(NC) if 0 <= i + by < NC])  23.6 us
    ppermute x7, waiting for transfers between devices, gather_x_far(): far_a = lax.ppermute(before[:half], 'seq', RIGHT)  22.7 us
  transfers between devices with their start and end apart: 92, of which 36 were waited for; matrix products, arithmetic and copies ran while one was open for 31% of the time, Pallas kernels for 21%

profile of v2, /device:TPU:14, one launch (start us, length us, event | category | flops | bytes accessed | tf_op | source)
XLA Modules:
  0.0 740.6 jit_solution(11688080939813255190)
XLA Ops:
  22.0 6.7 collective-permute-done
  30.8 6.8 collective-permute-start.5
  53.0 9.4 %collective-permute-done.7 = bf16[64,1664]{1,0:T(8,128)(2,1)S(1)} collective-permute-done((bf16[64,1664]{1,0:T(8,128)(2,1)S(1)}, bf16[64,1664]{1,0:T(8,128)(2,1)S(1)}, u32[]{:S(2)}, u32[]{:S(2)}) %collective-permute-start.7) | collective-permute-done | bytes 213024 | tf_op jit(solution)/shard_map/ppermute | solution.py:68
  77.1 15.5 %all-gather.4.cloned.1.call-done = bf16[1792,4608]{1,0:T(8,128)(2,1)} async-done(((bf16[56,4608]{1,0:T(8,128)(2,1)}), bf16[1792,4608]{1,0:T(8,128)(2,1)}) %all-gather.4.cloned.1.call-update) | async-done | bytes 16515088 | tf_op jit(solution)/shard_map/all_gather | solution.py:691
  97.4 6.9 fusion.26
  142.5 9.4 %shard_map.330 = (f32[4,16,896]{2,1,0:T(8,128)}, f32[4,1,896]{2,1,0:T(1,128)}) custom-call(f32[512,896]{1,0:T(8,128)} %get-tuple-element.417.step, bf16[512,896]{1,0:T(8,128)(2,1)} %copy-done.16, f32[16,512]{1,0:T(8,128)} %get-tuple-element.385.b_t, f32[16,896]{1,0:T(8,128)} %fusion.148.rate2), custom_call_target="tpu_custom_call" | custom-call | flops 8000000000 | bytes 8000000 | tf_op jit(solution)/shard_map/pallas_call | solution.py:401
  176.9 17.6 %shard_map.331 = (bf16[128,1600]{1,0:T(8,128)(2,1)}, f32[5,640,1]{2,1,0:T(8,128)}) custom-call(s32[2]{0:T(128)} %pad_add_fusion.1.place, bf16[128,2304]{1,0:T(8,128)(2,1)} %fusion.36.projected, bf16[640,640]{1,0:T(8,128)(2,1)} %copy-done.109, bf16[640,640]{1,0:T(8,128)(2,1)} %copy-done.116), custom_call_target="tpu_custom_call" | custom-call | flops 15000000512 | bytes 15000000 | tf_op jit(solution)/shard_map/pallas_call | solution.py:506
  195.7 15.6 %shard_map.332 = (bf16[4,2048,896]{2,1,0:T(8,128)(2,1)}, f32[512,896]{1,0:T(8,128)}, bf16[512,896]{1,0:T(8,128)(2,1)}) custom-call(f32[512,896]{1,0:T(8,128)} %get-tuple-element.417.step, bf16[512,896]{1,0:T(8,128)(2,1)} %copy-done.16, f32[512,896]{1,0:T(8,128)} %get-tuple-element.311.gate_z, f32[16,512]{1,0:T(8,128)} %get-tuple-element.385.b_t, ...), custom_call_target="tpu_custom_call" | custom-call | flops 14000000000 | bytes 14000000 | tf_op jit(solution)/shard_map/pallas_call | solution.py:401
  215.8 7.1 fusion.39
  270.7 9.1 %fusion.10 = f32[512,2816]{1,0:T(8,128)S(1)} fusion(bf16[512,1792]{1,0:T(8,128)(2,1)S(1)} %constant_dynamic-update-slice_fusion.17.refs_0_, bf16[1792,4480]{1,0:T(8,128)(2,1)} %all-gather.8.cloned.1.call-done), kind=kOutput, calls=%fused_computation.18 | convolution fusion | flops 5167382528 | bytes 17694720 | tf_op jit(solution)/shard_map/dot_general | solution.py:51
  284.3 9.8 %fusion.54 = bf16[512,1792]{1,0:T(8,128)(2,1)S(1)} fusion(bf16[1792,4480]{1,0:T(8,128)(2,1)} %all-gather.8.cloned.1.call-done, bf16[512,1408]{1,0:T(8,128)(2,1)S(1)} %get-tuple-element.308, bf16[512,1408]{1,0:T(8,128)(2,1)S(1)} %get-tuple-element.307), kind=kOutput, calls=%fused_computation.58 | convolution fusion | flops 5174067200 | bytes 14811136 | tf_op jit(solution)/shard_map/dot_general | solution.py:51
  307.9 15.5 %shard_map.333 = bf16[2048,4480]{1,0:T(8,128)(2,1)} custom-call(bf16[512,1792]{1,0:T(8,128)(2,1)} %copy-done.93, bf16[512,2816]{1,0:T(8,128)(2,1)} %pad_maximum_fusion.1.refs_1_, bf16[512,1792]{1,0:T(8,128)(2,1)} %convolution_convert_fusion.refs_2_, bf16[512,1664]{1,0:T(8,128)(2,1)} %constant_dynamic-update-slice_fusion.7.refs_3_), custom_call_target="tpu_custom_call" | custom-call | flops 14000000000 | bytes 14000000 | tf_op jit(solution)/shard_map/pallas_call | solution.py:551
  337.1 8.0 %fusion.48 = bf16[512,1664]{1,0:T(8,128)(2,1)} fusion(bf16[512,1792]{1,0:T(8,128)(2,1)S(1)} %copy-done.117, bf16[1792,4480]{1,0:T(8,128)(2,1)} %all-gather.8.cloned.1.call-done), kind=kOutput, calls=%fused_computation.54 | convolution fusion | flops 3054305280 | bytes 9502720 | tf_op jit(solution)/shard_map/dot_general | solution.py:51
  345.1 9.8 %convolution_convert_fusion.2.g_out = bf16[128,1600]{1,0:T(8,128)(2,1)} fusion(bf16[1792,1600]{0,1:T(8,128)(2,1)} %bitcast.184, bf16[1792,3328]{1,0:T(8,128)(2,1)} %all-gather.6.cloned.1.call-done, bf16[128,1600]{1,0:T(8,128)(2,1)S(1)} %get-tuple-element.361), kind=kOutput, calls=%fused_computation.72 | convolution fusion | flops 1497800704 | bytes 12517376 | tf_op jit(solution)/shard_map/dot_general | solution.py:51
  378.1 10.0 %shard_map.334 = f32[4,16,896]{2,1,0:T(8,128)} custom-call(f32[512,896]{1,0:T(8,128)} %get-tuple-element.417.step, f32[512,896]{1,0:T(8,128)} %get-tuple-element.290.g_scan, f32[16,512]{1,0:T(8,128)} %get-tuple-element.384.c_t, f32[16,896]{1,0:T(8,128)} %fusion.148.rate2), custom_call_target="tpu_custom_call" | custom-call | flops 8000000000 | bytes 8000000 | tf_op jit(solution)/shard_map/pallas_call | solution.py:401
  395.9 24.1 %shard_map.335 = (bf16[128,1600]{1,0:T(8,128)(2,1)}, bf16[640,640]{1,0:T(8,128)(2,1)}, bf16[512,640]{1,0:T(8,128)(2,1)}) custom-call(s32[2]{0:T(128)} %pad_add_fusion.1.place, bf16[128,2304]{1,0:T(8,128)(2,1)} %fusion.36.projected, bf16[640,640]{1,0:T(8,128)(2,1)} %copy-done.109, bf16[640,640]{1,0:T(8,128)(2,1)} %copy-done.116, ...), custom_call_target="tpu_custom_call" | custom-call | flops 22000001024 | bytes 22000000 | tf_op jit(solution)/shard_map/pallas_call | solution.py:506
  425.4 13.5 %shard_map.336._ = bf16[2048,6528]{1,0:T(8,128)(2,1)} custom-call(bf16[128,1792]{1,0:T(8,128)(2,1)} %copy-done.73, bf16[128,1664]{1,0:T(8,128)(2,1)} %pad.158.refs_1_, bf16[512,1792]{1,0:T(8,128)(2,1)} %convolution_convert_fusion.1.refs_2_, bf16[512,1664]{1,0:T(8,128)(2,1)} %copy-done.94, ...), custom_call_target="tpu_custom_call" | custom-call | flops 12000000000 | bytes 12000000 | tf_op jit(solution)/shard_map/pallas_call | solution.py:551
  460.5 10.7 %shard_map.337 = bf16[2048,6528]{1,0:T(8,128)(2,1)} custom-call(bf16[128,1792]{1,0:T(8,128)(2,1)} %copy-done.27, bf16[128,2304]{1,0:T(8,128)(2,1)} %fusion.98.b_ref, bf16[2048,6528]{1,0:T(8,128)(2,1)} %shard_map.336._), custom_call_target="tpu_custom_call", output_to_operand_aliasing={{}: (2, {})} | custom-call | flops 4000000000 | bytes 4000000 | tf_op jit(solution)/shard_map/pallas_call | solution.py:570
  474.7 33.9 %shard_map.338 = (f32[512,896]{1,0:T(8,128)}, f32[512,896]{1,0:T(8,128)}, f32[4,16,896]{2,1,0:T(8,128)}, f32[16,512]{1,0:T(8,128)}, f32[16,512]{1,0:T(8,128)}) custom-call(f32[512,896]{1,0:T(8,128)} %get-tuple-element.417.step, bf16[512,896]{1,0:T(8,128)(2,1)} %copy-done.16, f32[512,896]{1,0:T(8,128)} %get-tuple-element.290.g_scan, ...), custom_call_target="tpu_custom_call" | custom-call | flops 24999999488 | bytes 25000000 | tf_op jit(solution)/shard_map/pallas_call | solution.py:401
  562.8 7.6 %multiply_reduce_fusion.6 = (f32[1792]{0:T(1024)S(1)}, f32[128,1792]{1,0:T(8,128)}) fusion(bf16[128,1792]{1,0:T(8,128)(2,1)S(1)} %copy-done.28, bf16[128,2304]{1,0:T(8,128)(2,1)S(1)} %copy-done.38, bf16[1792,4608]{1,0:T(8,128)(2,1)} %all-gather.4.cloned.1.call-done), kind=kOutput, calls=%fused_computation.139 | convolution fusion | flops 1057650944 | bytes 10230784 | tf_op jit(solution)/shard_map/dot_general | solution.py:51
  570.3 8.0 %multiply_reduce_fusion = (f32[1792]{0:T(1024)S(1)}, bf16[512,1792]{1,0:T(8,128)(2,1)}) fusion(bf16[512,1792]{1,0:T(8,128)(2,1)} %constant_dynamic-update-slice_fusion.2.refs_4_.refs_0_, bf16[512,1792]{1,0:T(8,128)(2,1)S(1)} %pad_maximum_fusion.5, bf16[1792,4608]{1,0:T(8,128)(2,1)} %all-gather.4.cloned.1.call-done), kind=kOutput, calls=%fused_computation.48 | convolution fusion | flops 3292920064 | bytes 11934720 | tf_op jit(solution)/shard_map/dot_general | solution.py:51
  620.1 14.2 %collective-permute-done.68 = bf16[4,56,1152]{2,1,0:T(8,128)(2,1)} collective-permute-done((bf16[4,56,1152]{2,1,0:T(8,128)(2,1)}, bf16[4,56,1152]{2,1,0:T(8,128)(2,1)}, u32[]{:S(2)}, u32[]{:S(2)}) %collective-permute-start.68) | collective-permute-done | bytes 516128 | tf_op jit(solution)/shard_map/ppermute | solution.py:605
  668.5 6.8 all-to-all-start
  693.1 8.9 %collective-permute-start.77 = (bf16[144,1664]{1,0:T(8,128)(2,1)S(1)}, bf16[144,1664]{1,0:T(8,128)(2,1)S(1)}, u32[]{:S(2)}, u32[]{:S(2)}) collective-permute-start(bf16[144,1664]{1,0:T(8,128)(2,1)S(1)} %fusion.103), channel_id=1, source_target_pairs={{0,96},{32,0},{64,32},{96,64},{1,97},{33,1},{65,33},{97,65},{2,98}... | collective-permute-start | bytes 1437704 | tf_op jit(solution)/shard_map/ppermute | solution.py:63
  (805 shorter events, 437.9 us)
Async XLA Ops:
  7.2 85.4 %all-gather.4.cloned.1.call-start = ((), (), s32[]{:S(2)}) async-start(), calls=%async_computation.3 | async-start | bytes 17031168 | tf_op jit(solution)/shard_map/all_gather | solution.py:691
  12.9 202.9 %all-gather.6.cloned.1.call-start = ((), (), s32[]{:S(2)}) async-start(), calls=%async_computation.4 | async-start | bytes 12300288 | tf_op jit(solution)/shard_map/all_gather | solution.py:716
  29.5 218.3 %all-gather.8.cloned.1.call-start = ((), (), s32[]{:S(2)}) async-start(), calls=%async_computation.5 | async-start | bytes 16558080 | tf_op jit(solution)/shard_map/all_gather | solution.py:722
  92.6 378.6 %reduce-scatter.3.cloned.1.call-start = ((), (), s32[]{:S(2)}) async-start(), calls=%async_computation.6 | async-start | bytes 18923520 | tf_op jit(solution)/shard_map/reduce_scatter | solution.py:587
  125.5 26.6 %collective-permute-start.16 = (bf16[128,640]{1,0:T(8,128)(2,1)S(1)}, bf16[128,640]{1,0:T(8,128)(2,1)S(1)}, u32[]{:S(2)}, u32[]{:S(2)}) collective-permute-start(bf16[128,640]{1,0:T(8,128)(2,1)S(1)} %slice.681), channel_id=1, source_target_pairs={{0,2},{1,3},{2,4},{3,5},{4,6},{5,7},{6,8},{7,9},{8,10},{9,11},{10,... | collective-permute-start | bytes 491528 | tf_op jit(solution)/shard_map/ppermute | solution.py:142
  128.9 23.1 %collective-permute-start.15 = (bf16[128,640]{1,0:T(8,128)(2,1)S(1)}, bf16[128,640]{1,0:T(8,128)(2,1)S(1)}, u32[]{:S(2)}, u32[]{:S(2)}) collective-permute-start(bf16[128,640]{1,0:T(8,128)(2,1)S(1)} %slice.681), channel_id=1, source_target_pairs={{0,4},{1,5},{2,6},{3,7},{4,8},{5,9},{6,10},{7,11},{8,12},{9,13},{1... | collective-permute-start | bytes 491528 | tf_op jit(solution)/shard_map/ppermute | solution.py:142
  167.8 26.8 %collective-permute-start.24 = (bf16[68,896]{1,0:T(8,128)(2,1)S(1)}, bf16[68,896]{1,0:T(8,128)(2,1)S(1)}, u32[]{:S(2)}, u32[]{:S(2)}) collective-permute-start(bf16[68,896]{1,0:T(8,128)(2,1)S(1)} %pad_maximum_fusion.28), channel_id=1, source_target_pairs={{0,24},{1,25},{2,26},{3,27},{4,28},{5,29},{6,30},{7,31},{32,56},{3... | collective-permute-start | bytes 365576 | tf_op jit(solution)/shard_map/ppermute | solution.py:163
  172.9 21.7 %collective-permute-start.23 = (bf16[68,896]{1,0:T(8,128)(2,1)S(1)}, bf16[68,896]{1,0:T(8,128)(2,1)S(1)}, u32[]{:S(2)}, u32[]{:S(2)}) collective-permute-start(bf16[68,896]{1,0:T(8,128)(2,1)S(1)} %pad_maximum_fusion.28), channel_id=1, source_target_pairs={{0,16},{1,17},{2,18},{3,19},{4,20},{5,21},{6,22},{7,23},{8,24},{9,... | collective-permute-start | bytes 365576 | tf_op jit(solution)/shard_map/ppermute | solution.py:163
  324.6 320.6 %reduce-scatter.5.cloned.1.call-start = ((), (), s32[]{:S(2)}) async-start(), calls=%async_computation.7 | async-start | bytes 27574272 | tf_op jit(solution)/shard_map/reduce_scatter | solution.py:587
  390.9 29.3 %collective-permute-start.44 = (bf16[68,896]{1,0:T(8,128)(2,1)S(1)}, bf16[68,896]{1,0:T(8,128)(2,1)S(1)}, u32[]{:S(2)}, u32[]{:S(2)}) collective-permute-start(bf16[68,896]{1,0:T(8,128)(2,1)S(1)} %pad_maximum_fusion.29), channel_id=1, source_target_pairs={{0,2},{1,3},{2,4},{3,5},{4,6},{5,7},{6,0},{7,1},{8,10},{9,11},{10,... | collective-permute-start | bytes 365576 | tf_op jit(solution)/shard_map/ppermute | solution.py:163
  391.0 29.2 %collective-permute-start.43 = (bf16[68,896]{1,0:T(8,128)(2,1)S(1)}, bf16[68,896]{1,0:T(8,128)(2,1)S(1)}, u32[]{:S(2)}, u32[]{:S(2)}) collective-permute-start(bf16[68,896]{1,0:T(8,128)(2,1)S(1)} %pad_maximum_fusion.29), channel_id=1, source_target_pairs={{0,4},{1,5},{2,6},{3,7},{4,0},{5,1},{6,2},{7,3},{8,12},{9,13},{10,... | collective-permute-start | bytes 365576 | tf_op jit(solution)/shard_map/ppermute | solution.py:163
  393.7 26.6 %collective-permute-start.42 = (bf16[68,896]{1,0:T(8,128)(2,1)S(1)}, bf16[68,896]{1,0:T(8,128)(2,1)S(1)}, u32[]{:S(2)}, u32[]{:S(2)}) collective-permute-start(bf16[68,896]{1,0:T(8,128)(2,1)S(1)} %pad_maximum_fusion.29), channel_id=1, source_target_pairs={{0,6},{1,7},{2,0},{3,1},{4,2},{5,3},{6,4},{7,5},{8,14},{9,15},{10,... | collective-permute-start | bytes 365576 | tf_op jit(solution)/shard_map/ppermute | solution.py:163
  420.1 22.9 %collective-permute-start.48 = (bf16[512,640]{1,0:T(8,128)(2,1)}, bf16[512,640]{1,0:T(8,128)(2,1)}, u32[]{:S(2)}, u32[]{:S(2)}) collective-permute-start(bf16[512,640]{1,0:T(8,128)(2,1)} %get-tuple-element.152), channel_id=1, source_target_pairs={{0,1},{1,0},{2,3},{3,2},{4,5},{5,4},{6,7},{7,6},{8,9},{9,8},{10,11... | collective-permute-start | bytes 1966088 | tf_op jit(solution)/shard_map/ppermute | solution.py:191
  472.4 40.5 %collective-permute-start.54 = (bf16[56,2816]{1,0:T(8,128)(2,1)S(1)}, bf16[56,2816]{1,0:T(8,128)(2,1)S(1)}, u32[]{:S(2)}, u32[]{:S(2)}) collective-permute-start(bf16[56,2816]{1,0:T(8,128)(2,1)S(1)} %slice.741), channel_id=1, source_target_pairs={{0,32},{32,64},{64,96},{96,0},{1,33},{33,65},{65,97},{97,1},{2,34}... | collective-permute-start | bytes 946184 | tf_op jit(solution)/shard_map/ppermute | solution.py:63
  472.7 40.2 %collective-permute-start.53 = (bf16[56,2816]{1,0:T(8,128)(2,1)S(1)}, bf16[56,2816]{1,0:T(8,128)(2,1)S(1)}, u32[]{:S(2)}, u32[]{:S(2)}) collective-permute-start(bf16[56,2816]{1,0:T(8,128)(2,1)S(1)} %slice.741), channel_id=1, source_target_pairs={{0,96},{32,0},{64,32},{96,64},{1,97},{33,1},{65,33},{97,65},{2,98}... | collective-permute-start | bytes 946184 | tf_op jit(solution)/shard_map/ppermute | solution.py:63
  560.0 21.2 %collective-permute-start.61 = (bf16[16,56,1152]{2,1,0:T(8,128)(2,1)}, bf16[16,56,1152]{2,1,0:T(8,128)(2,1)}, u32[]{:S(2)}, u32[]{:S(2)}) collective-permute-start(bf16[16,56,1152]{2,1,0:T(8,128)(2,1)} %pad_maximum_fusion.2), channel_id=1, source_target_pairs={{0,1},{1,0},{2,3},{3,2},{4,5},{5,4},{6,7},{7,6},{8,9},{9,8},{10,11... | collective-permute-start | bytes 6193160 | tf_op jit(solution)/shard_map/ppermute | solution.py:628
  608.0 26.4 %collective-permute-start.68 = (bf16[4,56,1152]{2,1,0:T(8,128)(2,1)}, bf16[4,56,1152]{2,1,0:T(8,128)(2,1)}, u32[]{:S(2)}, u32[]{:S(2)}) collective-permute-start(bf16[4,56,1152]{2,1,0:T(8,128)(2,1)} %pad_maximum_fusion.9), channel_id=1, source_target_pairs={{0,8},{1,9},{2,10},{3,11},{4,12},{5,13},{6,14},{7,15},{8,16},{9,17... | collective-permute-start | bytes 1548296 | tf_op jit(solution)/shard_map/ppermute | solution.py:605
  608.0 26.4 %collective-permute-start.69 = (bf16[4,56,1152]{2,1,0:T(8,128)(2,1)}, bf16[4,56,1152]{2,1,0:T(8,128)(2,1)}, u32[]{:S(2)}, u32[]{:S(2)}) collective-permute-start(bf16[4,56,1152]{2,1,0:T(8,128)(2,1)} %pad_maximum_fusion.10), channel_id=1, source_target_pairs={{0,24},{1,25},{2,26},{3,27},{4,28},{5,29},{6,30},{7,31},{8,0},{9,1... | collective-permute-start | bytes 1548296 | tf_op jit(solution)/shard_map/ppermute | solution.py:606
  611.9 24.6 %collective-permute-start.66 = (bf16[128,3456]{1,0:T(8,128)(2,1)}, bf16[128,3456]{1,0:T(8,128)(2,1)}, u32[]{:S(2)}, u32[]{:S(2)}) collective-permute-start(bf16[128,3456]{1,0:T(8,128)(2,1)} %pad_maximum_fusion.6), channel_id=1, source_target_pairs={{0,32},{32,64},{64,96},{96,0},{1,33},{33,65},{65,97},{97,1},{2,34}... | collective-permute-start | bytes 2654216 | tf_op jit(solution)/shard_map/ppermute | solution.py:96
  614.9 21.6 %collective-permute-start.67 = (bf16[128,3456]{1,0:T(8,128)(2,1)}, bf16[128,3456]{1,0:T(8,128)(2,1)}, u32[]{:S(2)}, u32[]{:S(2)}) collective-permute-start(bf16[128,3456]{1,0:T(8,128)(2,1)} %pad_maximum_fusion.7), channel_id=1, source_target_pairs={{0,96},{32,0},{64,32},{96,64},{1,97},{33,1},{65,33},{97,65},{2,98}... | collective-permute-start | bytes 2654216 | tf_op jit(solution)/shard_map/ppermute | solution.py:97
  658.6 22.7 %collective-permute-start.80 = (bf16[56,4864]{1,0:T(8,128)(2,1)}, bf16[56,4864]{1,0:T(8,128)(2,1)S(1)}, u32[]{:S(2)}, u32[]{:S(2)}) collective-permute-start(bf16[56,4864]{1,0:T(8,128)(2,1)} %pad_maximum_fusion.8), channel_id=1, source_target_pairs={{0,32},{32,64},{64,96},{96,0},{1,33},{33,65},{65,97},{97,1},{2,34}... | collective-permute-start | bytes 1634312 | tf_op jit(solution)/shard_map/ppermute | solution.py:63
  659.0 23.8 %collective-permute-start.79 = (bf16[56,4864]{1,0:T(8,128)(2,1)}, bf16[56,4864]{1,0:T(8,128)(2,1)S(1)}, u32[]{:S(2)}, u32[]{:S(2)}) collective-permute-start(bf16[56,4864]{1,0:T(8,128)(2,1)} %pad_maximum_fusion.8), channel_id=1, source_target_pairs={{0,96},{32,0},{64,32},{96,64},{1,97},{33,1},{65,33},{97,65},{2,98}... | collective-permute-start | bytes 1634312 | tf_op jit(solution)/shard_map/ppermute | solution.py:63
  682.0 22.8 %collective-permute-start.81 = (bf16[28,4864]{1,0:T(8,128)(2,1)}, bf16[28,4864]{1,0:T(8,128)(2,1)S(1)}, u32[]{:S(2)}, u32[]{:S(2)}) collective-permute-start(bf16[28,4864]{1,0:T(8,128)(2,1)} %slice.949), channel_id=1, source_target_pairs={{0,32},{32,64},{64,96},{96,0},{1,33},{33,65},{65,97},{97,1},{2,34}... | collective-permute-start | bytes 817160 | tf_op jit(solution)/shard_map/ppermute | solution.py:68
  693.1 25.8 %collective-permute-start.77 = (bf16[144,1664]{1,0:T(8,128)(2,1)S(1)}, bf16[144,1664]{1,0:T(8,128)(2,1)S(1)}, u32[]{:S(2)}, u32[]{:S(2)}) collective-permute-start(bf16[144,1664]{1,0:T(8,128)(2,1)S(1)} %fusion.103), channel_id=1, source_target_pairs={{0,96},{32,0},{64,32},{96,64},{1,97},{33,1},{65,33},{97,65},{2,98}... | collective-permute-start | bytes 1437704 | tf_op jit(solution)/shard_map/ppermute | solution.py:63
  (196 other events, 2209.4 us)
Sparse Core Ops, SparseCore 0:
  13.0 79.5 all-gather.3
  95.5 67.2 all-gather.5
  165.7 78.1 all-gather.7
  324.7 124.3 reduce-scatter.2
  471.4 164.4 reduce-scatter.4

commit v3 on v2

--- a/solution.py
+++ b/solution.py
@@ -42,6 +42,9 @@
 AO_P = 1664
 XD = 256
 
+CTX = ("zy", "core")
+SEQ_CTX = ("seq",) + CTX
+
 F32 = jnp.float32
 BF16 = jnp.bfloat16
 VMEM_LIMIT = 60 * 1024 * 1024
@@ -77,6 +80,18 @@
 def spread_x(v):
     far = lax.ppermute(v, "seq", [(i, (i + 2) % NX) for i in range(NX)])
     return [v, lax.ppermute(v, "seq", LEFT), far, lax.ppermute(v, "seq", RIGHT)]
+
+
+def total_x_pairs(v):
+    half = -(-v.shape[1] // 256) * 128
+    pairs = ([(0, 1), (1, 0), (2, 3), (3, 2)], [(0, 3), (3, 0), (1, 2), (2, 1)])
+    out = []
+    for part, order in ((v[:, :half], pairs), (v[:, half:], pairs[::-1])):
+        for each in order:
+            other = lax.ppermute(part, "seq", each)
+            part = (part.astype(F32) + other.astype(F32)).astype(BF16)
+        out.append(part)
+    return jnp.concatenate(out, axis=1)
 
 
 def scatter_x_far(parts):
@@ -139,7 +154,7 @@
 
 
 def shift_ctx(v, by):
-    return lax.ppermute(v, "ctx", [(i, i + by) for i in range(NC) if 0 <= i + by < NC])
+    return lax.ppermute(v, CTX, [(i, i + by) for i in range(NC) if 0 <= i + by < NC])
 
 
 def tie(*values):
@@ -160,7 +175,7 @@
 
     def send(part, pairs):
         flat = jnp.concatenate([part[0].reshape(NX * N_STATE, CHP), part[1].reshape(NX, CHP)])
-        flat = lax.ppermute(flat.astype(BF16), "ctx", pairs).astype(F32)
+        flat = lax.ppermute(flat.astype(BF16), CTX, pairs).astype(F32)
         return (flat[: NX * N_STATE].reshape(NX, N_STATE, CHP), flat[NX * N_STATE :].reshape(NX, 1, CHP))
 
     part = (state, steps)
@@ -187,12 +202,16 @@
     return after(after(plane_pre, row_pre), inside)[0], beside
 
 
-def key_window_back(even, odd, core):
-    other = lax.ppermute(odd, "ctx", SWAP)
+def key_window_chip(even, odd, core):
+    other = lax.ppermute(odd, CTX, SWAP)
     none = jnp.zeros((T, odd.shape[1]), BF16)
     mine = even.astype(F32) + jnp.where(
         core == 0, jnp.concatenate([none, other]), jnp.concatenate([other, none])
     ).astype(F32)
+    return mine
+
+
+def key_window_back(mine):
     total = mine[4 * T :]
     for k in range(1, 5):
         term = mine[(4 - k) * T : (5 - k) * T].astype(BF16)
@@ -542,7 +561,7 @@
         at += width
 
 
-def products(pairs, us, rows_out=ROWS_64, spare=0):
+def products(pairs, us, rows_out=ROWS_64):
     width = sum(b.shape[1] for _, b in pairs)
     specs = []
     for a, b in pairs:
@@ -553,45 +572,68 @@
         grid=(2,),
         in_specs=specs,
         out_specs=pl.BlockSpec((NC // 2 * rows_out, width), lambda i: (i, 0)),
-        out_shape=jax.ShapeDtypeStruct((NC * rows_out, width + spare), BF16),
+        out_shape=jax.ShapeDtypeStruct((NC * rows_out, width), BF16),
         compiler_params=pltpu.CompilerParams(vmem_limit_bytes=VMEM_LIMIT),
         cost_estimate=cost(us),
     )(*[v for pair in pairs for v in pair])
 
 
-def product_into(held, a, b, us):
-    width = b.shape[1]
-    block = 384
-    skip = (held.shape[1] - width) // block
-
-    def kernel(a_ref, b_ref, _, out):
-        products_kernel(1, ROWS_64, a_ref, b_ref, out)
-
+def half_products_kernel(places, parity, *refs):
+    *ins, out, turned, rows = refs
+    count = len(places)
+    at = 0
+    for k, (held, offset) in enumerate(places):
+        a, b = ins[2 * k], ins[2 * k + 1]
+        depth, width = b.shape
+        turned[:, :depth] = a[...].astype(F32).T
+        for pair in range(NC // 4):
+            first = pl.multiple_of((2 * pair + parity[0]) * ROWS_P, 8)
+            block = jnp.concatenate(
+                [turned[pl.ds(first, ROWS_P), :depth], jnp.zeros((ROWS_64 - ROWS_P, depth), F32)]
+            )
+            rows[pair * ROWS_64 : (pair + 1) * ROWS_64, :depth] = block.astype(BF16)
+        for first in range(0, width, 512):
+            size = min(512, width - first)
+            product = dot(rows[:, :depth], b[:, first : first + size], 1, 0)
+            if held is not None:
+                other = ins[2 * count + held]
+                product = product + other[:, offset + first : offset + first + size].astype(F32)
+            out[:, at + first : at + first + size] = product.astype(BF16)
+        at += width
+
+
+def half_products(pairs, parity, us, held=(), places=None):
+    if places is None:
+        places = ((None, 0),) * len(pairs)
+    width = sum(b.shape[1] for _, b in pairs)
+    block = NC // 4 * ROWS_64
+    specs = [pl.BlockSpec(memory_space=pltpu.SMEM)]
+    for a, b in pairs:
+        specs.append(pl.BlockSpec((a.shape[0], DP // 2), lambda i: (0, i)))
+        specs.append(pl.BlockSpec(b.shape, lambda i: (0, 0)))
+    for v in held:
+        specs.append(pl.BlockSpec((block, v.shape[1]), lambda i: (i, 0)))
     return pl.pallas_call(
-        kernel,
-        grid=(2, width // block),
-        in_specs=[
-            pl.BlockSpec((a.shape[0], DP // 2), lambda i, j: (0, i)),
-            pl.BlockSpec((b.shape[0], block), lambda i, j: (0, j)),
-            pl.BlockSpec(memory_space=pl.ANY),
-        ],
-        out_specs=pl.BlockSpec((NC // 2 * ROWS_64, block), lambda i, j: (i, j + skip)),
-        out_shape=jax.ShapeDtypeStruct(held.shape, BF16),
-        input_output_aliases={2: 0},
+        functools.partial(half_products_kernel, places),
+        grid=(2,),
+        in_specs=specs,
+        out_specs=pl.BlockSpec((block, width), lambda i: (i, 0)),
+        out_shape=jax.ShapeDtypeStruct((2 * block, width), BF16),
+        scratch_shapes=[pltpu.VMEM((DP // 2, NX * T), F32), pltpu.VMEM((block, NX * T), BF16)],
         compiler_params=pltpu.CompilerParams(vmem_limit_bytes=VMEM_LIMIT),
         cost_estimate=cost(us),
-    )(a, b, held)
+    )(parity.astype(jnp.int32).reshape(1), *[v for pair in pairs for v in pair], *held)
 
 
 def rows_sum(v):
-    return lax.psum_scatter(v, "ctx", scatter_dimension=0, tiled=True)
+    return lax.psum_scatter(v, CTX, scatter_dimension=0, tiled=True)
 
 
 def ring_far(v, dim, place, plus, minus):
     parts = [lax.dynamic_index_in_dim(v, (place + k) % 4, dim, False) for k in range(4)]
     half = -(-v.shape[-1] // 256) * 128
-    from_left = lax.ppermute(parts[2][..., :half], "ctx", plus)
-    from_right = lax.ppermute(parts[2][..., half:], "ctx", minus)
+    from_left = lax.ppermute(parts[2][..., :half], CTX, plus)
+    from_right = lax.ppermute(parts[2][..., half:], CTX, minus)
     to_right = jnp.concatenate(
         [(parts[1][..., :half].astype(F32) + from_left.astype(F32)).astype(BF16), parts[1][..., half:]], axis=-1
     )
@@ -602,8 +644,8 @@
 
 
 def ring_near(own, to_right, to_left, plus, minus):
-    a = lax.ppermute(to_right, "ctx", plus)
-    b = lax.ppermute(to_left, "ctx", minus)
+    a = lax.ppermute(to_right, CTX, plus)
+    b = lax.ppermute(to_left, CTX, minus)
     return own.astype(F32) + a.astype(F32) + b.astype(F32)
 
 
@@ -625,7 +667,7 @@
 
 
 def core_sum(theirs, mine):
-    other = lax.ppermute(theirs, "ctx", SWAP)
+    other = lax.ppermute(theirs, CTX, SWAP)
     v = mine.astype(F32) + other.astype(F32)
     return v.reshape(4, 4, ROWS_P, v.shape[-1])
 
@@ -652,7 +694,7 @@
     cotangent,
 ):
     x = lax.axis_index("seq")
-    index = lax.axis_index("ctx")
+    index = lax.axis_index(CTX)
 
     def columns(v, first, count):
         return lax.dynamic_slice_in_dim(v, first, count, v.ndim - 1)
@@ -670,11 +712,11 @@
     def widen(v, matrix=None):
         return dot(v, widen_m if matrix is None else matrix, 1, 0, BF16)
 
-    narrow_m = lax.optimization_barrier(widen_m.T)
+    narrow_m = lax.optimization_barrier(jnp.pad(widen_m.T, ((0, 0), (0, AO_P - D))))
 
     def narrow(v, matrix=None):
         if matrix is None:
-            return dot(v.astype(BF16), narrow_m, 1, 0)
+            return dot(v.astype(BF16), narrow_m, 1, 0)[:, :D]
         return dot(v.astype(BF16), matrix, 1, 1)
 
     by_channel = pad_to(jnp.concatenate([xproj_weight, dt_weight], axis=1), 2 * ROWS, XD)
@@ -688,11 +730,11 @@
         ],
         axis=1,
     )
-    first = lax.all_gather(first, "ctx", axis=0, tiled=True)
+    first = lax.all_gather(first, CTX, axis=0, tiled=True)
     sub_mamba = lax.dynamic_slice_in_dim(mamba_out_weight, x * CSUB, CSUB, 0)
     sub_down = lax.dynamic_slice_in_dim(down_weight, x * FSUB, FSUB, 0)
     sub_wide = lax.ppermute(
-        jnp.concatenate([pad_to(sub_down, 48, D), pad_to(sub_mamba, 32, D)]), ("seq", "ctx"), TURN
+        jnp.concatenate([pad_to(sub_down, 48, D), pad_to(sub_mamba, 32, D)]), SEQ_CTX, TURN
     )
     second = jnp.concatenate(
         [
@@ -713,26 +755,8 @@
     normed_f, norm1_pullback = jax.vjp(norm_scale, inputs, norm_gain)
     normed = widen(normed_f.astype(BF16))
     normed, second = tie(normed, second)
-    second = lax.all_gather(second, "ctx", axis=0, tiled=True)
+    second = lax.all_gather(second, CTX, axis=0, tiled=True)
     normed_all = jnp.concatenate(gather_x(normed))
-    cot_all = jnp.concatenate(gather_x(pad_to(cotangent, T, AO_P)))
-    first, normed_all, cot_all, third, widen_m, narrow_m, widen_channels, widen_hidden = tie(
-        first, normed_all, cot_all, third, widen_m, narrow_m, widen_channels, widen_hidden
-    )
-    third = lax.all_gather(third, "ctx", axis=0, tiled=True)
-    w_in = first[:, : 2 * CHP]
-    small = first[:, 2 * CHP : 2 * CHP + 2 * XD].reshape(NC, ROWS_P, 2 * XD)
-    small = lax.dynamic_slice_in_dim(small, x * (NC // NX), NC // NX, 0)[:, :ROWS]
-    small = jnp.stack([small[:, :, :XD], small[:, :, XD:]], axis=1).reshape(CH, XD)
-    w_small = pad_to(small, CHP, XD)
-    w_xproj = w_small[:, : DT_RANK + 2 * N_STATE]
-    w_dt = w_small[:, DT_RANK + 2 * N_STATE : 2 * DT_RANK + 2 * N_STATE]
-    w_qkv = first[:, 2 * CHP + 2 * XD :]
-    w_attn = second[:, :AO_P]
-    w_mamba = second[:, AO_P:]
-    w_gate_up = third[:, : 2 * FFP]
-    w_down = third[:, 2 * FFP :]
-
     def channel(v):
         part = columns(v, x * CH, CH)
         return jnp.pad(part, ((0, 0),) * (v.ndim - 1) + ((0, CHP - CH),))
@@ -744,8 +768,27 @@
     decay_rate = -jnp.exp(channel(decay_log.T))
     rate2 = decay_rate * LOG2E
 
+    cot_all = jnp.concatenate(gather_x(pad_to(cotangent, T, AO_P)))
+    first, normed_all, cot_all, third, widen_m, narrow_m, widen_channels, widen_hidden, taps, conv_b, dt_b, skip, rate2 = tie(
+        first, normed_all, cot_all, third, widen_m, narrow_m, widen_channels, widen_hidden, taps, conv_b, dt_b, skip, rate2
+    )
+    third = lax.all_gather(third, CTX, axis=0, tiled=True)
+    w_in = first[:, : 2 * CHP]
+    w_qkv = first[:, 2 * CHP + 2 * XD :]
+    w_attn = second[:, :AO_P]
+    w_mamba = second[:, AO_P:]
+    w_gate_up = third[:, : 2 * FFP]
+    w_down = third[:, 2 * FFP :]
 
     in_proj = dot(normed_all, w_in, 1, 0)
+    in_proj, normed_q, first = tie(in_proj, normed, first)
+    small = first[:, 2 * CHP : 2 * CHP + 2 * XD]
+    small = small.reshape(NC, ROWS_P, 2 * XD)
+    small = lax.dynamic_slice_in_dim(small, x * (NC // NX), NC // NX, 0)[:, :ROWS]
+    small = jnp.stack([small[:, :, :XD], small[:, :, XD:]], axis=1).reshape(CH, XD)
+    w_small = pad_to(small, CHP, XD)
+    w_xproj = w_small[:, : DT_RANK + 2 * N_STATE]
+    w_dt = w_small[:, DT_RANK + 2 * N_STATE : 2 * DT_RANK + 2 * N_STATE]
     conv_in = in_proj[:, :CHP].reshape(NX, T, CHP)
     gate_z = in_proj[:, CHP:]
     tails = shift_ctx(conv_in[:, T - (CONV - 1) :].reshape(NX * (CONV - 1), CHP), 1)
@@ -757,7 +800,6 @@
     act_f, conv_pullback = jax.vjp(jax.nn.silu, conv_sum)
     act = act_f.astype(BF16)
     xproj_t = dot(w_xproj, act, 0, 1, BF16)
-    in_proj, normed_q = tie(in_proj, normed)
     projected = dot(normed_q, w_qkv, 1, 0, BF16)
     xproj_t, projected = tie(xproj_t, projected)
     xproj_t = total_x(xproj_t)
@@ -778,7 +820,7 @@
     )
 
     scan_end, kv_mine = tie(scan_end, kv_mine)
-    kv_other = lax.ppermute(kv_mine, "ctx", SWAP)
+    kv_other = lax.ppermute(kv_mine, CTX, SWAP)
     start, kv_other = carried(scan_end, steps, rate2, index, False, kv_other)
     place_here = jnp.stack([jnp.maximum(0, WINDOW - index * T), core]).astype(jnp.int32)
     attended, lse = head_call(
@@ -830,10 +872,10 @@
     residual = inputs + mixed
     ffn_f, norm2_pullback = jax.vjp(norm_scale, residual, ffn_gain)
     ffn_near = gather_x_near(widen(ffn_f.astype(BF16)))
-    (g_hidden,) = tie(dot(cot_all, w_down, 1, 1, BF16))
+    g_hidden = dot(cot_all, w_down, 1, 1, BF16)
+    g_hidden, *ffn_near = tie(g_hidden, *ffn_near)
     g_hidden = narrow(g_hidden, widen_hidden)
-    g_hidden, *ffn_near = tie(g_hidden, *ffn_near)
-    ffn_all = jnp.concatenate(gather_x_far(*ffn_near))
+    ffn_all, g_hidden = tie(jnp.concatenate(gather_x_far(*ffn_near)), g_hidden)
     gate_up = dot(ffn_all, w_gate_up, 1, 0)
 
     def swiglu(gate, up):
@@ -857,11 +899,10 @@
     g_attn = pad_to(g_attn_f.astype(BF16), T, AO_P)
     g_mamba_near = gather_x_near(pad_to(g_mamba_f.astype(BF16), T, AO_P))
 
-    g_attended = narrow(dot(g_attn, w_attn, 1, 1, BF16)).astype(BF16)
-    down_terms = dot(hidden, w_down, 1, 0, BF16)
+    (g_attended,) = tie(dot(g_attn, w_attn, 1, 1, BF16))
+    g_attended = narrow(g_attended).astype(BF16)
     g_attended, *g_mamba_near = tie(g_attended, *g_mamba_near)
     g_mamba_all = jnp.concatenate(gather_x_far(*g_mamba_near))
-    g_mamba_all, down_terms = tie(g_mamba_all, down_terms)
     (g_gated,) = tie(dot(g_mamba_all, w_mamba, 1, 1, BF16))
     (g_gated,) = tie(narrow(g_gated, widen_channels))
     silu_z, gate_pullback = jax.vjp(jax.nn.silu, gate_z)
@@ -897,19 +938,16 @@
         ],
         22,
     )
-    g_projected = jnp.concatenate([g_queries, key_window_back(g_even, g_odd, core).astype(BF16)], axis=1)
-    g_projected = pad_to(g_projected, T, QKV_P)
-    branch_term = products(
-        [(attended, g_attn), (gated, g_mamba_all), (normed_all, g_gate_z.astype(BF16))],
-        12,
-        spare=QKV_P,
-    )
-    branch_term = product_into(branch_term, normed, g_projected, 4)
-    later, branch_term, ffn_sum = tie(later, branch_term, ffn_sum)
-    branch_sum = rows_sum(branch_term)
-
-    gate_up_near = gather_x_near(ffn_sum[:ROWS_P, : 2 * FFP])
-
+    kv_chip = key_window_chip(g_even, g_odd, core)
+    branch_pairs = [
+        (attended, g_attn),
+        (gated, g_mamba_all),
+        (normed_all, g_gate_z.astype(BF16)),
+    ]
+    theirs_1 = half_products(branch_pairs, 1 - core, 8)
+    later, theirs_1, kv_chip = tie(later, theirs_1, kv_chip)
+    other_1 = lax.ppermute(theirs_1, CTX, SWAP)
+    g_kv_own = key_window_back(kv_chip)
     g_step, g_act, g_rate, g_b, g_c = seq_call(
         adjoint_kernel,
         [
@@ -942,7 +980,15 @@
         ],
         cost(25),
     )
-    g_step, *gate_up_near = tie(g_step, *gate_up_near)
+    g_step, other_1, g_kv_own, ffn_sum = tie(g_step, other_1, g_kv_own, ffn_sum)
+    gate_up_near = gather_x_near(ffn_sum[:ROWS_P, : 2 * FFP])
+    g_projected = pad_to(jnp.concatenate([g_queries, g_kv_own.astype(BF16)], axis=1), T, QKV_P)
+    branch_pairs.append((normed, g_projected))
+    other_2 = lax.ppermute(half_products(branch_pairs[3:], 1 - core, 3), CTX, SWAP)
+    branch_pairs = [branch_pairs[0], branch_pairs[3], branch_pairs[1], branch_pairs[2]]
+    branch_term = half_products(
+        branch_pairs, core, 12, [other_1, other_2], ((0, 0), (1, 0), (0, AO_P), (0, 2 * AO_P))
+    )
     g_decay = jnp.sum(g_rate, axis=0) * decay_rate
     g_pre_f = g_step * jax.nn.sigmoid(pre)
     g_dt_bias = jnp.sum(g_pre_f, axis=0)
@@ -950,7 +996,8 @@
     dt_term = dot(g_pre, dt_low_t, 0, 1, BF16)
     g_xproj_t = jnp.concatenate([dot(w_dt, g_pre, 0, 1), g_b, g_c]).astype(BF16)
     g_xproj_t = total_x(g_xproj_t).astype(BF16)
-    g_xproj_t, *gate_up = tie(g_xproj_t, *gather_x_far(*gate_up_near))
+    g_xproj_t, branch_term, *gate_up_near = tie(g_xproj_t, branch_term, *gate_up_near)
+    branch_sum = lax.psum_scatter(branch_term, "zy", scatter_dimension=0, tiled=True)
     xproj_term = dot(act, g_xproj_t, 0, 1, BF16)
     g_act = g_act + dot(g_xproj_t, w_xproj, 0, 1)
     (g_conv_sum,) = conv_pullback(g_act)
@@ -970,14 +1017,10 @@
     small_term = jnp.pad(small_term.reshape(NC, CSUB, XD), ((0, 0), (0, ROWS_P - CSUB), (0, 0)))
     in_c_term = products([(normed_all, g_in_proj[:, :CHP])], 4, ROWS_P)
     theirs, mine = core_halves([in_c_term, small_term.reshape(DP, XD)], core)
-    theirs, mine, g_in_proj, g_projected = tie(theirs, mine, g_in_proj, g_projected)
+    theirs, mine, hidden = tie(theirs, mine, hidden)
+    down_terms = dot(hidden, w_down, 1, 0, BF16)
     in_half = core_sum(theirs, mine)
-    g_normed_attn = dot(g_projected, w_qkv, 1, 1)
-    g_normed_terms = dot(g_in_proj, w_in, 1, 1, BF16)
-    g_norm_gain = jnp.sum(g_normed_terms.astype(F32) * normed_all.astype(F32), axis=0)
-    g_norm_gain = g_norm_gain + jnp.sum(g_normed_attn * normed.astype(F32), axis=0)
-    g_norm_gain = g_norm_gain.reshape(NC, ROWS_P)[:, :ROWS].reshape(D) / norm_gain
-    gains = jnp.stack([g_norm_gain, g_attn_gain, g_mamba_gain, g_ffn_gain])
+    gains = jnp.stack([jnp.zeros_like(g_attn_gain), g_attn_gain, g_mamba_gain, g_ffn_gain])
     gains = jnp.pad(gains, ((0, 0), (0, 2 * CHP - D))).reshape(8, CHP)
     table = jnp.concatenate(
         [
@@ -993,41 +1036,52 @@
     table = jnp.pad(table, ((0, 0), (0, 4 * XD - CHP))).reshape(NC // 2, 8, XD)
     table = jnp.pad(table, ((0, 0), (32, ROWS_P - 40), (CHP, 0))).reshape(4, 4, ROWS_P, CHP + XD)
     in_half = (in_half + table).astype(BF16)
+    in_half, g_in_proj, g_projected, down_terms = tie(in_half, g_in_proj, g_projected, down_terms)
+    g_normed_terms = dot(g_in_proj, w_in, 1, 1, BF16)
     both = jnp.concatenate([g_normed_terms, down_terms], axis=1)
-    in_half, both = tie(in_half, both)
     both = scatter_x_far([both[k * T : (k + 1) * T] for k in range(NX)])
     along_z = (ring_pairs(8, 1), ring_pairs(8, -1))
     along_y = (ring_pairs(2, 1), ring_pairs(2, -1))
     in_half = ring_far(in_half, 0, index // 8, *along_z)
     in_half, both = tie(in_half, both)
+    both = scatter_x_near(*both)
+    g_normed_attn = dot(g_projected, w_qkv, 1, 1)
+    in_half, g_normed_attn, gate_up_near = tie(in_half, g_normed_attn, gate_up_near)
+    gate_up = gather_x_far(*gate_up_near)
     in_half = ring_near(*in_half, *along_z).astype(BF16)
-    both = scatter_x_near(*both)
-    in_half, branch_sum = tie(in_half, branch_sum)
-    branch = jnp.concatenate([branch_sum[:ROWS_P, :AO_P], branch_sum[:ROWS_P, 2 * AO_P :]], axis=1)
-    branch = gather_x_near(branch)
-    in_sum = ring_near(*ring_far(in_half, 0, (index // 2) % 4, *along_y), *along_y)
-    table = jnp.broadcast_to(in_sum[None, 32:40, CHP:], (NC, 8, XD))
+    in_half, both = tie(in_half, both)
+    in_half = ring_far(in_half, 0, (index // 2) % 4, *along_y)
+    (g_normed,) = tie(narrow(both[:, :DP] + g_normed_attn))
+    g_norm1, g_norm_gain = norm1_pullback(g_normed)
+    in_half, g_norm1, g_norm_gain = tie(in_half, g_norm1, g_norm_gain)
+    tokens_grad = g_residual + g_norm1
+    output = (residual + both[:, DP : DP + D]).astype(BF16)
+    in_sum = ring_near(*in_half, *along_y)
+    in_sum, branch_sum = tie(in_sum, branch_sum)
+    branch = total_x_pairs(branch_sum[:ROWS_P, : AO_P + QKV_P])
+    g_norm_gain = jnp.pad(g_norm_gain, (0, 8 * XD - D)).reshape(8, XD)
+    table = jnp.concatenate([in_sum[32:40, CHP:], g_norm_gain])
+    table = jnp.broadcast_to(table[None], (NC, 16, XD))
     in_sum = in_sum.astype(BF16)
     owned = jnp.concatenate(
         [
             ffn_sum[:48, 2 * FFP : 2 * FFP + AO_P],
-            branch_sum[:32, AO_P : 2 * AO_P],
+            branch_sum[:32, AO_P + QKV_P : 2 * AO_P + QKV_P],
             pad_to(in_sum[:32, CHP:], 32, AO_P),
         ]
     )
-    owned = lax.ppermute(owned, ("seq", "ctx"), TURN_BACK)
-    in_parts = in_order(spread_x(in_sum[:, :CHP]), x)
-    table = lax.all_to_all(table, "ctx", 0, 0, tiled=True)
-    table = jnp.sum(table.reshape(NC // 2, 2, 2, 4 * XD), axis=1).reshape(NC, 4 * XD)
-    last = gather_x(jnp.concatenate([owned, pad_to(table.astype(BF16), NC, AO_P)]))
-    last = in_order(last, x)
-    by_rows = jnp.concatenate([v[112:136, :CH] for v in last], axis=1).astype(F32)
-    gains = sum(v[136:144, :CHP].astype(F32) for v in last).reshape(4, 2 * CHP)[:, :D]
-
-    (g_normed,) = tie(narrow(both[:, :DP] + g_normed_attn))
-    g_norm1, _ = norm1_pullback(g_normed)
-    tokens_grad = g_residual + g_norm1
-    output = (residual + both[:, DP : DP + D]).astype(BF16)
+    owned = lax.ppermute(owned, SEQ_CTX, TURN_BACK)
+    in_both = jnp.concatenate([in_sum[:, :CHP], branch_sum[:ROWS_P, 2 * AO_P + QKV_P :]], axis=1)
+    in_parts = in_order(spread_x(in_both), x)
+    table = lax.all_to_all(table, CTX, 0, 0, tiled=True)
+    g_norm_gain = jnp.sum(table[:, 8:], axis=0).reshape(2, 4 * XD)
+    table = jnp.sum(table[:, :8].reshape(NC // 2, 2, 2, 4 * XD), axis=1).reshape(NC, 4 * XD)
+    table = jnp.concatenate([table, jnp.pad(g_norm_gain, ((0, 14), (0, 0)))])
+    last = in_order(gather_x(owned), x)
+    tables = in_order(spread_x(table.astype(BF16)), x)
+    by_rows = jnp.concatenate([v[:24, :CH] for v in tables], axis=1).astype(F32)
+    gains = sum(v[24:32, :CHP].astype(F32) for v in tables).reshape(4, 2 * CHP)[:, :D]
+    g_norm_gain = sum(v[32:34].astype(F32) for v in tables).reshape(8 * XD)[:D]
 
     def side_by_side(parts, width):
         halves = []
@@ -1036,15 +1090,14 @@
             halves += [p[:ROWS, first_column : first_column + width] for p in parts]
         return jnp.concatenate(halves, axis=1).astype(F32)
 
-    branch = gather_x_far(*branch)
-    attn_w = sum(v[:ROWS, :D].astype(F32) for v in branch)
-    qkv_w = sum(v[:ROWS, AO_P + CHP : AO_P + CHP + QKV].astype(F32) for v in branch)
+    branch = branch.astype(F32)
+    attn_w = branch[:ROWS, :D]
+    qkv_w = branch[:ROWS, AO_P : AO_P + QKV]
     down_w = jnp.concatenate([v[:FSUB, :D] for v in last]).astype(F32)
     mamba_w = jnp.concatenate([v[48 : 48 + CSUB, :D] for v in last]).astype(F32)
     small_rows = jnp.concatenate([v[80 : 80 + CSUB, :XD] for v in last]).astype(F32)
-    in_z = in_order([v[:, AO_P : AO_P + CHP] for v in branch], x)
     in_w = jnp.concatenate(
-        [v[:ROWS, :CH] for v in in_parts + in_z], axis=1
+        [v[:ROWS, :CH] for v in in_parts] + [v[:ROWS, CHP : CHP + CH] for v in in_parts], axis=1
     ).astype(F32)
     g_xproj_w = small_rows[:, : DT_RANK + 2 * N_STATE]
     g_dt_w = small_rows[:, DT_RANK + 2 * N_STATE : 2 * DT_RANK + 2 * N_STATE]
@@ -1052,7 +1105,7 @@
     return (
         output,
         tokens_grad,
-        gains[0],
+        g_norm_gain,
         qkv_w,
         attn_w,
         in_w,
@@ -1073,9 +1126,10 @@
 
 
 def solution(mesh):
+    mesh = jax.sharding.Mesh(mesh.devices.reshape(NX, NC // 2, 2), SEQ_CTX)
     whole = P()
-    ctx = P("ctx", None)
-    both = P(("seq", "ctx"), None)
+    ctx = P(CTX, None)
+    both = P(SEQ_CTX, None)
     return jax.shard_map(
         body,
         mesh=mesh,

time: 752 us -> 727 us (0.967)
  waiting for transfers between devices: 127 us -> 95.9 us
  matrix products: 122 us -> 110 us
  starting transfers between devices: 157 us -> 168 us
  local copies, waits for them, and re-layouts: 77.2 us -> 86 us
    ppermute x36 -> x42, waiting for transfers between devices: 42.9 us -> 24.2 us  [the longest x14 8.64 us: send(): flat = lax.ppermute(flat.astype(BF16), CTX, pairs).astype(F32)]
    pallas_call x1 -> x3, Pallas kernels: 10.7 us -> 28.3 us  [half_products(): pl.pallas_call(functools.partial(half_products_kernel, places), grid=(2,)...]
    all_gather x3, waiting for transfers between devices: 15.5 us -> 1.26 us  [the longest x1 1.25 us: body(): first = lax.all_gather(first, CTX, axis=0, tiled=True)]
    pallas_call x3 -> x2, Pallas kernels: 33.9 us -> 20.8 us  [products(): pl.pallas_call(functools.partial(products_kernel, len(pairs), rows_out),...]
    dot_general x27 -> x28, matrix products: 122 us -> 110 us  [dot(): lax.dot_general(a, b, (((ca,), (cb,)), ((), ())), preferred_element_type=...]
    ppermute x36 -> x42, starting transfers between devices: 67.9 us -> 73.3 us  [the longest x10 23.7 us: shift_ctx(): lax.ppermute(v, CTX, [(i, i + by) for i in range(NC) if 0 <= i + by < NC])]
    ppermute x7 -> x6, waiting for transfers between devices: 22.7 us -> 19.9 us  [gather_x_far(): far_a = lax.ppermute(before[:half], 'seq', RIGHT)]
    ppermute x14 -> x12, starting transfers between devices: 30.3 us -> 31.2 us  [gather_x_near(): return (v, lax.ppermute(v, 'seq', LEFT), lax.ppermute(v, 'seq', RIGHT))]
  transfers between devices with their start and end apart: 92 -> 97, of which waited for: 36 -> 38; matrix products, arithmetic and copies ran while one was open for 31% -> 31% of each run, Pallas kernels for 21% -> 22%
where the time goes in v3:
time: 727 us; the launch traced here: 717 us
  starting transfers between devices  168 us (23%)
  Pallas kernels  159 us (22%)
  matrix products  110 us (15%)
  waiting for transfers between devices  95.9 us (13%)
  local copies, waits for them, and re-layouts  86 us (12%)
  other arithmetic  80 us (11%)
  between operations  17.8 us (2%)
    dot_general x28, matrix products, dot(): lax.dot_general(a, b, (((ca,), (cb,)), ((), ())), preferred_element_type=...  110 us
    pallas_call x4, Pallas kernels, seq_call(): pl.pallas_call(kernel, grid=(NX,), in_specs=[spec(a.shape, kind) for a, k...  68.4 us
    pallas_call x2, Pallas kernels, head_call(): pl.pallas_call(kernel, in_specs=[pl.BlockSpec(memory_space=pltpu.SMEM)] +...  41.6 us
    ppermute x12, starting transfers between devices, gather_x_near(): return (v, lax.ppermute(v, 'seq', LEFT), lax.ppermute(v, 'seq', RIGHT))  31.2 us
    pallas_call x3, Pallas kernels, half_products(): pl.pallas_call(functools.partial(half_products_kernel, places), grid=(2,)...  28.3 us
    unnamed x252, local copies, waits for them, and re-layouts  24.8 us
    ppermute x10, starting transfers between devices, shift_ctx(): lax.ppermute(v, CTX, [(i, i + by) for i in range(NC) if 0 <= i + by < NC])  23.7 us
    pallas_call x2, Pallas kernels, products(): pl.pallas_call(functools.partial(products_kernel, len(pairs), rows_out),...  20.8 us
  transfers between devices with their start and end apart: 97, of which 38 were waited for; matrix products, arithmetic and copies ran while one was open for 31% of the time, Pallas kernels for 22%

profile of v3, /device:TPU:14, one launch (start us, length us, event | category | flops | bytes accessed | tf_op | source)
XLA Modules:
  0.0 717.3 jit_solution(10925567955585707566)
XLA Ops:
  30.9 6.8 collective-permute-start.5
  37.7 5.6 pad.161
  64.2 10.8 %collective-permute-done.7 = bf16[64,1664]{1,0:T(8,128)(2,1)S(1)} collective-permute-done((bf16[64,1664]{1,0:T(8,128)(2,1)S(1)}, bf16[64,1664]{1,0:T(8,128)(2,1)S(1)}, u32[]{:S(2)}, u32[]{:S(2)}) %collective-permute-start.7) | collective-permute-done | bytes 213024 | tf_op jit(solution)/shard_map/ppermute | solution.py:71
  92.9 6.9 fusion.26
  108.8 5.6 fusion.40.projected
  140.0 9.4 %shard_map.330 = (f32[4,16,896]{2,1,0:T(8,128)}, f32[4,1,896]{2,1,0:T(1,128)}) custom-call(f32[512,896]{1,0:T(8,128)} %get-tuple-element.471.step, bf16[512,896]{1,0:T(8,128)(2,1)} %copy-done.15, f32[16,512]{1,0:T(8,128)} %get-tuple-element.431.b_t, f32[16,896]{1,0:T(8,128)} %fusion.143.rate2), custom_call_target="tpu_custom_call" | custom-call | flops 8000000000 | bytes 8000000 | tf_op jit(solution)/shard_map/pallas_call | solution.py:420
  174.8 17.7 %shard_map.331 = (bf16[128,1600]{1,0:T(8,128)(2,1)}, f32[5,640,1]{2,1,0:T(8,128)}) custom-call(s32[2]{0:T(128)} %pad_add_fusion.1.place, bf16[128,2304]{1,0:T(8,128)(2,1)} %fusion.40.projected, bf16[640,640]{1,0:T(8,128)(2,1)} %constant_dynamic-update-slice_fusion.12.mine, bf16[640,640]{1,0:T(8,128)(2,1)} %copy-done.86), custom_call_target="tpu_custom_call" | custom-call | flops 15000000512 | bytes 15000000 | tf_op jit(solution)/shard_map/pallas_call | solution.py:525
  193.5 15.6 %shard_map.332 = (bf16[4,2048,896]{2,1,0:T(8,128)(2,1)}, f32[512,896]{1,0:T(8,128)}, bf16[512,896]{1,0:T(8,128)(2,1)}) custom-call(f32[512,896]{1,0:T(8,128)} %get-tuple-element.471.step, bf16[512,896]{1,0:T(8,128)(2,1)} %copy-done.15, f32[512,896]{1,0:T(8,128)} %get-tuple-element.354.gate_z, f32[16,512]{1,0:T(8,128)} %get-tuple-element.431.b_t, ...), custom_call_target="tpu_custom_call" | custom-call | flops 14000000000 | bytes 14000000 | tf_op jit(solution)/shard_map/pallas_call | solution.py:420
  213.7 7.2 %fusion.43 = bf16[512,1664]{1,0:T(8,128)(2,1)S(1)} fusion(bf16[512,1792]{1,0:T(8,128)(2,1)} %convolution_convert_fusion.1.refs_2_.refs_4_, bf16[1792,3328]{1,0:T(8,128)(2,1)} %all-gather.6.cloned.1.call-done), kind=kOutput, calls=%fused_computation.65 | convolution fusion | flops 3054305280 | bytes 9502720 | tf_op jit(solution)/shard_map/dot_general | solution.py:54
  234.4 6.7 collective-permute-done.28
  246.3 6.7 fusion.49
  267.9 9.1 %fusion.10 = f32[512,2816]{1,0:T(8,128)S(1)} fusion(bf16[512,1792]{1,0:T(8,128)(2,1)S(1)} %constant_dynamic-update-slice_fusion.17.refs_0_, bf16[1792,4480]{1,0:T(8,128)(2,1)} %all-gather.8.cloned.1.call-done), kind=kOutput, calls=%fused_computation.18 | convolution fusion | flops 5167382528 | bytes 17694720 | tf_op jit(solution)/shard_map/dot_general | solution.py:54
  281.5 9.8 %fusion.58 = bf16[512,1792]{1,0:T(8,128)(2,1)S(1)} fusion(bf16[1792,4480]{1,0:T(8,128)(2,1)} %all-gather.8.cloned.1.call-done, bf16[512,1408]{1,0:T(8,128)(2,1)S(1)} %get-tuple-element.351, bf16[512,1408]{1,0:T(8,128)(2,1)S(1)} %get-tuple-element.350), kind=kOutput, calls=%fused_computation.72 | convolution fusion | flops 5174067200 | bytes 14811136 | tf_op jit(solution)/shard_map/dot_general | solution.py:54
  307.0 15.4 %shard_map.333 = bf16[2048,4480]{1,0:T(8,128)(2,1)} custom-call(bf16[512,1792]{1,0:T(8,128)(2,1)} %copy-done.61, bf16[512,2816]{1,0:T(8,128)(2,1)} %pad_maximum_fusion.refs_1_, bf16[512,1792]{1,0:T(8,128)(2,1)} %convolution_convert_fusion.refs_2_, bf16[512,1664]{1,0:T(8,128)(2,1)} %constant_dynamic-update-slice_fusion.7.refs_3_), custom_call_target="tpu_custom_call" | custom-call | flops 14000000000 | bytes 14000000 | tf_op jit(solution)/shard_map/pallas_call | solution.py:570
  367.3 9.4 %shard_map.334 = f32[4,16,896]{2,1,0:T(8,128)} custom-call(f32[512,896]{1,0:T(8,128)} %get-tuple-element.471.step, f32[512,896]{1,0:T(8,128)} %get-tuple-element.333.g_scan, f32[16,512]{1,0:T(8,128)} %get-tuple-element.430.c_t, f32[16,896]{1,0:T(8,128)} %fusion.143.rate2), custom_call_target="tpu_custom_call" | custom-call | flops 8000000000 | bytes 8000000 | tf_op jit(solution)/shard_map/pallas_call | solution.py:420
  383.7 24.0 %shard_map.336 = (bf16[128,1600]{1,0:T(8,128)(2,1)}, bf16[640,640]{1,0:T(8,128)(2,1)}, bf16[512,640]{1,0:T(8,128)(2,1)}) custom-call(s32[2]{0:T(128)} %pad_add_fusion.1.place, bf16[128,2304]{1,0:T(8,128)(2,1)} %fusion.40.projected, bf16[640,640]{1,0:T(8,128)(2,1)} %constant_dynamic-update-slice_fusion.12.mine, bf16[640,640]{1,0:T(8,128)(2,1)} %copy-done.86, ...), custom_call_target="tpu_custom_call" | custom-call | flops 22000001024 | bytes 22000000 | tf_op jit(solution)/shard_map/pallas_call | solution.py:525
  413.0 9.8 %shard_map.335 = bf16[1024,4224]{1,0:T(8,128)(2,1)} custom-call(s32[1]{0:T(128)} %bitcast.47.parity, bf16[128,1792]{1,0:T(8,128)(2,1)} %copy-done.47, bf16[128,1664]{1,0:T(8,128)(2,1)} %pad.168.refs_1_, bf16[512,1792]{1,0:T(8,128)(2,1)} %convolution_convert_fusion.1.refs_2_.refs_4_, bf16[512,1664]{1,0:T(8,128)(2,1)} %copy-done.62, ...), custom_call_target="tpu_custom_call" | custom-call | flops 8000000000 | bytes 8000000 | tf_op jit(solution)/shard_map/pallas_call | solution.py:616
  436.6 34.0 %shard_map.337 = (f32[512,896]{1,0:T(8,128)}, f32[512,896]{1,0:T(8,128)}, f32[4,16,896]{2,1,0:T(8,128)}, f32[16,512]{1,0:T(8,128)}, f32[16,512]{1,0:T(8,128)}) custom-call(f32[512,896]{1,0:T(8,128)} %get-tuple-element.471.step, bf16[512,896]{1,0:T(8,128)(2,1)} %copy-done.15, f32[512,896]{1,0:T(8,128)} %get-tuple-element.333.g_scan, ...), custom_call_target="tpu_custom_call" | custom-call | flops 24999999488 | bytes 25000000 | tf_op jit(solution)/shard_map/pallas_call | solution.py:420
  491.5 14.0 %shard_map.339 = bf16[1024,6528]{1,0:T(8,128)(2,1)} custom-call(s32[1]{0:T(128)} %bitcast.29.parity, bf16[128,1792]{1,0:T(8,128)(2,1)} %copy-done.47, bf16[128,1664]{1,0:T(8,128)(2,1)} %pad.168.refs_1_, bf16[128,1792]{1,0:T(8,128)(2,1)} %copy-done.32, bf16[128,2304]{1,0:T(8,128)(2,1)} %fusion.99.refs_1_.refs_3_, ...), custom_call_target="tpu_custom_call" | custom-call | flops 12000000000 | bytes 12000000 | tf_op jit(solution)/shard_map/pallas_call | solution.py:616
  537.7 6.8 fusion.52
  547.9 5.5 collective-permute-start.62
  639.0 6.8 all-to-all-start
  649.3 5.8 collective-permute-start.84
  665.8 13.9 %collective-permute-start.85 = (bf16[112,1664]{1,0:T(8,128)(2,1)S(1)}, bf16[112,1664]{1,0:T(8,128)(2,1)S(1)}, u32[]{:S(2)}, u32[]{:S(2)}) collective-permute-start(bf16[112,1664]{1,0:T(8,128)(2,1)S(1)} %collective-permute-done.84), channel_id=1, source_target_pairs={{0,32},{32,64},{64,96},{96,0},{1,33},{33,65},{65,97},{97,1},{2,34}... | collective-permute-start | bytes 1118216 | tf_op jit(solution)/shard_map/ppermute | solution.py:66
  (791 shorter events, 436.2 us)
Async XLA Ops:
  7.2 85.4 %all-gather.4.cloned.1.call-start = ((), (), s32[]{:S(2)}) async-start(), calls=%async_computation.3 | async-start | bytes 17031168 | tf_op jit(solution)/shard_map/all_gather | solution.py:733
  12.9 200.8 %all-gather.6.cloned.1.call-start = ((), (), s32[]{:S(2)}) async-start(), calls=%async_computation.4 | async-start | bytes 12300288 | tf_op jit(solution)/shard_map/all_gather | solution.py:758
  29.5 216.8 %all-gather.8.cloned.1.call-start = ((), (), s32[]{:S(2)}) async-start(), calls=%async_computation.5 | async-start | bytes 16558080 | tf_op jit(solution)/shard_map/all_gather | solution.py:775
  30.9 30.5 %collective-permute-start.5 = (bf16[128,1664]{1,0:T(8,128)(2,1)}, bf16[128,1664]{1,0:T(8,128)(2,1)S(1)}, u32[]{:S(2)}, u32[]{:S(2)}) collective-permute-start(bf16[128,1664]{1,0:T(8,128)(2,1)} %get-tuple-element.416), channel_id=1, source_target_pairs={{0,96},{32,0},{64,32},{96,64},{1,97},{33,1},{65,33},{97,65},{2,98}... | collective-permute-start | bytes 1277960 | tf_op jit(solution)/shard_map/ppermute | solution.py:66
  37.7 23.5 %collective-permute-start.6 = (bf16[128,1664]{1,0:T(8,128)(2,1)}, bf16[128,1664]{1,0:T(8,128)(2,1)S(1)}, u32[]{:S(2)}, u32[]{:S(2)}) collective-permute-start(bf16[128,1664]{1,0:T(8,128)(2,1)} %get-tuple-element.416), channel_id=1, source_target_pairs={{0,32},{32,64},{64,96},{96,0},{1,33},{33,65},{65,97},{97,1},{2,34}... | collective-permute-start | bytes 1277960 | tf_op jit(solution)/shard_map/ppermute | solution.py:66
  56.3 24.8 %collective-permute-start.1 = (bf16[128,1792]{1,0:T(8,128)(2,1)S(1)}, bf16[128,1792]{1,0:T(8,128)(2,1)S(1)}, u32[]{:S(2)}, u32[]{:S(2)}) collective-permute-start(bf16[128,1792]{1,0:T(8,128)(2,1)S(1)} %convolution_convert_fusion.4.refs_0_.refs_2_), channel_id=1, source_target_pairs={{0,96},{32,0},{64,32},{96,64},{1,97},{33,1},{65,33},{97,65},{2,98}... | collective-permute-start | bytes 1376264 | tf_op jit(solution)/shard_map/ppermute | solution.py:66
  92.6 379.1 %reduce-scatter.3.cloned.1.call-start = ((), (), s32[]{:S(2)}) async-start(), calls=%async_computation.6 | async-start | bytes 18923520 | tf_op jit(solution)/shard_map/reduce_scatter | solution.py:629
  122.1 27.3 %collective-permute-start.13 = (bf16[128,640]{1,0:T(8,128)(2,1)S(1)}, bf16[128,640]{1,0:T(8,128)(2,1)S(1)}, u32[]{:S(2)}, u32[]{:S(2)}) collective-permute-start(bf16[128,640]{1,0:T(8,128)(2,1)S(1)} %slice.672), channel_id=1, source_target_pairs={{0,8},{1,9},{2,10},{3,11},{4,12},{5,13},{6,14},{7,15},{8,16},{9,17... | collective-permute-start | bytes 491528 | tf_op jit(solution)/shard_map/ppermute | solution.py:157
  124.0 26.1 %collective-permute-start.14 = (bf16[128,640]{1,0:T(8,128)(2,1)S(1)}, bf16[128,640]{1,0:T(8,128)(2,1)S(1)}, u32[]{:S(2)}, u32[]{:S(2)}) collective-permute-start(bf16[128,640]{1,0:T(8,128)(2,1)S(1)} %slice.672), channel_id=1, source_target_pairs={{0,6},{1,7},{2,8},{3,9},{4,10},{5,11},{6,12},{7,13},{8,14},{9,15},... | collective-permute-start | bytes 491528 | tf_op jit(solution)/shard_map/ppermute | solution.py:157
  128.4 22.3 %collective-permute-start.15 = (bf16[128,640]{1,0:T(8,128)(2,1)S(1)}, bf16[128,640]{1,0:T(8,128)(2,1)S(1)}, u32[]{:S(2)}, u32[]{:S(2)}) collective-permute-start(bf16[128,640]{1,0:T(8,128)(2,1)S(1)} %slice.672), channel_id=1, source_target_pairs={{0,4},{1,5},{2,6},{3,7},{4,8},{5,9},{6,10},{7,11},{8,12},{9,13},{1... | collective-permute-start | bytes 491528 | tf_op jit(solution)/shard_map/ppermute | solution.py:157
  167.6 24.8 %collective-permute-start.22 = (bf16[68,896]{1,0:T(8,128)(2,1)S(1)}, bf16[68,896]{1,0:T(8,128)(2,1)S(1)}, u32[]{:S(2)}, u32[]{:S(2)}) collective-permute-start(bf16[68,896]{1,0:T(8,128)(2,1)S(1)} %pad_maximum_fusion.28), channel_id=1, source_target_pairs={{0,8},{1,9},{2,10},{3,11},{4,12},{5,13},{6,14},{7,15},{8,16},{9,17... | collective-permute-start | bytes 365576 | tf_op jit(solution)/shard_map/ppermute | solution.py:178
  324.5 305.0 %reduce-scatter.5.cloned.1.call-start = ((), (), s32[]{:S(2)}) async-start(), calls=%async_computation.7 | async-start | bytes 14204928 | tf_op jit(solution)/shard_map/reduce_scatter | solution.py:1000
  379.7 28.1 %collective-permute-start.44 = (bf16[68,896]{1,0:T(8,128)(2,1)S(1)}, bf16[68,896]{1,0:T(8,128)(2,1)S(1)}, u32[]{:S(2)}, u32[]{:S(2)}) collective-permute-start(bf16[68,896]{1,0:T(8,128)(2,1)S(1)} %pad_maximum_fusion.29), channel_id=1, source_target_pairs={{0,2},{1,3},{2,4},{3,5},{4,6},{5,7},{6,0},{7,1},{8,10},{9,11},{10,... | collective-permute-start | bytes 365576 | tf_op jit(solution)/shard_map/ppermute | solution.py:178
  379.8 28.1 %collective-permute-start.43 = (bf16[68,896]{1,0:T(8,128)(2,1)S(1)}, bf16[68,896]{1,0:T(8,128)(2,1)S(1)}, u32[]{:S(2)}, u32[]{:S(2)}) collective-permute-start(bf16[68,896]{1,0:T(8,128)(2,1)S(1)} %pad_maximum_fusion.29), channel_id=1, source_target_pairs={{0,4},{1,5},{2,6},{3,7},{4,0},{5,1},{6,2},{7,3},{8,12},{9,13},{10,... | collective-permute-start | bytes 365576 | tf_op jit(solution)/shard_map/ppermute | solution.py:178
  383.1 24.8 %collective-permute-start.42 = (bf16[68,896]{1,0:T(8,128)(2,1)S(1)}, bf16[68,896]{1,0:T(8,128)(2,1)S(1)}, u32[]{:S(2)}, u32[]{:S(2)}) collective-permute-start(bf16[68,896]{1,0:T(8,128)(2,1)S(1)} %pad_maximum_fusion.29), channel_id=1, source_target_pairs={{0,6},{1,7},{2,0},{3,1},{4,2},{5,3},{6,4},{7,5},{8,14},{9,15},{10,... | collective-permute-start | bytes 365576 | tf_op jit(solution)/shard_map/ppermute | solution.py:178
  428.8 42.9 %collective-permute-start.49 = (bf16[1024,4224]{1,0:T(8,128)(2,1)}, bf16[1024,4224]{1,0:T(8,128)(2,1)}, u32[]{:S(2)}, u32[]{:S(2)}) collective-permute-start(bf16[1024,4224]{1,0:T(8,128)(2,1)} %shard_map.335), channel_id=1, source_target_pairs={{0,1},{1,0},{2,3},{3,2},{4,5},{5,4},{6,7},{7,6},{8,9},{9,8},{10,11... | collective-permute-start | bytes 25952264 | tf_op jit(solution)/shard_map/ppermute | solution.py:949
  430.0 40.6 %collective-permute-start.53 = (bf16[128,640]{1,0:T(8,128)(2,1)S(1)}, bf16[128,640]{1,0:T(8,128)(2,1)S(1)}, u32[]{:S(2)}, u32[]{:S(2)}) collective-permute-start(bf16[128,640]{1,0:T(8,128)(2,1)S(1)} %get-tuple-element.401), channel_id=1, source_target_pairs={{8,0},{9,1},{10,2},{11,3},{12,4},{13,5},{14,6},{15,7},{16,8},{17,9... | collective-permute-start | bytes 491528 | tf_op jit(solution)/shard_map/ppermute | solution.py:157
  431.3 39.3 %collective-permute-start.52 = (bf16[128,640]{1,0:T(8,128)(2,1)S(1)}, bf16[128,640]{1,0:T(8,128)(2,1)S(1)}, u32[]{:S(2)}, u32[]{:S(2)}) collective-permute-start(bf16[128,640]{1,0:T(8,128)(2,1)S(1)} %get-tuple-element.402), channel_id=1, source_target_pairs={{6,0},{7,1},{8,2},{9,3},{10,4},{11,5},{12,6},{13,7},{14,8},{15,9},... | collective-permute-start | bytes 491528 | tf_op jit(solution)/shard_map/ppermute | solution.py:157
  432.6 38.0 %collective-permute-start.51 = (bf16[128,640]{1,0:T(8,128)(2,1)S(1)}, bf16[128,640]{1,0:T(8,128)(2,1)S(1)}, u32[]{:S(2)}, u32[]{:S(2)}) collective-permute-start(bf16[128,640]{1,0:T(8,128)(2,1)S(1)} %get-tuple-element.403), channel_id=1, source_target_pairs={{4,0},{5,1},{6,2},{7,3},{8,4},{9,5},{10,6},{11,7},{12,8},{13,9},{1... | collective-permute-start | bytes 491528 | tf_op jit(solution)/shard_map/ppermute | solution.py:157
  433.9 36.8 %collective-permute-start.50 = (bf16[128,640]{1,0:T(8,128)(2,1)S(1)}, bf16[128,640]{1,0:T(8,128)(2,1)S(1)}, u32[]{:S(2)}, u32[]{:S(2)}) collective-permute-start(bf16[128,640]{1,0:T(8,128)(2,1)S(1)} %get-tuple-element.400), channel_id=1, source_target_pairs={{2,0},{3,1},{4,2},{5,3},{6,4},{7,5},{8,6},{9,7},{10,8},{11,9},{12,... | collective-permute-start | bytes 491528 | tf_op jit(solution)/shard_map/ppermute | solution.py:157
  547.9 22.7 %collective-permute-start.62 = (bf16[4,56,640]{2,1,0:T(8,128)(2,1)S(1)}, bf16[4,56,640]{2,1,0:T(8,128)(2,1)S(1)}, u32[]{:S(2)}, u32[]{:S(2)}) collective-permute-start(bf16[4,56,640]{2,1,0:T(8,128)(2,1)S(1)} %slice.913), channel_id=1, source_target_pairs={{0,8},{1,9},{2,10},{3,11},{4,12},{5,13},{6,14},{7,15},{8,16},{9,17... | collective-permute-start | bytes 860168 | tf_op jit(solution)/shard_map/ppermute | solution.py:635
  588.5 22.1 %collective-permute-start.69 = (bf16[128,3456]{1,0:T(8,128)(2,1)}, bf16[128,3456]{1,0:T(8,128)(2,1)}, u32[]{:S(2)}, u32[]{:S(2)}) collective-permute-start(bf16[128,3456]{1,0:T(8,128)(2,1)} %pad_maximum_fusion.6), channel_id=1, source_target_pairs={{0,96},{32,0},{64,32},{96,64},{1,97},{33,1},{65,33},{97,65},{2,98}... | collective-permute-start | bytes 2654216 | tf_op jit(solution)/shard_map/ppermute | solution.py:112
  639.0 40.9 %all-to-all-start = ((f32[32,16,256]{2,1,0:T(8,128)}), f32[32,16,256]{2,1,0:T(8,128)S(1)}, u32[]{:S(2)}, u32[]{:S(2)}) async-start(f32[32,16,256]{2,1,0:T(8,128)} %broadcast_in_dim.123), calls=%async_computation.2 | async-start | bytes 1048576 | tf_op jit(solution)/shard_map/all_to_all | solution.py:1076
  665.8 31.9 %collective-permute-start.85 = (bf16[112,1664]{1,0:T(8,128)(2,1)S(1)}, bf16[112,1664]{1,0:T(8,128)(2,1)S(1)}, u32[]{:S(2)}, u32[]{:S(2)}) collective-permute-start(bf16[112,1664]{1,0:T(8,128)(2,1)S(1)} %collective-permute-done.84), channel_id=1, source_target_pairs={{0,32},{32,64},{64,96},{96,0},{1,33},{33,65},{65,97},{97,1},{2,34}... | collective-permute-start | bytes 1118216 | tf_op jit(solution)/shard_map/ppermute | solution.py:66
  (180 other events, 1975.4 us)
Sparse Core Ops, SparseCore 0:
  13.0 79.5 all-gather.3
  95.5 66.2 all-gather.5
  164.7 76.5 all-gather.7
  324.6 133.9 reduce-scatter.2
  505.6 111.9 reduce-scatter.4

commit v4 on v3

--- a/solution.py
+++ b/solution.py
@@ -1042,21 +1042,18 @@
     both = scatter_x_far([both[k * T : (k + 1) * T] for k in range(NX)])
     along_z = (ring_pairs(8, 1), ring_pairs(8, -1))
     along_y = (ring_pairs(2, 1), ring_pairs(2, -1))
-    in_half = ring_far(in_half, 0, index // 8, *along_z)
-    in_half, both = tie(in_half, both)
+    in_half = ring_far(in_half, 1, (index // 2) % 4, *along_y)
     both = scatter_x_near(*both)
     g_normed_attn = dot(g_projected, w_qkv, 1, 1)
     in_half, g_normed_attn, gate_up_near = tie(in_half, g_normed_attn, gate_up_near)
     gate_up = gather_x_far(*gate_up_near)
-    in_half = ring_near(*in_half, *along_z).astype(BF16)
-    in_half, both = tie(in_half, both)
-    in_half = ring_far(in_half, 0, (index // 2) % 4, *along_y)
+    in_half = ring_near(*in_half, *along_y).astype(BF16)
+    in_half = ring_far(in_half, 0, index // 8, *along_z)
     (g_normed,) = tie(narrow(both[:, :DP] + g_normed_attn))
     g_norm1, g_norm_gain = norm1_pullback(g_normed)
-    in_half, g_norm1, g_norm_gain = tie(in_half, g_norm1, g_norm_gain)
     tokens_grad = g_residual + g_norm1
     output = (residual + both[:, DP : DP + D]).astype(BF16)
-    in_sum = ring_near(*in_half, *along_y)
+    in_sum = ring_near(*in_half, *along_z)
     in_sum, branch_sum = tie(in_sum, branch_sum)
     branch = total_x_pairs(branch_sum[:ROWS_P, : AO_P + QKV_P])
     g_norm_gain = jnp.pad(g_norm_gain, (0, 8 * XD - D)).reshape(8, XD)
@@ -1066,8 +1063,8 @@
     owned = jnp.concatenate(
         [
             ffn_sum[:48, 2 * FFP : 2 * FFP + AO_P],
-            branch_sum[:32, AO_P + QKV_P : 2 * AO_P + QKV_P],
-            pad_to(in_sum[:32, CHP:], 32, AO_P),
+            branch_sum[:CSUB, AO_P + QKV_P : 2 * AO_P + QKV_P],
+            pad_to(in_sum[:CSUB, CHP:].reshape(CSUB * XD // D, D), 32 - CSUB, AO_P),
         ]
     )
     owned = lax.ppermute(owned, SEQ_CTX, TURN_BACK)
@@ -1095,7 +1092,7 @@
     qkv_w = branch[:ROWS, AO_P : AO_P + QKV]
     down_w = jnp.concatenate([v[:FSUB, :D] for v in last]).astype(F32)
     mamba_w = jnp.concatenate([v[48 : 48 + CSUB, :D] for v in last]).astype(F32)
-    small_rows = jnp.concatenate([v[80 : 80 + CSUB, :XD] for v in last]).astype(F32)
+    small_rows = jnp.concatenate([v[48 + CSUB : 52 + CSUB, :D].reshape(CSUB, XD) for v in last]).astype(F32)
     in_w = jnp.concatenate(
         [v[:ROWS, :CH] for v in in_parts] + [v[:ROWS, CHP : CHP + CH] for v in in_parts], axis=1
     ).astype(F32)

time: 727 us -> 708 us (0.974)
  waiting for transfers between devices: 95.9 us -> 84.8 us
  starting transfers between devices: 168 us -> 158 us
    ppermute x2, waiting for transfers between devices: 0.01 us -> 13.1 us  [ring_far(): from_right = lax.ppermute(parts[2][..., half:], CTX, minus)]
  transfers between devices with their start and end apart: 97 -> 97, of which waited for: 38 -> 34; matrix products, arithmetic and copies ran while one was open for 31% -> 32% of each run, Pallas kernels for 22% -> 22%
where the time goes in v4:
time: 708 us; the launch traced here: 698 us
  Pallas kernels  159 us (22%)
  starting transfers between devices  158 us (22%)
  matrix products  113 us (16%)
  local copies, waits for them, and re-layouts  85.9 us (12%)
  waiting for transfers between devices  84.8 us (12%)
  other arithmetic  78.6 us (11%)
  between operations  17.9 us (3%)
    dot_general x28, matrix products, dot(): lax.dot_general(a, b, (((ca,), (cb,)), ((), ())), preferred_element_type=...  113 us
    pallas_call x4, Pallas kernels, seq_call(): pl.pallas_call(kernel, grid=(NX,), in_specs=[spec(a.shape, kind) for a, k...  68.5 us
    pallas_call x2, Pallas kernels, head_call(): pl.pallas_call(kernel, in_specs=[pl.BlockSpec(memory_space=pltpu.SMEM)] +...  41.6 us
    pallas_call x3, Pallas kernels, half_products(): pl.pallas_call(functools.partial(half_products_kernel, places), grid=(2,)...  28.3 us
    unnamed x252, local copies, waits for them, and re-layouts  26.6 us
    ppermute x12, starting transfers between devices, gather_x_near(): return (v, lax.ppermute(v, 'seq', LEFT), lax.ppermute(v, 'seq', RIGHT))  25.9 us
    ppermute x10, starting transfers between devices, shift_ctx(): lax.ppermute(v, CTX, [(i, i + by) for i in range(NC) if 0 <= i + by < NC])  23.6 us
    pallas_call x2, Pallas kernels, products(): pl.pallas_call(functools.partial(products_kernel, len(pairs), rows_out),...  20.8 us
  transfers between devices with their start and end apart: 97, of which 34 were waited for; matrix products, arithmetic and copies ran while one was open for 32% of the time, Pallas kernels for 22%

profile of v4, /device:TPU:14, one launch (start us, length us, event | category | flops | bytes accessed | tf_op | source)
XLA Modules:
  0.0 697.7 jit_solution(1470174859393734977)
XLA Ops:
  30.9 6.8 collective-permute-start.5
  37.7 5.6 pad.161
  64.3 10.8 %collective-permute-done.7 = bf16[64,1664]{1,0:T(8,128)(2,1)S(1)} collective-permute-done((bf16[64,1664]{1,0:T(8,128)(2,1)S(1)}, bf16[64,1664]{1,0:T(8,128)(2,1)S(1)}, u32[]{:S(2)}, u32[]{:S(2)}) %collective-permute-start.7) | collective-permute-done | bytes 213024 | tf_op jit(solution)/shard_map/ppermute | solution.py:71
  92.9 6.9 fusion.26
  108.8 5.6 fusion.40.projected
  140.0 9.4 %shard_map.330 = (f32[4,16,896]{2,1,0:T(8,128)}, f32[4,1,896]{2,1,0:T(1,128)}) custom-call(f32[512,896]{1,0:T(8,128)} %get-tuple-element.444.step, bf16[512,896]{1,0:T(8,128)(2,1)} %copy-done.17, f32[16,512]{1,0:T(8,128)} %get-tuple-element.404.b_t, f32[16,896]{1,0:T(8,128)} %fusion.148.rate2), custom_call_target="tpu_custom_call" | custom-call | flops 8000000000 | bytes 8000000 | tf_op jit(solution)/shard_map/pallas_call | solution.py:420
  174.7 17.7 %shard_map.331 = (bf16[128,1600]{1,0:T(8,128)(2,1)}, f32[5,640,1]{2,1,0:T(8,128)}) custom-call(s32[2]{0:T(128)} %pad_add_fusion.1.place, bf16[128,2304]{1,0:T(8,128)(2,1)} %fusion.40.projected, bf16[640,640]{1,0:T(8,128)(2,1)} %constant_dynamic-update-slice_fusion.12.mine, bf16[640,640]{1,0:T(8,128)(2,1)} %copy-done.88), custom_call_target="tpu_custom_call" | custom-call | flops 15000000512 | bytes 15000000 | tf_op jit(solution)/shard_map/pallas_call | solution.py:525
  193.5 15.6 %shard_map.332 = (bf16[4,2048,896]{2,1,0:T(8,128)(2,1)}, f32[512,896]{1,0:T(8,128)}, bf16[512,896]{1,0:T(8,128)(2,1)}) custom-call(f32[512,896]{1,0:T(8,128)} %get-tuple-element.444.step, bf16[512,896]{1,0:T(8,128)(2,1)} %copy-done.17, f32[512,896]{1,0:T(8,128)} %get-tuple-element.328.gate_z, f32[16,512]{1,0:T(8,128)} %get-tuple-element.404.b_t, ...), custom_call_target="tpu_custom_call" | custom-call | flops 14000000000 | bytes 14000000 | tf_op jit(solution)/shard_map/pallas_call | solution.py:420
  213.7 7.2 %fusion.43 = bf16[512,1664]{1,0:T(8,128)(2,1)S(1)} fusion(bf16[512,1792]{1,0:T(8,128)(2,1)} %convolution_convert_fusion.1.refs_2_.refs_4_, bf16[1792,3328]{1,0:T(8,128)(2,1)} %all-gather.6.cloned.1.call-done), kind=kOutput, calls=%fused_computation.65 | convolution fusion | flops 3054305280 | bytes 9502720 | tf_op jit(solution)/shard_map/dot_general | solution.py:54
  234.3 6.6 collective-permute-done.28
  246.2 6.7 fusion.49
  267.7 9.1 %fusion.10 = f32[512,2816]{1,0:T(8,128)S(1)} fusion(bf16[512,1792]{1,0:T(8,128)(2,1)S(1)} %constant_dynamic-update-slice_fusion.17.refs_0_, bf16[1792,4480]{1,0:T(8,128)(2,1)} %all-gather.8.cloned.1.call-done), kind=kOutput, calls=%fused_computation.18 | convolution fusion | flops 5167382528 | bytes 17694720 | tf_op jit(solution)/shard_map/dot_general | solution.py:54
  281.4 9.8 %fusion.58 = bf16[512,1792]{1,0:T(8,128)(2,1)S(1)} fusion(bf16[1792,4480]{1,0:T(8,128)(2,1)} %all-gather.8.cloned.1.call-done, bf16[512,1408]{1,0:T(8,128)(2,1)S(1)} %get-tuple-element.325, bf16[512,1408]{1,0:T(8,128)(2,1)S(1)} %get-tuple-element.324), kind=kOutput, calls=%fused_computation.72 | convolution fusion | flops 5174067200 | bytes 14811136 | tf_op jit(solution)/shard_map/dot_general | solution.py:54
  306.9 15.4 %shard_map.333 = bf16[2048,4480]{1,0:T(8,128)(2,1)} custom-call(bf16[512,1792]{1,0:T(8,128)(2,1)} %copy-done.63, bf16[512,2816]{1,0:T(8,128)(2,1)} %pad_maximum_fusion.refs_1_, bf16[512,1792]{1,0:T(8,128)(2,1)} %convolution_convert_fusion.refs_2_, bf16[512,1664]{1,0:T(8,128)(2,1)} %constant_dynamic-update-slice_fusion.7.refs_3_), custom_call_target="tpu_custom_call" | custom-call | flops 14000000000 | bytes 14000000 | tf_op jit(solution)/shard_map/pallas_call | solution.py:570
  367.2 9.4 %shard_map.334 = f32[4,16,896]{2,1,0:T(8,128)} custom-call(f32[512,896]{1,0:T(8,128)} %get-tuple-element.444.step, f32[512,896]{1,0:T(8,128)} %get-tuple-element.307.g_scan, f32[16,512]{1,0:T(8,128)} %get-tuple-element.403.c_t, f32[16,896]{1,0:T(8,128)} %fusion.148.rate2), custom_call_target="tpu_custom_call" | custom-call | flops 8000000000 | bytes 8000000 | tf_op jit(solution)/shard_map/pallas_call | solution.py:420
  383.9 24.0 %shard_map.336 = (bf16[128,1600]{1,0:T(8,128)(2,1)}, bf16[640,640]{1,0:T(8,128)(2,1)}, bf16[512,640]{1,0:T(8,128)(2,1)}) custom-call(s32[2]{0:T(128)} %pad_add_fusion.1.place, bf16[128,2304]{1,0:T(8,128)(2,1)} %fusion.40.projected, bf16[640,640]{1,0:T(8,128)(2,1)} %constant_dynamic-update-slice_fusion.12.mine, bf16[640,640]{1,0:T(8,128)(2,1)} %copy-done.88, ...), custom_call_target="tpu_custom_call" | custom-call | flops 22000001024 | bytes 22000000 | tf_op jit(solution)/shard_map/pallas_call | solution.py:525
  413.1 9.8 %shard_map.335 = bf16[1024,4224]{1,0:T(8,128)(2,1)} custom-call(s32[1]{0:T(128)} %bitcast.47.parity, bf16[128,1792]{1,0:T(8,128)(2,1)} %copy-done.49, bf16[128,1664]{1,0:T(8,128)(2,1)} %pad.168.refs_1_, bf16[512,1792]{1,0:T(8,128)(2,1)} %convolution_convert_fusion.1.refs_2_.refs_4_, bf16[512,1664]{1,0:T(8,128)(2,1)} %copy-done.64, ...), custom_call_target="tpu_custom_call" | custom-call | flops 8000000000 | bytes 8000000 | tf_op jit(solution)/shard_map/pallas_call | solution.py:616
  436.5 34.1 %shard_map.337 = (f32[512,896]{1,0:T(8,128)}, f32[512,896]{1,0:T(8,128)}, f32[4,16,896]{2,1,0:T(8,128)}, f32[16,512]{1,0:T(8,128)}, f32[16,512]{1,0:T(8,128)}) custom-call(f32[512,896]{1,0:T(8,128)} %get-tuple-element.444.step, bf16[512,896]{1,0:T(8,128)(2,1)} %copy-done.17, f32[512,896]{1,0:T(8,128)} %get-tuple-element.307.g_scan, ...), custom_call_target="tpu_custom_call" | custom-call | flops 24999999488 | bytes 25000000 | tf_op jit(solution)/shard_map/pallas_call | solution.py:420
  491.5 14.0 %shard_map.339 = bf16[1024,6528]{1,0:T(8,128)(2,1)} custom-call(s32[1]{0:T(128)} %bitcast.29.parity, bf16[128,1792]{1,0:T(8,128)(2,1)} %copy-done.49, bf16[128,1664]{1,0:T(8,128)(2,1)} %pad.168.refs_1_, bf16[128,1792]{1,0:T(8,128)(2,1)} %copy-done.34, bf16[128,2304]{1,0:T(8,128)(2,1)} %fusion.101.refs_1_.refs_3_, ...), custom_call_target="tpu_custom_call" | custom-call | flops 12000000000 | bytes 12000000 | tf_op jit(solution)/shard_map/pallas_call | solution.py:616
  538.7 6.6 fusion.52
  561.0 11.7 %collective-permute-done.67 = bf16[4,56,512]{2,1,0:T(8,128)(2,1)S(1)} collective-permute-done((bf16[4,56,512]{2,1,0:T(8,128)(2,1)S(1)}, bf16[4,56,512]{2,1,0:T(8,128)(2,1)S(1)}, u32[]{:S(2)}, u32[]{:S(2)}) %collective-permute-start.67) | collective-permute-done | bytes 229408 | tf_op jit(solution)/shard_map/ppermute | solution.py:636
  635.1 6.5 all-to-all-start
  645.5 6.2 collective-permute-start.84
  658.9 8.6 %collective-permute-start.85 = (bf16[80,1664]{1,0:T(8,128)(2,1)S(1)}, bf16[80,1664]{1,0:T(8,128)(2,1)S(1)}, u32[]{:S(2)}, u32[]{:S(2)}) collective-permute-start(bf16[80,1664]{1,0:T(8,128)(2,1)S(1)} %collective-permute-done.84), channel_id=1, source_target_pairs={{0,32},{32,64},{64,96},{96,0},{1,33},{33,65},{65,97},{97,1},{2,34}... | collective-permute-start | bytes 798728 | tf_op jit(solution)/shard_map/ppermute | solution.py:66
  (793 shorter events, 415.7 us)
Async XLA Ops:
  7.2 85.4 %all-gather.4.cloned.1.call-start = ((), (), s32[]{:S(2)}) async-start(), calls=%async_computation.3 | async-start | bytes 17031168 | tf_op jit(solution)/shard_map/all_gather | solution.py:733
  12.9 200.8 %all-gather.6.cloned.1.call-start = ((), (), s32[]{:S(2)}) async-start(), calls=%async_computation.4 | async-start | bytes 12300288 | tf_op jit(solution)/shard_map/all_gather | solution.py:758
  29.5 216.7 %all-gather.8.cloned.1.call-start = ((), (), s32[]{:S(2)}) async-start(), calls=%async_computation.5 | async-start | bytes 16558080 | tf_op jit(solution)/shard_map/all_gather | solution.py:775
  30.9 30.5 %collective-permute-start.5 = (bf16[128,1664]{1,0:T(8,128)(2,1)}, bf16[128,1664]{1,0:T(8,128)(2,1)S(1)}, u32[]{:S(2)}, u32[]{:S(2)}) collective-permute-start(bf16[128,1664]{1,0:T(8,128)(2,1)} %get-tuple-element.389), channel_id=1, source_target_pairs={{0,96},{32,0},{64,32},{96,64},{1,97},{33,1},{65,33},{97,65},{2,98}... | collective-permute-start | bytes 1277960 | tf_op jit(solution)/shard_map/ppermute | solution.py:66
  37.7 23.6 %collective-permute-start.6 = (bf16[128,1664]{1,0:T(8,128)(2,1)}, bf16[128,1664]{1,0:T(8,128)(2,1)S(1)}, u32[]{:S(2)}, u32[]{:S(2)}) collective-permute-start(bf16[128,1664]{1,0:T(8,128)(2,1)} %get-tuple-element.389), channel_id=1, source_target_pairs={{0,32},{32,64},{64,96},{96,0},{1,33},{33,65},{65,97},{97,1},{2,34}... | collective-permute-start | bytes 1277960 | tf_op jit(solution)/shard_map/ppermute | solution.py:66
  56.3 24.8 %collective-permute-start.1 = (bf16[128,1792]{1,0:T(8,128)(2,1)S(1)}, bf16[128,1792]{1,0:T(8,128)(2,1)S(1)}, u32[]{:S(2)}, u32[]{:S(2)}) collective-permute-start(bf16[128,1792]{1,0:T(8,128)(2,1)S(1)} %convolution_convert_fusion.4.refs_0_.refs_2_), channel_id=1, source_target_pairs={{0,96},{32,0},{64,32},{96,64},{1,97},{33,1},{65,33},{97,65},{2,98}... | collective-permute-start | bytes 1376264 | tf_op jit(solution)/shard_map/ppermute | solution.py:66
  92.6 379.2 %reduce-scatter.3.cloned.1.call-start = ((), (), s32[]{:S(2)}) async-start(), calls=%async_computation.6 | async-start | bytes 18923520 | tf_op jit(solution)/shard_map/reduce_scatter | solution.py:629
  122.1 27.3 %collective-permute-start.13 = (bf16[128,640]{1,0:T(8,128)(2,1)S(1)}, bf16[128,640]{1,0:T(8,128)(2,1)S(1)}, u32[]{:S(2)}, u32[]{:S(2)}) collective-permute-start(bf16[128,640]{1,0:T(8,128)(2,1)S(1)} %slice.672), channel_id=1, source_target_pairs={{0,8},{1,9},{2,10},{3,11},{4,12},{5,13},{6,14},{7,15},{8,16},{9,17... | collective-permute-start | bytes 491528 | tf_op jit(solution)/shard_map/ppermute | solution.py:157
  124.0 26.1 %collective-permute-start.14 = (bf16[128,640]{1,0:T(8,128)(2,1)S(1)}, bf16[128,640]{1,0:T(8,128)(2,1)S(1)}, u32[]{:S(2)}, u32[]{:S(2)}) collective-permute-start(bf16[128,640]{1,0:T(8,128)(2,1)S(1)} %slice.672), channel_id=1, source_target_pairs={{0,6},{1,7},{2,8},{3,9},{4,10},{5,11},{6,12},{7,13},{8,14},{9,15},... | collective-permute-start | bytes 491528 | tf_op jit(solution)/shard_map/ppermute | solution.py:157
  167.6 24.8 %collective-permute-start.22 = (bf16[68,896]{1,0:T(8,128)(2,1)S(1)}, bf16[68,896]{1,0:T(8,128)(2,1)S(1)}, u32[]{:S(2)}, u32[]{:S(2)}) collective-permute-start(bf16[68,896]{1,0:T(8,128)(2,1)S(1)} %pad_maximum_fusion.28), channel_id=1, source_target_pairs={{0,8},{1,9},{2,10},{3,11},{4,12},{5,13},{6,14},{7,15},{8,16},{9,17... | collective-permute-start | bytes 365576 | tf_op jit(solution)/shard_map/ppermute | solution.py:178
  324.4 302.4 %reduce-scatter.5.cloned.1.call-start = ((), (), s32[]{:S(2)}) async-start(), calls=%async_computation.7 | async-start | bytes 14204928 | tf_op jit(solution)/shard_map/reduce_scatter | solution.py:1000
  379.6 28.3 %collective-permute-start.44 = (bf16[68,896]{1,0:T(8,128)(2,1)S(1)}, bf16[68,896]{1,0:T(8,128)(2,1)S(1)}, u32[]{:S(2)}, u32[]{:S(2)}) collective-permute-start(bf16[68,896]{1,0:T(8,128)(2,1)S(1)} %pad_maximum_fusion.29), channel_id=1, source_target_pairs={{0,2},{1,3},{2,4},{3,5},{4,6},{5,7},{6,0},{7,1},{8,10},{9,11},{10,... | collective-permute-start | bytes 365576 | tf_op jit(solution)/shard_map/ppermute | solution.py:178
  379.7 28.3 %collective-permute-start.43 = (bf16[68,896]{1,0:T(8,128)(2,1)S(1)}, bf16[68,896]{1,0:T(8,128)(2,1)S(1)}, u32[]{:S(2)}, u32[]{:S(2)}) collective-permute-start(bf16[68,896]{1,0:T(8,128)(2,1)S(1)} %pad_maximum_fusion.29), channel_id=1, source_target_pairs={{0,4},{1,5},{2,6},{3,7},{4,0},{5,1},{6,2},{7,3},{8,12},{9,13},{10,... | collective-permute-start | bytes 365576 | tf_op jit(solution)/shard_map/ppermute | solution.py:178
  383.1 24.9 %collective-permute-start.42 = (bf16[68,896]{1,0:T(8,128)(2,1)S(1)}, bf16[68,896]{1,0:T(8,128)(2,1)S(1)}, u32[]{:S(2)}, u32[]{:S(2)}) collective-permute-start(bf16[68,896]{1,0:T(8,128)(2,1)S(1)} %pad_maximum_fusion.29), channel_id=1, source_target_pairs={{0,6},{1,7},{2,0},{3,1},{4,2},{5,3},{6,4},{7,5},{8,14},{9,15},{10,... | collective-permute-start | bytes 365576 | tf_op jit(solution)/shard_map/ppermute | solution.py:178
  428.8 42.9 %collective-permute-start.49 = (bf16[1024,4224]{1,0:T(8,128)(2,1)}, bf16[1024,4224]{1,0:T(8,128)(2,1)}, u32[]{:S(2)}, u32[]{:S(2)}) collective-permute-start(bf16[1024,4224]{1,0:T(8,128)(2,1)} %shard_map.335), channel_id=1, source_target_pairs={{0,1},{1,0},{2,3},{3,2},{4,5},{5,4},{6,7},{7,6},{8,9},{9,8},{10,11... | collective-permute-start | bytes 25952264 | tf_op jit(solution)/shard_map/ppermute | solution.py:949
  430.0 40.6 %collective-permute-start.53 = (bf16[128,640]{1,0:T(8,128)(2,1)S(1)}, bf16[128,640]{1,0:T(8,128)(2,1)S(1)}, u32[]{:S(2)}, u32[]{:S(2)}) collective-permute-start(bf16[128,640]{1,0:T(8,128)(2,1)S(1)} %get-tuple-element.375), channel_id=1, source_target_pairs={{8,0},{9,1},{10,2},{11,3},{12,4},{13,5},{14,6},{15,7},{16,8},{17,9... | collective-permute-start | bytes 491528 | tf_op jit(solution)/shard_map/ppermute | solution.py:157
  431.3 39.3 %collective-permute-start.52 = (bf16[128,640]{1,0:T(8,128)(2,1)S(1)}, bf16[128,640]{1,0:T(8,128)(2,1)S(1)}, u32[]{:S(2)}, u32[]{:S(2)}) collective-permute-start(bf16[128,640]{1,0:T(8,128)(2,1)S(1)} %get-tuple-element.376), channel_id=1, source_target_pairs={{6,0},{7,1},{8,2},{9,3},{10,4},{11,5},{12,6},{13,7},{14,8},{15,9},... | collective-permute-start | bytes 491528 | tf_op jit(solution)/shard_map/ppermute | solution.py:157
  432.6 38.1 %collective-permute-start.51 = (bf16[128,640]{1,0:T(8,128)(2,1)S(1)}, bf16[128,640]{1,0:T(8,128)(2,1)S(1)}, u32[]{:S(2)}, u32[]{:S(2)}) collective-permute-start(bf16[128,640]{1,0:T(8,128)(2,1)S(1)} %get-tuple-element.377), channel_id=1, source_target_pairs={{4,0},{5,1},{6,2},{7,3},{8,4},{9,5},{10,6},{11,7},{12,8},{13,9},{1... | collective-permute-start | bytes 491528 | tf_op jit(solution)/shard_map/ppermute | solution.py:157
  433.9 36.8 %collective-permute-start.50 = (bf16[128,640]{1,0:T(8,128)(2,1)S(1)}, bf16[128,640]{1,0:T(8,128)(2,1)S(1)}, u32[]{:S(2)}, u32[]{:S(2)}) collective-permute-start(bf16[128,640]{1,0:T(8,128)(2,1)S(1)} %get-tuple-element.374), channel_id=1, source_target_pairs={{2,0},{3,1},{4,2},{5,3},{6,4},{7,5},{8,6},{9,7},{10,8},{11,9},{12,... | collective-permute-start | bytes 491528 | tf_op jit(solution)/shard_map/ppermute | solution.py:157
  552.7 25.6 %collective-permute-start.62 = (bf16[64,3456]{1,0:T(8,128)(2,1)S(1)}, bf16[64,3456]{1,0:T(8,128)(2,1)S(1)}, u32[]{:S(2)}, u32[]{:S(2)}) collective-permute-start(bf16[64,3456]{1,0:T(8,128)(2,1)S(1)} %get-tuple-element.332), channel_id=1, source_target_pairs={{0,32},{32,64},{64,96},{96,0},{1,33},{33,65},{65,97},{97,1},{2,34}... | collective-permute-start | bytes 1327112 | tf_op jit(solution)/shard_map/ppermute | solution.py:99
  553.6 27.9 %collective-permute-start.64 = (bf16[64,3456]{1,0:T(8,128)(2,1)S(1)}, bf16[64,3456]{1,0:T(8,128)(2,1)S(1)}, u32[]{:S(2)}, u32[]{:S(2)}) collective-permute-start(bf16[64,3456]{1,0:T(8,128)(2,1)S(1)} %get-tuple-element.335), channel_id=1, source_target_pairs={{0,96},{32,0},{64,32},{96,64},{1,97},{33,1},{65,33},{97,65},{2,98}... | collective-permute-start | bytes 1327112 | tf_op jit(solution)/shard_map/ppermute | solution.py:100
  582.7 31.9 %collective-permute-start.65 = (bf16[128,3456]{1,0:T(8,128)(2,1)}, bf16[128,3456]{1,0:T(8,128)(2,1)}, u32[]{:S(2)}, u32[]{:S(2)}) collective-permute-start(bf16[128,3456]{1,0:T(8,128)(2,1)} %pad_maximum_fusion.6), channel_id=1, source_target_pairs={{0,96},{32,0},{64,32},{96,64},{1,97},{33,1},{65,33},{97,65},{2,98}... | collective-permute-start | bytes 2654216 | tf_op jit(solution)/shard_map/ppermute | solution.py:112
  584.0 30.7 %collective-permute-start.63 = (bf16[128,3456]{1,0:T(8,128)(2,1)}, bf16[128,3456]{1,0:T(8,128)(2,1)}, u32[]{:S(2)}, u32[]{:S(2)}) collective-permute-start(bf16[128,3456]{1,0:T(8,128)(2,1)} %pad_maximum_fusion.5), channel_id=1, source_target_pairs={{0,32},{32,64},{64,96},{96,0},{1,33},{33,65},{65,97},{97,1},{2,34}... | collective-permute-start | bytes 2654216 | tf_op jit(solution)/shard_map/ppermute | solution.py:111
  635.1 32.7 %all-to-all-start = ((f32[32,16,256]{2,1,0:T(8,128)}), f32[32,16,256]{2,1,0:T(8,128)S(1)}, u32[]{:S(2)}, u32[]{:S(2)}) async-start(f32[32,16,256]{2,1,0:T(8,128)} %broadcast_in_dim.123), calls=%async_computation.2 | async-start | bytes 1048576 | tf_op jit(solution)/shard_map/all_to_all | solution.py:1073
  (180 other events, 1930.3 us)
Sparse Core Ops, SparseCore 0:
  13.0 79.5 all-gather.3
  95.5 66.2 all-gather.5
  164.7 76.5 all-gather.7
  324.5 134.0 reduce-scatter.2
  505.6 115.6 reduce-scatter.4
